TPU v7x, 128 devices: a whole 4x4x4 slice. The times are simulated.
128 devices in a mesh: lon: 32 (over x, z, core), lat: 4 (over y).
Axes of the slice: x: 4, y: 4, z: 4, core: 2. Of those that a mesh axis runs over, the one named last changes fastest.
Arguments:
- obs_value: float32 [1310720], P(('lon', 'lat')), may hold values from -6 to 6
- send_list: int32 [16384, 80], P(('lon', 'lat')), may hold values from -1 to 10239, as said below
- recv_cell: int32 [16384, 80], P(('lon', 'lat')), may hold values from -1 to 767999, as said below
- column_depth: int32 [160, 4096], P('lat', 'lon'), may hold values from 0 to 75
- zonal_weight: float32 [2, 160, 4096], P(None, 'lat', 'lon'), may hold values from 1000 to 30000
- merid_weight: float32 [2, 160, 4096], P(None, 'lat', 'lon'), may hold values from 400 to 6400
- vert_inverse: float32 [2, 75, 75], replicated, may hold values from 0 to 2
- norm_scale: float32 [2, 75, 160, 4096], P(None, None, 'lat', 'lon'), may hold values from 20 to 200
Outputs:
- increment: float32 [2, 75, 160, 4096], P(None, None, 'lat', 'lon')
- obs_result: float32 [1310720], P(('lon', 'lat'))
Inputs may be any that keep to these rules, and one draw needn't show every extreme that they name: `send_list`: row q * 128 + r names, in its first slots, the positions among device q's 10240 observations that device q sends to device r, and -1 in the rest; no position appears twice among device q's rows. Some device receives 80 observations from every device. `recv_cell`: row r * 128 + q, slot k, is the cell of owner r that receives slot k of row q * 128 + r of send_list, and -1 exactly where that slot is -1.
All inputs are finite; a program needn't handle non-finite values.
Results may differ from a plain program's by a relative error of at most 0.0007.
Values sent between devices are 32-bit elements; how exact they have to be, the bound alone decides.
A program may use at most 128 MiB of HBM per device.

v0:
```python
import jax
import jax.numpy as jnp
from jax import lax
from jax.experimental import pallas as pl
from jax.experimental.pallas import tpu as pltpu
from jax.sharding import PartitionSpec as P

F32 = jnp.float32
BF16 = jnp.bfloat16
MESH = pl.DeviceIdType.MESH
NF, NZ, NLAT, NLON = 2, 75, 40, 128
ZP = 80
RANKS, CAP = 128, 80
N_LON, N_LAT = 32, 4
SOLVERS = 19
LANES = 128
CHUNK = 4
GRIDS = 4
ROWS = NF * NLAT * ZP
VMEM_SPEC = pl.BlockSpec(memory_space=pltpu.VMEM)
SMEM_SPEC = pl.BlockSpec(memory_space=pltpu.SMEM)
ANY_SPEC = pl.BlockSpec(memory_space=pl.ANY)


def lane_iota(rows):
    return lax.broadcasted_iota(jnp.int32, (rows, LANES), 1)


def split(value):
    high = value.astype(BF16)
    return high, (value - high.astype(F32)).astype(BF16)


def lane_pick(table, index):
    return jnp.take_along_axis(table, index, axis=1, mode="promise_in_bounds")


def prepare_kernel(
    obs_ref, send_ref, zw_ref, mw_ref, north_ref, vert_in,
    out_ref, zs_ref, zr_ref, zco_ref, ms_ref, mr_ref, mco_ref, vert_ref,
    idx_ref, iw_ref, st_ref, rt_ref, miw_ref,
):
    for field in range(NF):
        product = lax.dot_general(
            vert_in[field], vert_in[field], (((1,), (1,)), ((), ())),
            precision=lax.Precision.HIGHEST, preferred_element_type=F32,
        )
        high, low = split(product)
        vert_ref[field] = jnp.concatenate([high, low, high], axis=1)
    idx_ref[...] = jnp.full((RANKS, LANES), -1, jnp.int32)
    idx_ref[:, :CAP] = send_ref[...]
    part = 64
    for start in range(0, RANKS, part):
        index = idx_ref[start : start + part, :]
        low = index & 127
        high = index >> 7

        def gather_row(row, acc, low=low, high=high):
            line = jnp.broadcast_to(obs_ref[pl.ds(row, 1), :], (part, LANES))
            return jnp.where(high == row, lane_pick(line, low), acc)

        picked = lax.fori_loop(0, CAP, gather_row, jnp.zeros((part, LANES), F32), unroll=4)
        out_ref[start : start + part, :] = picked[:, :CAP]

    iw_ref[...] = jnp.full((LANES, LANES), 1e-3, F32)
    iw_ref[: NF * NLAT, :] = 1.0 / zw_ref[...]
    iw_ref[...] = jnp.transpose(iw_ref[...])
    zero = north_ref[...] * 0.0
    one = zero + 1.0

    def zonal_step(step, carry):
        s_val, s_flux, s_sum, r_val, r_flux, r_sum = carry
        back = LANES - 1 - step
        st_ref[pl.ds(step, 1), :] = s_val[0:1]
        s_sum = s_sum + s_val
        s_val = s_val + s_flux * iw_ref[pl.ds(step, 1), :]
        s_flux = s_flux + s_val
        r_sum = r_sum + r_val
        r_val = r_val + r_flux * iw_ref[pl.ds(back, 1), :]
        rt_ref[pl.ds(back, 1), :] = r_val[0:1]
        r_flux = r_flux + r_val
        return s_val, s_flux, s_sum, r_val, r_flux, r_sum

    _, _, s_sum, r_first, _, r_sum = lax.fori_loop(
        0, LANES, zonal_step, (zero, one, zero, zero, one, zero), unroll=8
    )
    coupling = 1.0 / r_first[0:1]
    zco_ref[...] = jnp.zeros((8, LANES), F32)
    zco_ref[0:1, :] = coupling
    zco_ref[1:2, :] = r_sum[0:1] * coupling
    zco_ref[2:3, :] = s_sum[0:1] * coupling
    zs_ref[...] = jnp.transpose(st_ref[...])[: NF * NLAT, :]
    zr_ref[...] = jnp.transpose(rt_ref[...] * coupling)[: NF * NLAT, :]

    north = north_ref[...]
    miw_ref[...] = 1.0 / mw_ref[...]
    mco_ref[...] = jnp.zeros((NF, 8, LANES), F32)
    for field in range(NF):
        s_val, s_flux, s_sum = zero, one, zero
        for row in range(NLAT):
            ms_ref[field, row : row + 1, :] = s_val[0:1]
            s_sum = s_sum + s_val
            s_val = s_val + s_flux * miw_ref[field, row : row + 1, :]
            s_flux = s_flux + s_val
        r_val = jnp.where(north > 0.5, 1.0, miw_ref[field, NLAT - 1 : NLAT, :] + zero)
        r_flux = jnp.where(north > 0.5, 0.0, one)
        r_sum = zero
        mr_ref[field, NLAT - 1 : NLAT, :] = r_val[0:1]
        for row in range(NLAT - 2, -1, -1):
            r_sum = r_sum + r_val
            r_flux = r_flux + r_val
            r_val = r_val + r_flux * miw_ref[field, row : row + 1, :]
            mr_ref[field, row : row + 1, :] = r_val[0:1]
        inverse = 1.0 / r_val[0:1]
        coupling = jnp.where(north[0:1] > 0.5, 0.0, inverse)
        mr_ref[field] = mr_ref[field] * inverse
        mco_ref[field, 0:1, :] = coupling
        mco_ref[field, 1:2, :] = r_sum[0:1] * inverse
        mco_ref[field, 2:3, :] = s_sum[0:1] * coupling


def prepare(obs, send_list, zonal_weight, merid_weight, north, vert_inverse):
    shape = lambda *dims: jax.ShapeDtypeStruct(dims, F32)
    return pl.pallas_call(
        prepare_kernel,
        out_shape=(
            shape(RANKS, CAP), shape(80, LANES), shape(80, LANES), shape(8, LANES),
            shape(NF, NLAT, LANES), shape(NF, NLAT, LANES), shape(NF, 8, LANES),
            jax.ShapeDtypeStruct((NF, ZP, 3 * ZP), BF16),
        ),
        in_specs=[VMEM_SPEC] * 6,
        out_specs=(VMEM_SPEC,) * 8,
        scratch_shapes=[
            pltpu.VMEM((RANKS, LANES), jnp.int32),
            pltpu.VMEM((LANES, LANES), F32),
            pltpu.VMEM((LANES, LANES), F32),
            pltpu.VMEM((LANES, LANES), F32),
            pltpu.VMEM((NF, NLAT, LANES), F32),
        ],
        compiler_params=pltpu.CompilerParams(vmem_limit_bytes=16 << 20),
        name="prepare",
    )(obs, send_list, zonal_weight.reshape(NF * NLAT, LANES), merid_weight, north, vert_inverse)


def scatter_kernel(rows_ref, lane_ref, in_ref, depth_ref, norm_ref, field_ref, scale_ref, *scratch):
    grids = scratch[:GRIDS]
    value_ref, spread_ref = scratch[GRIDS:]

    def clear(step, _):
        at = pl.ds(pl.multiple_of(step * 64, 64), 64)
        for grid in grids:
            grid[at, :] = jnp.zeros((64, LANES), F32)
        return 0

    lax.fori_loop(0, ROWS // 64, clear, 0)
    value_ref[...] = jnp.zeros((RANKS, LANES), F32)
    value_ref[:, :CAP] = in_ref[...]
    value_ref[...] = jnp.transpose(value_ref[...])
    iota = lane_iota(CAP)

    def sender(q, _):
        index = jnp.full((CAP, LANES), q, jnp.int32)
        value = lane_pick(value_ref[:CAP, :], index)
        lane = lane_pick(lane_ref[...], index)
        slot = q & 1
        spread_ref[slot] = jnp.where(iota == lane, value, 0.0)
        for k in range(CAP):
            row = rows_ref[q * CAP + k]
            grid = grids[k % GRIDS]
            at = pl.ds(row, 1)
            grid[at, :] = grid[at, :] + spread_ref[slot, k : k + 1, :]
        return 0

    lax.fori_loop(0, RANKS, sender, 0)
    level = lax.broadcasted_iota(jnp.int32, (ZP, LANES), 0)
    for field in range(NF):

        def finish(row, _, field=field):
            at = pl.ds(pl.multiple_of((field * NLAT + row) * ZP, ZP), ZP)
            total = grids[0][at, :]
            for grid in grids[1:]:
                total = total + grid[at, :]
            wet = level < depth_ref[pl.ds(row, 1), :]
            scale = jnp.where(wet, norm_ref[field, row], 0.0)
            scale_ref[field, row] = scale
            field_ref[field, row] = jnp.where(wet, scale * total, 0.0)
            return 0

        lax.fori_loop(0, NLAT, finish, 0)


def scatter(rows, lanes, incoming, depth, norm):
    full = jax.ShapeDtypeStruct((NF, NLAT, ZP, LANES), F32)
    return pl.pallas_call(
        scatter_kernel,
        out_shape=(full, full),
        in_specs=[SMEM_SPEC] + [VMEM_SPEC] * 4,
        out_specs=(VMEM_SPEC, VMEM_SPEC),
        scratch_shapes=[pltpu.VMEM((ROWS, LANES), F32)] * GRIDS
        + [pltpu.VMEM((RANKS, LANES), F32), pltpu.VMEM((2, CAP, LANES), F32)],
        compiler_params=pltpu.CompilerParams(vmem_limit_bytes=40 << 20),
        name="scatter",
    )(rows, lanes, incoming, depth, norm)


def push(source, target, send_sem, recv_sem, axis, device):
    return pltpu.make_async_remote_copy(
        src_ref=source, dst_ref=target, send_sem=send_sem, recv_sem=recv_sem,
        device_id={axis: device}, device_id_type=MESH,
    )


def solve_kernel(
    field_ref, scale_ref, zs_ref, zr_ref, zco_ref, ms_ref, mr_ref, mco_ref, vert_ref, sums_ref,
    x_ref,
    zco_all, mco_all, alpha, gamma, minv,
    zsend, zrecv, zret, zres, msend, mrecv, mret, mres,
    acc_a, acc_b, ubuf, gbuf, mtot,
    zco_s, zco_r, mco_s, mco_r, z1s, z1r, z2s, z2r, m1s, m1r, m2s, m2r,
):
    me = lax.axis_index("lon")
    my = lax.axis_index("lat")
    iota = lane_iota(ZP)
    is_solver = me < SOLVERS

    barrier = pltpu.get_barrier_semaphore()

    def greet_lon(step, _):
        pl.semaphore_signal(barrier, inc=1, device_id={"lon": (me + step) % N_LON}, device_id_type=MESH)
        return 0

    def greet_lat(step, _):
        pl.semaphore_signal(barrier, inc=1, device_id={"lat": (my + step) % N_LAT}, device_id_type=MESH)
        return 0

    lax.fori_loop(1, N_LON, greet_lon, 0)
    lax.fori_loop(1, N_LAT, greet_lat, 0)
    pl.semaphore_wait(barrier, N_LON - 1 + N_LAT - 1)

    def zco_copy(device, slot):
        return push(zco_ref, zco_all.at[slot], zco_s.at[device], zco_r.at[slot], "lon", device)

    def mco_copy(device, slot):
        return push(mco_ref, mco_all.at[slot], mco_s.at[device], mco_r.at[slot], "lat", device)

    def over_solvers(action):
        def body(step, _):
            device = (me + step) % N_LON

            @pl.when(device < SOLVERS)
            def _():
                action(device)

            return 0

        lax.fori_loop(1, N_LON, body, 0)

    def over_lon(action):
        def body(step, _):
            action((me + step) % N_LON)
            return 0

        lax.fori_loop(1, N_LON, body, 0)

    def over_lat(action):
        def body(step, _):
            action((my + step) % N_LAT)
            return 0

        lax.fori_loop(1, N_LAT, body, 0)

    over_solvers(lambda device: zco_copy(device, me).start())
    over_lat(lambda device: mco_copy(device, my).start())
    zco_all[me] = zco_ref[...]
    mco_all[my] = mco_ref[...]

    def zonal_pass(field, chunk, load, field_base):
        lines, left = [], []
        for step in range(CHUNK):
            row = chunk * CHUNK + step
            at = pl.ds(field_base + row, 1)
            s_row, r_row = zs_ref[at, :], zr_ref[at, :]
            value = load(row, step)
            for coef in (s_row, r_row):
                high, low = split(coef * value)
                left.append(jnp.concatenate([high, low], axis=1))
            lines.append((row, s_row, r_row))
        sums = jnp.dot(jnp.concatenate(left, axis=0), sums_ref[...], preferred_element_type=F32)
        tot_a, tot_b = acc_a[...], acc_b[...]
        for step, (row, s_row, r_row) in enumerate(lines):
            a_part = sums[2 * step * ZP : (2 * step + 1) * ZP]
            b_part = sums[(2 * step + 1) * ZP : (2 * step + 2) * ZP]
            x_ref[field, row] = r_row * a_part[:, :LANES] - s_row * b_part[:, :LANES]
            mine = iota == field_base + row
            tot_a = jnp.where(mine, a_part[:, LANES:], tot_a)
            tot_b = jnp.where(mine, b_part[:, LANES:], tot_b)
        acc_a[...] = tot_a
        acc_b[...] = tot_b

    def zonal_send(turn):
        acc_a[...] = acc_a[...] * zco_ref[0:1, :]
        for solver in range(SOLVERS):
            zsend[turn, solver, 0:4, :] = acc_b[4 * solver : 4 * solver + 4, :]
            zsend[turn, solver, 4:8, :] = acc_a[4 * solver : 4 * solver + 4, :]
        over_solvers(lambda device: zonal_out(turn, device, me).start())

        @pl.when(is_solver)
        def _():
            zrecv[turn, me] = zsend[turn, me]

    def zonal_out(turn, device, slot):
        return push(
            zsend.at[turn, device], zrecv.at[turn, slot], z1s.at[turn, device], z1r.at[turn, slot], "lon", device
        )

    def zonal_back(turn, device, slot):
        return push(
            zret.at[turn, device], zres.at[turn, slot], z2s.at[turn, device], z2r.at[turn, slot], "lon", device
        )

    def zonal_factor():
        over_lon(lambda device: zco_copy(0, device).wait_recv())
        coupling = zco_all[:, 0, :]
        west = jnp.concatenate([coupling[-1:], coupling[:-1]], axis=0)
        spill = zco_all[:, 2, :]
        mass = 1.0 + zco_all[:, 1, :] + jnp.concatenate([spill[-1:], spill[:-1]], axis=0)
        east = coupling
        for bit in range(5):
            stride = 1 << bit
            down = lambda v: jnp.concatenate([v[-stride:], v[:-stride]], axis=0)
            up = lambda v: jnp.concatenate([v[stride:], v[:stride]], axis=0)
            inverse = 1.0 / (mass + west + east)
            left = west * down(inverse)
            right = east * up(inverse)
            alpha[bit] = left
            gamma[bit] = right
            mass = mass + left * down(mass) + right * up(mass)
            west, east = left * down(west), right * up(east)
        minv[...] = 1.0 / mass

    def zonal_reduced(turn):
        over_lon(lambda device: zonal_out(turn, 0, device).wait_recv())
        tiles = [zrecv[turn, k] for k in range(N_LON)]
        flip = lambda v: jnp.concatenate([v[4:], v[:4]], axis=0)
        right_side = [tiles[k] + flip(tiles[k - 1]) for k in range(N_LON)]
        for bit in range(5):
            stride = 1 << bit
            right_side = [
                right_side[k]
                + alpha[bit, k : k + 1, :] * right_side[(k - stride) % N_LON]
                + gamma[bit, k : k + 1, :] * right_side[(k + stride) % N_LON]
                for k in range(N_LON)
            ]
        values = [right_side[k] * minv[k : k + 1, :] for k in range(N_LON)]
        for k in range(N_LON):
            zret[turn, k] = jnp.concatenate([values[k][:4], values[(k + 1) % N_LON][:4]], axis=0)
        over_lon(lambda device: zonal_back(turn, device, me).start())
        zres[turn, me] = zret[turn, me]

    def zonal_receive(turn):
        over_solvers(lambda device: zonal_back(turn, 0, device).wait_recv())
        ubuf[72:80, :] = jnp.zeros((8, LANES), F32)
        gbuf[72:80, :] = jnp.zeros((8, LANES), F32)
        for solver in range(SOLVERS):
            ubuf[4 * solver : 4 * solver + 4, :] = zres[turn, solver, 0:4, :]
            gbuf[4 * solver : 4 * solver + 4, :] = zres[turn, solver, 4:8, :]
        gbuf[...] = gbuf[...] * zco_ref[0:1, :] + acc_b[...]

    def zonal_values(field, chunk, field_base):
        u_all, g_all = ubuf[...], gbuf[...]
        found = []
        for step in range(CHUNK):
            row = chunk * CHUNK + step
            at = pl.ds(field_base + row, 1)
            found.append(
                x_ref[field, row]
                + zr_ref[at, :] * jnp.broadcast_to(u_all[:, step : step + 1], (ZP, LANES))
                + zs_ref[at, :] * jnp.broadcast_to(g_all[:, step : step + 1], (ZP, LANES))
            )
        ubuf[...] = pltpu.roll(u_all, LANES - CHUNK, 1)
        gbuf[...] = pltpu.roll(g_all, LANES - CHUNK, 1)
        return found

    def vertical(field, value):
        high, low = split(value)
        return jnp.dot(
            vert_ref[field], jnp.concatenate([high, high, low], axis=0), preferred_element_type=F32
        )

    def vertical_field(field):
        def body(pair, _):
            row = pair * 2
            both = jnp.concatenate([x_ref[field, row], x_ref[field, row + 1]], axis=1)
            both = vertical(field, both)
            x_ref[field, row] = both[:, :LANES]
            x_ref[field, row + 1] = both[:, LANES:]
            return 0

        lax.fori_loop(0, NLAT // 2, body, 0)

    def merid_out(turn, device, slot):
        return push(
            msend.at[turn, device], mrecv.at[turn, slot], m1s.at[turn, device], m1r.at[turn, slot], "lat", device
        )

    def merid_back(turn, device, slot):
        return push(
            mret.at[turn, device], mres.at[turn, slot], m2s.at[turn, device], m2r.at[turn, slot], "lat", device
        )

    def merid_step(field, row, value, tot_a, tot_b):
        s_row, r_row = ms_ref[field, pl.ds(row, 1), :], mr_ref[field, pl.ds(row, 1), :]
        tot_a = tot_a + s_row * value
        tot_b = tot_b + r_row * value
        x_ref[field, row] = r_row * tot_a - s_row * tot_b
        return tot_a, tot_b

    def merid_send(turn, field, tot_a, tot_b):
        mtot[field] = tot_b
        tot_a = tot_a * mco_ref[field, 0:1, :]
        for half in range(2):
            msend[turn, 2 * field + half, 0] = tot_b[40 * half : 40 * half + 40]
            msend[turn, 2 * field + half, 1] = tot_a[40 * half : 40 * half + 40]
        for half in range(2):
            solver = 2 * field + half

            @pl.when(my != solver)
            def _(solver=solver):
                merid_out(turn, solver, my).start()

            @pl.when(my == solver)
            def _(solver=solver):
                mrecv[turn, solver] = msend[turn, solver]

    def merid_reduced(turn):
        if turn == 0:
            over_lat(lambda device: mco_copy(0, device).wait_recv())
        field = my // 2
        over_lat(lambda device: merid_out(turn, 0, device).wait_recv())
        rows = [mco_all[k, field] for k in range(N_LAT)]
        mass = 1.0 + rows[0][1:2]
        reduced = mrecv[turn, 0, 0]
        kept, inverses = [], []
        for k in range(N_LAT):
            coupling = rows[k][0:1]
            inverse = 1.0 / (mass + coupling)
            kept.append(reduced)
            inverses.append(inverse)
            if k + 1 < N_LAT:
                factor = coupling * inverse
                mass = 1.0 + rows[k + 1][1:2] + rows[k][2:3] + factor * mass
                reduced = mrecv[turn, k + 1, 0] + mrecv[turn, k, 1] + factor * reduced
        value = kept[N_LAT - 1] * inverses[N_LAT - 1]
        mret[turn, N_LAT - 1, 0] = value
        mret[turn, N_LAT - 1, 1] = jnp.zeros_like(value)
        for k in range(N_LAT - 2, -1, -1):
            mret[turn, k, 1] = value
            value = (kept[k] + rows[k][0:1] * value) * inverses[k]
            mret[turn, k, 0] = value
        over_lat(lambda device: merid_back(turn, device, my).start())
        mres[turn, my] = mret[turn, my]

    def merid_edges(turn, field):
        for half in range(2):
            solver = 2 * field + half

            @pl.when(my != solver)
            def _(solver=solver):
                merid_back(turn, 0, solver).wait_recv()

        own = jnp.concatenate([mres[turn, 2 * field, 0], mres[turn, 2 * field + 1, 0]], axis=0)
        after = jnp.concatenate([mres[turn, 2 * field, 1], mres[turn, 2 * field + 1, 1]], axis=0)
        ubuf[...] = own
        gbuf[...] = after * mco_ref[field, 0:1, :] + mtot[field]

    def merid_value(field, row):
        return (
            x_ref[field, row]
            + mr_ref[field, pl.ds(row, 1), :] * ubuf[...]
            + ms_ref[field, pl.ds(row, 1), :] * gbuf[...]
        )

    nothing = jnp.zeros((ZP, LANES), F32)

    acc_a[...] = nothing
    acc_b[...] = nothing
    for field in range(NF):

        def first_pass(chunk, _, field=field):
            zonal_pass(field, chunk, lambda row, step: field_ref[field, row], field * NLAT)
            return 0

        lax.fori_loop(0, NLAT // CHUNK, first_pass, 0)
    zonal_send(0)

    @pl.when(is_solver)
    def _():
        zonal_factor()

    vertical_field(0)

    @pl.when(is_solver)
    def _():
        zonal_reduced(0)

    vertical_field(1)
    zonal_receive(0)
    both = jnp.concatenate([ubuf[...], gbuf[...]], axis=1)
    upper = vertical(0, both)
    lower = vertical(1, both)
    first_field = iota < NLAT
    ubuf[...] = jnp.where(first_field, upper[:, :LANES], lower[:, :LANES])
    gbuf[...] = jnp.where(first_field, upper[:, LANES:], lower[:, LANES:])

    for field in range(NF):

        def second_pass(chunk, carry, field=field):
            tot_a, tot_b = carry
            found = zonal_values(field, chunk, field * NLAT)
            for step in range(CHUNK):
                tot_a, tot_b = merid_step(field, chunk * CHUNK + step, found[step], tot_a, tot_b)
            return tot_a, tot_b

        tot_a, tot_b = lax.fori_loop(0, NLAT // CHUNK, second_pass, (nothing, nothing))
        merid_send(0, field, tot_a, tot_b)
    merid_reduced(0)

    for field in range(NF):
        merid_edges(0, field)

        def third_pass(row, carry, field=field):
            return merid_step(field, row, merid_value(field, row), *carry)

        tot_a, tot_b = lax.fori_loop(0, NLAT, third_pass, (nothing, nothing), unroll=2)
        merid_send(1, field, tot_a, tot_b)
    merid_reduced(1)

    acc_a[...] = nothing
    acc_b[...] = nothing
    for field in range(NF):
        merid_edges(1, field)

        def fourth_pass(chunk, _, field=field):
            zonal_pass(field, chunk, lambda row, step: merid_value(field, row), field * NLAT)
            return 0

        lax.fori_loop(0, NLAT // CHUNK, fourth_pass, 0)
    zonal_send(1)

    @pl.when(is_solver)
    def _():
        zonal_reduced(1)

    zonal_receive(1)
    for field in range(NF):

        def last_pass(chunk, _, field=field):
            found = zonal_values(field, chunk, field * NLAT)
            for step in range(CHUNK):
                row = chunk * CHUNK + step
                x_ref[field, row] = found[step] * scale_ref[field, row]
            return 0

        lax.fori_loop(0, NLAT // CHUNK, last_pass, 0)

    over_solvers(lambda device: zco_copy(device, me).wait_send())
    over_lat(lambda device: mco_copy(device, my).wait_send())
    for turn in range(2):
        over_solvers(lambda device: zonal_out(turn, device, me).wait_send())
        over_lat(lambda device: merid_out(turn, device, my).wait_send())
        over_lat(lambda device: merid_back(turn, device, my).wait_send())

        @pl.when(is_solver)
        def _(turn=turn):
            over_lon(lambda device: zonal_back(turn, device, me).wait_send())


def solve(field, scale, coefs, vert, sums):
    dma = pltpu.SemaphoreType.DMA
    vmem = lambda *dims: pltpu.VMEM(dims, F32)
    return pl.pallas_call(
        solve_kernel,
        out_shape=jax.ShapeDtypeStruct((NF, NLAT, ZP, LANES), F32),
        in_specs=[VMEM_SPEC] * 10,
        out_specs=VMEM_SPEC,
        scratch_shapes=[
            vmem(N_LON, 8, LANES), vmem(N_LAT, NF, 8, LANES),
            vmem(5, N_LON, LANES), vmem(5, N_LON, LANES), vmem(N_LON, LANES),
            vmem(2, SOLVERS, 8, LANES), vmem(2, N_LON, 8, LANES),
            vmem(2, N_LON, 8, LANES), vmem(2, SOLVERS, 8, LANES),
            vmem(2, N_LAT, 2, 40, LANES), vmem(2, N_LAT, 2, 40, LANES),
            vmem(2, N_LAT, 2, 40, LANES), vmem(2, N_LAT, 2, 40, LANES),
            vmem(ZP, LANES), vmem(ZP, LANES), vmem(ZP, LANES), vmem(ZP, LANES),
            vmem(NF, ZP, LANES),
            dma((N_LON,)), dma((N_LON,)), dma((N_LAT,)), dma((N_LAT,)),
            dma((2, N_LON)), dma((2, N_LON)), dma((2, N_LON)), dma((2, N_LON)),
            dma((2, N_LAT)), dma((2, N_LAT)), dma((2, N_LAT)), dma((2, N_LAT)),
        ],
        compiler_params=pltpu.CompilerParams(
            collective_id=1, has_side_effects=True, vmem_limit_bytes=40 << 20
        ),
        name="solve",
    )(field, scale, *coefs, vert, sums)


def pick_kernel(rows_ref, lane_ref, x_ref, out_ref, copy_ref):
    iota = lane_iota(8)

    def sender(q, acc):
        slot = q & 1
        for k in range(CAP):
            row = rows_ref[q * CAP + k]
            copy_ref[slot, k : k + 1, :] = x_ref[pl.ds(row, 1), :]
        result = []
        for part in range(CAP // 8):
            at = slice(8 * part, 8 * part + 8)
            found = lane_pick(copy_ref[slot, at, :], lane_ref[at, :])
            result.append(jnp.where(iota == q, found, acc[part]))
        return tuple(result)

    acc = lax.fori_loop(0, RANKS, sender, (jnp.zeros((8, LANES), F32),) * (CAP // 8))
    whole = jnp.concatenate(list(acc) + [jnp.zeros((LANES - CAP, LANES), F32)], axis=0)
    out_ref[...] = jnp.transpose(whole)[:, :CAP]


def pick(rows, lanes, increment):
    return pl.pallas_call(
        pick_kernel,
        out_shape=jax.ShapeDtypeStruct((RANKS, CAP), F32),
        in_specs=[SMEM_SPEC, VMEM_SPEC, VMEM_SPEC],
        out_specs=VMEM_SPEC,
        scratch_shapes=[pltpu.VMEM((2, CAP, LANES), F32)],
        compiler_params=pltpu.CompilerParams(vmem_limit_bytes=40 << 20),
        name="pick",
    )(rows, lanes, increment.reshape(ROWS, LANES))


def place_kernel(back_ref, send_ref, out_ref, idx_ref, val_ref):
    idx_ref[...] = jnp.full((RANKS, LANES), -1, jnp.int32)
    idx_ref[:, :CAP] = send_ref[...]
    val_ref[...] = jnp.zeros((RANKS, LANES), F32)
    val_ref[:, :CAP] = back_ref[...]
    row_iota = lax.broadcasted_iota(jnp.int32, (CAP, 2 * LANES), 0)
    col_iota = lax.broadcasted_iota(jnp.int32, (LANES, 2 * LANES), 0)

    def pair(step, acc):
        first, second = pl.ds(2 * step, 1), pl.ds(2 * step + 1, 1)
        index = jnp.concatenate([idx_ref[first, :], idx_ref[second, :]], axis=1)
        value = jnp.concatenate([val_ref[first, :], val_ref[second, :]], axis=1)
        high = value.astype(BF16).astype(F32)
        low = value - high
        rows = jnp.where(row_iota == (index >> 7), 1.0, 0.0).astype(BF16)
        here = col_iota == (index & 127)
        columns = jnp.concatenate(
            [jnp.where(here, high, 0.0).astype(BF16), jnp.where(here, low, 0.0).astype(BF16)], axis=0
        )
        return acc + lax.dot_general(
            rows, columns, (((1,), (1,)), ((), ())), preferred_element_type=F32
        )

    acc = lax.fori_loop(0, RANKS // 2, pair, jnp.zeros((CAP, 2 * LANES), F32), unroll=2)
    out_ref[...] = acc[:, :LANES] + acc[:, LANES:]


def place(back, send_list):
    return pl.pallas_call(
        place_kernel,
        out_shape=jax.ShapeDtypeStruct((CAP, LANES), F32),
        in_specs=[VMEM_SPEC] * 2,
        out_specs=VMEM_SPEC,
        scratch_shapes=[pltpu.VMEM((RANKS, LANES), jnp.int32), pltpu.VMEM((RANKS, LANES), F32)],
        compiler_params=pltpu.CompilerParams(vmem_limit_bytes=16 << 20),
        name="place",
    )(back, send_list)


def exchange(values):
    return lax.all_to_all(values, ("lon", "lat"), split_axis=0, concat_axis=0, tiled=True)


def local(
    obs_value, send_list, recv_cell, column_depth, zonal_weight, merid_weight, vert_inverse, norm_scale
):
    is_north = lax.axis_index("lat") == N_LAT - 1
    north = jnp.full((8, LANES), jnp.where(is_north, 1.0, 0.0), F32)
    padded = jnp.pad(vert_inverse, ((0, 0), (0, ZP - NZ), (0, ZP - NZ)))
    outgoing, *coefs, vert = prepare(
        obs_value.reshape(CAP, LANES), send_list, zonal_weight, merid_weight, north, padded
    )
    incoming = exchange(outgoing)

    cell = jnp.maximum(recv_cell, 0)
    line = cell >> 7
    lat_row = line % NLAT
    plane = line // NLAT
    field = plane // NZ
    level = plane - field * NZ
    rows = ((field * NLAT + lat_row) * ZP + level).reshape(-1)
    lanes = jnp.transpose(cell & 127)

    sums = jnp.where(
        (jnp.arange(2 * LANES)[:, None] % LANES <= jnp.arange(2 * LANES)[None, :]), 1.0, 0.0
    ).astype(BF16)

    norm = jnp.pad(jnp.transpose(norm_scale, (0, 2, 1, 3)), ((0, 0), (0, 0), (0, ZP - NZ), (0, 0)))
    gridded, scale = scatter(rows, lanes, incoming, column_depth, norm)
    whole = solve(gridded, scale, coefs, vert, sums)
    picked = pick(rows, lanes, whole)
    returned = exchange(picked)
    result = place(returned, send_list)
    increment = jnp.transpose(whole[:, :, :NZ], (0, 2, 1, 3))
    return increment, result.reshape(-1)


def solution(mesh):
    in_specs = (
        P(("lon", "lat")),
        P(("lon", "lat"), None),
        P(("lon", "lat"), None),
        P("lat", "lon"),
        P(None, "lat", "lon"),
        P(None, "lat", "lon"),
        P(),
        P(None, None, "lat", "lon"),
    )
    out_specs = (P(None, None, "lat", "lon"), P(("lon", "lat")))
    return jax.shard_map(local, mesh=mesh, in_specs=in_specs, out_specs=out_specs, check_vma=False)
```

profile of v0, /device:TPU:1, one launch (start us, length us, event | category | flops | bytes accessed | tf_op | source)
XLA Modules:
  0.0 179.2 jit_solution(12888485274882272763)
XLA Ops:
  0.6 0.9 copy.23.send_ref
  1.5 0.9 copy.22
  2.4 0.0 copy-start.2
  2.4 0.8 copy-done.2
  3.2 0.8 copy-done.3
  4.0 0.8 copy-done.4
  4.8 7.8 %prepare.1 = (f32[128,80]{1,0:T(8,128)}, f32[80,128]{1,0:T(8,128)S(1)}, f32[80,128]{1,0:T(8,128)S(1)}, f32[8,128]{1,0:T(8,128)S(1)}, f32[2,40,128]{2,1,0:T(8,128...) custom-call(f32[80,128]{1,0:T(8,128)S(1)} %bitcast.21, ...), custom_call_target="tpu_custom_call" | custom-call | tf_op jit(solution)/shard_map/prepare/pallas_call | solution.py:124
  12.6 0.6 copy-done
  13.2 0.6 copy-done.5
  13.8 0.6 copy-done.7
  14.5 0.6 copy-done.9
  15.1 0.6 copy-done.11
  15.7 0.6 copy-done.14
  16.3 0.6 copy-done.16
  16.9 12.0 %all-to-all-start = ((f32[128,1,80]{2,1,0:T(1,128)}), f32[128,1,80]{2,1,0:T(1,128)}, u32[]{:S(2)}, u32[]{:S(2)}) async-start(f32[128,1,80]{2,1,0:T(1,128)} %bitcast.4), calls=%async_computation | async-start | bytes 131072 | tf_op jit(solution)/shard_map/all_to_all | solution.py:678
  28.8 0.1 select_convert_fusion.sums_ref
  28.9 0.9 and_bitcast_fusion
  29.8 0.1 copy.21
  29.9 0.1 reshape.38.rows_ref
  30.0 2.5 %copy.30 = f32[2,75,40,128]{3,1,2,0:T(8,128)S(1)} copy(f32[2,75,40,128]{3,2,1,0:T(8,128)} %param.15) | data formatting | bytes 6144000 | tf_op args[7]
  32.5 0.2 pad.9.norm_ref
  32.7 5.9 %all-to-all-done = f32[128,1,80]{2,1,0:T(1,128)} async-done(((f32[128,1,80]{2,1,0:T(1,128)}), f32[128,1,80]{2,1,0:T(1,128)}, u32[]{:S(2)}, u32[]{:S(2)}) %all-to-all-start) | async-done | bytes 40992 | tf_op jit(solution)/shard_map/all_to_all | solution.py:678
  38.7 0.0 copy-start.13
  38.7 0.8 copy-done.13
  39.4 32.8 %scatter.1 = (f32[2,40,80,128]{3,2,1,0:T(8,128)S(1)}, f32[2,40,80,128]{3,2,1,0:T(8,128)S(1)}) custom-call(s32[10240]{0:T(1024)S(1)} %reshape.38.rows_ref, s32[80,128]{1,0:T(8,128)S(1)} %get-tuple-element.28.lane_ref, f32[128,80]{1,0:T(8,128)} %bitcast.5.in_ref, s32[40,128]{1,0:T(8,128)S(1)} %copy-done.13, f32[2,40,80,128]{3,2,1,0:T(8,128)S(1)} %pad.9.norm_ref), custom_call_target="tpu_custom_call" | custom-call | tf_op jit(solution)/shard_map/scatter/pallas_call | solution.py:194
  72.2 62.1 %solve.1 = f32[2,40,80,128]{3,2,1,0:T(8,128)S(1)} custom-call(f32[2,40,80,128]{3,2,1,0:T(8,128)S(1)} %get-tuple-element.13.field_ref, f32[2,40,80,128]{3,2,1,0:T(8,128)S(1)} %get-tuple-element.14.scale_ref, f32[80,128]{1,0:T(8,128)S(1)} %copy-done.6, f32[80,128]{1,0:T(8,128)S(1)} %copy-done.8, f32[8,128]{1,0:T(8,128)S(1)} %copy-done.17, ...), custom_call_target="tpu_custom_call" | custom-call | tf_op jit(solution)/shard_map/solve/pallas_call | solution.py:581
  134.4 21.5 %pick.1 = f32[128,80]{1,0:T(8,128)} custom-call(s32[10240]{0:T(1024)S(1)} %reshape.38.rows_ref, s32[80,128]{1,0:T(8,128)S(1)} %get-tuple-element.28.lane_ref, f32[6400,128]{1,0:T(8,128)S(1)} %bitcast.19), custom_call_target="tpu_custom_call" | custom-call | tf_op jit(solution)/shard_map/pick/pallas_call | solution.py:627
  155.9 5.8 %all-to-all-start.1 = ((f32[128,1,80]{2,1,0:T(1,128)}), f32[128,1,80]{2,1,0:T(1,128)S(1)}, u32[]{:S(2)}, u32[]{:S(2)}) async-start(f32[128,1,80]{2,1,0:T(1,128)} %bitcast.10), calls=%async_computation.1 | async-start | bytes 131072 | tf_op jit(solution)/shard_map/all_to_all | solution.py:678
  161.7 0.2 slice_bitcast_fusion
  161.9 2.6 %copy.28 = f32[2,75,40,128]{3,2,1,0:T(8,128)} copy(f32[2,75,40,128]{3,1,2,0:T(8,128)S(1)} %slice_bitcast_fusion) | data formatting | bytes 6144000
  164.4 7.1 %all-to-all-done.1 = f32[128,1,80]{2,1,0:T(1,128)S(1)} async-done(((f32[128,1,80]{2,1,0:T(1,128)}), f32[128,1,80]{2,1,0:T(1,128)S(1)}, u32[]{:S(2)}, u32[]{:S(2)}) %all-to-all-start.1) | async-done | bytes 40992 | tf_op jit(solution)/shard_map/all_to_all | solution.py:678
  171.5 7.6 %place.1 = f32[80,128]{1,0:T(8,128)} custom-call(f32[128,80]{1,0:T(8,128)S(1)} %bitcast.20, s32[128,80]{1,0:T(8,128)S(1)} %copy.23.send_ref), custom_call_target="tpu_custom_call" | custom-call | tf_op jit(solution)/shard_map/place/pallas_call | solution.py:666
  (26 shorter events, 0.1 us)
Async XLA Ops:
  2.4 0.8 copy-start.2
  3.2 0.8 copy-start.3
  4.0 0.8 copy-start.4
  12.6 0.6 copy-start
  13.2 0.6 copy-start.5
  13.8 0.6 copy-start.7
  14.5 0.6 copy-start.9
  15.1 0.6 copy-start.11
  15.7 0.6 copy-start.14
  16.3 0.6 copy-start.16
  16.9 21.8 %all-to-all-start = ((f32[128,1,80]{2,1,0:T(1,128)}), f32[128,1,80]{2,1,0:T(1,128)}, u32[]{:S(2)}, u32[]{:S(2)}) async-start(f32[128,1,80]{2,1,0:T(1,128)} %bitcast.4), calls=%async_computation | async-start | bytes 131072 | tf_op jit(solution)/shard_map/all_to_all | solution.py:678
  38.6 33.6 %copy-start.1 = (bf16[2,80,240]{2,1,0:T(8,128)(2,1)S(1)}, bf16[2,80,240]{2,1,0:T(8,128)(2,1)}, u32[]{:S(2)}) copy-start(bf16[2,80,240]{2,1,0:T(8,128)(2,1)} %copy-done) | copy-start | bytes 230404
  38.6 33.6 %copy-start.6 = (f32[80,128]{1,0:T(8,128)S(1)}, f32[80,128]{1,0:T(8,128)}, u32[]{:S(2)}) copy-start(f32[80,128]{1,0:T(8,128)} %copy-done.5) | copy-start | bytes 122884
  38.6 33.6 %copy-start.8 = (f32[80,128]{1,0:T(8,128)S(1)}, f32[80,128]{1,0:T(8,128)}, u32[]{:S(2)}) copy-start(f32[80,128]{1,0:T(8,128)} %copy-done.7) | copy-start | bytes 122884
  38.6 33.6 %copy-start.10 = (f32[2,40,128]{2,1,0:T(8,128)S(1)}, f32[2,40,128]{2,1,0:T(8,128)}, u32[]{:S(2)}) copy-start(f32[2,40,128]{2,1,0:T(8,128)} %copy-done.9) | copy-start | bytes 122884
  38.6 33.6 %copy-start.12 = (f32[2,40,128]{2,1,0:T(8,128)S(1)}, f32[2,40,128]{2,1,0:T(8,128)}, u32[]{:S(2)}) copy-start(f32[2,40,128]{2,1,0:T(8,128)} %copy-done.11) | copy-start | bytes 122884
  38.7 0.8 copy-start.13
  39.4 32.8 %copy-start.15 = (f32[2,8,128]{2,1,0:T(8,128)S(1)}, f32[2,8,128]{2,1,0:T(8,128)}, u32[]{:S(2)}) copy-start(f32[2,8,128]{2,1,0:T(8,128)} %copy-done.14) | copy-start | bytes 24580
  39.4 32.8 %copy-start.17 = (f32[8,128]{1,0:T(8,128)S(1)}, f32[8,128]{1,0:T(8,128)}, u32[]{:S(2)}) copy-start(f32[8,128]{1,0:T(8,128)} %copy-done.16) | copy-start | bytes 12292
  155.9 15.7 %all-to-all-start.1 = ((f32[128,1,80]{2,1,0:T(1,128)}), f32[128,1,80]{2,1,0:T(1,128)S(1)}, u32[]{:S(2)}, u32[]{:S(2)}) async-start(f32[128,1,80]{2,1,0:T(1,128)} %bitcast.10), calls=%async_computation.1 | async-start | bytes 131072 | tf_op jit(solution)/shard_map/all_to_all | solution.py:678
where the time goes:
time: 180 us; the launch traced here: 179 us
  Pallas kernels  132 us (73%)
  starting transfers between devices  17.7 us (10%)
  local copies, waits for them, and re-layouts  14.8 us (8%)
  waiting for transfers between devices  13 us (7%)
    pallas_call x1, Pallas kernels, solve(): pl.pallas_call(solve_kernel, out_shape=jax.ShapeDtypeStruct((NF, NLAT, ZP...  62.1 us
    pallas_call x1, Pallas kernels, scatter(): pl.pallas_call(scatter_kernel, out_shape=(full, full), in_specs=[SMEM_SPE...  32.8 us
    pallas_call x1, Pallas kernels, pick(): pl.pallas_call(pick_kernel, out_shape=jax.ShapeDtypeStruct((RANKS, CAP),...  21.5 us
    all_to_all x2, starting transfers between devices, exchange(): lax.all_to_all(values, ('lon', 'lat'), split_axis=0, concat_axis=0, tiled...  17.7 us
    unnamed x40, local copies, waits for them, and re-layouts  14.2 us
    all_to_all x2, waiting for transfers between devices, exchange(): lax.all_to_all(values, ('lon', 'lat'), split_axis=0, concat_axis=0, tiled...  13 us
    pallas_call x1, Pallas kernels, prepare(): pl.pallas_call(prepare_kernel, out_shape=(shape(RANKS, CAP), shape(80, LA...  7.81 us
    pallas_call x1, Pallas kernels, place(): pl.pallas_call(place_kernel, out_shape=jax.ShapeDtypeStruct((CAP, LANES),...  7.64 us
  transfers between devices with their start and end apart: 2, of which 2 were waited for; matrix products, arithmetic and copies ran while one was open for 4% of the time, Pallas kernels for 0%

commit v1 on v0

--- a/solution.py
+++ b/solution.py
@@ -14,8 +14,8 @@
 N_LON, N_LAT = 32, 4
 SOLVERS = 19
 LANES = 128
-CHUNK = 4
-GRIDS = 4
+CHUNK = 8
+GRIDS = 8
 ROWS = NF * NLAT * ZP
 VMEM_SPEC = pl.BlockSpec(memory_space=pltpu.VMEM)
 SMEM_SPEC = pl.BlockSpec(memory_space=pltpu.SMEM)
@@ -35,38 +35,58 @@
     return jnp.take_along_axis(table, index, axis=1, mode="promise_in_bounds")
 
 
-def prepare_kernel(
-    obs_ref, send_ref, zw_ref, mw_ref, north_ref, vert_in,
-    out_ref, zs_ref, zr_ref, zco_ref, ms_ref, mr_ref, mco_ref, vert_ref,
-    idx_ref, iw_ref, st_ref, rt_ref, miw_ref,
-):
-    for field in range(NF):
-        product = lax.dot_general(
-            vert_in[field], vert_in[field], (((1,), (1,)), ((), ())),
-            precision=lax.Precision.HIGHEST, preferred_element_type=F32,
-        )
-        high, low = split(product)
-        vert_ref[field] = jnp.concatenate([high, low, high], axis=1)
-    idx_ref[...] = jnp.full((RANKS, LANES), -1, jnp.int32)
-    idx_ref[:, :CAP] = send_ref[...]
-    part = 64
-    for start in range(0, RANKS, part):
-        index = idx_ref[start : start + part, :]
-        low = index & 127
-        high = index >> 7
-
-        def gather_row(row, acc, low=low, high=high):
-            line = jnp.broadcast_to(obs_ref[pl.ds(row, 1), :], (part, LANES))
-            return jnp.where(high == row, lane_pick(line, low), acc)
-
-        picked = lax.fori_loop(0, CAP, gather_row, jnp.zeros((part, LANES), F32), unroll=4)
-        out_ref[start : start + part, :] = picked[:, :CAP]
-
+def push(source, target, send_sem, recv_sem, axis, device):
+    return pltpu.make_async_remote_copy(
+        src_ref=source, dst_ref=target, send_sem=send_sem, recv_sem=recv_sem,
+        device_id={axis: device}, device_id_type=MESH,
+    )
+
+
+def over(axis, count, action, limit=None):
+    mine = lax.axis_index(axis)
+
+    def body(step, _):
+        device = (mine + step) % count
+        if limit is None:
+            action(device)
+        else:
+            pl.when(device < limit)(lambda: action(device))
+        return 0
+
+    lax.fori_loop(1, count, body, 0)
+
+
+def over_lon(action, limit=None):
+    over("lon", N_LON, action, limit)
+
+
+def over_lat(action):
+    over("lat", N_LAT, action)
+
+
+def greet():
+    barrier = pltpu.get_barrier_semaphore()
+    over_lon(
+        lambda device: pl.semaphore_signal(
+            barrier, inc=1, device_id={"lon": device}, device_id_type=MESH
+        )
+    )
+    over_lat(
+        lambda device: pl.semaphore_signal(
+            barrier, inc=1, device_id={"lat": device}, device_id_type=MESH
+        )
+    )
+
+
+def greeted():
+    pl.semaphore_wait(pltpu.get_barrier_semaphore(), N_LON - 1 + N_LAT - 1)
+
+
+def zonal_coefs(zw_ref, zs_ref, zr_ref, zco_ref, iw_ref, st_ref, rt_ref, zero):
+    one = zero + 1.0
     iw_ref[...] = jnp.full((LANES, LANES), 1e-3, F32)
     iw_ref[: NF * NLAT, :] = 1.0 / zw_ref[...]
     iw_ref[...] = jnp.transpose(iw_ref[...])
-    zero = north_ref[...] * 0.0
-    one = zero + 1.0
 
     def zonal_step(step, carry):
         s_val, s_flux, s_sum, r_val, r_flux, r_sum = carry
@@ -92,7 +112,9 @@
     zs_ref[...] = jnp.transpose(st_ref[...])[: NF * NLAT, :]
     zr_ref[...] = jnp.transpose(rt_ref[...] * coupling)[: NF * NLAT, :]
 
-    north = north_ref[...]
+
+def merid_coefs(mw_ref, ms_ref, mr_ref, mco_ref, miw_ref, north, zero):
+    one = zero + 1.0
     miw_ref[...] = 1.0 / mw_ref[...]
     mco_ref[...] = jnp.zeros((NF, 8, LANES), F32)
     for field in range(NF):
@@ -119,32 +141,150 @@
         mco_ref[field, 2:3, :] = s_sum[0:1] * coupling
 
 
+def zonal_factor(zco_all, alpha, gamma, minv):
+    coupling = zco_all[:, 0, :]
+    west = jnp.concatenate([coupling[-1:], coupling[:-1]], axis=0)
+    spill = zco_all[:, 2, :]
+    mass = 1.0 + zco_all[:, 1, :] + jnp.concatenate([spill[-1:], spill[:-1]], axis=0)
+    east = coupling
+    for bit in range(5):
+        stride = 1 << bit
+        down = lambda v: jnp.concatenate([v[-stride:], v[:-stride]], axis=0)
+        up = lambda v: jnp.concatenate([v[stride:], v[:stride]], axis=0)
+        inverse = 1.0 / (mass + west + east)
+        left = west * down(inverse)
+        right = east * up(inverse)
+        alpha[bit] = left
+        gamma[bit] = right
+        mass = mass + left * down(mass) + right * up(mass)
+        west, east = left * down(west), right * up(east)
+    minv[...] = 1.0 / mass
+
+
+def prepare_kernel(
+    obs_ref, send_ref, zw_ref, mw_ref, north_ref, vert_in,
+    out_ref, zs_ref, zr_ref, zco_ref, ms_ref, mr_ref, mco_out, vert_ref, alpha, gamma, minv,
+    idx_ref, iw_ref, st_ref, rt_ref, miw_ref,
+    tile_out, tile_in, rows_out, rows_in, zco_all, mco_ref, mco_all,
+    o1s, o1r, o2s, o2r, zco_s, zco_r, mco_s, mco_r,
+):
+    me = lax.axis_index("lon")
+    my = lax.axis_index("lat")
+    greet()
+    idx_ref[...] = jnp.full((RANKS, LANES), -1, jnp.int32)
+    idx_ref[:, :CAP] = send_ref[...]
+    part = 64
+    for start in range(0, RANKS, part):
+        index = idx_ref[start : start + part, :]
+        low = index & 127
+        high = index >> 7
+
+        def gather_row(row, acc, low=low, high=high):
+            line = jnp.broadcast_to(obs_ref[pl.ds(row, 1), :], (part, LANES))
+            return jnp.where(high == row, lane_pick(line, low), acc)
+
+        picked = lax.fori_loop(0, CAP, gather_row, jnp.zeros((part, LANES), F32), unroll=8)
+        for step in range(part // N_LAT):
+            device = start // N_LAT + step
+            tile_out[device, 0:4, :] = picked[4 * step : 4 * step + 4]
+            tile_out[device, 4:8, :] = jnp.zeros((4, LANES), F32)
+
+    first = lambda device, slot: push(
+        tile_out.at[device], tile_in.at[slot], o1s.at[device], o1r.at[slot], "lon", device
+    )
+    second = lambda device, slot: push(
+        rows_out.at[device], rows_in.at[slot], o2s.at[device], o2r.at[slot], "lat", device
+    )
+    zco_copy = lambda device, slot: push(
+        zco_ref, zco_all.at[slot], zco_s.at[device], zco_r.at[slot], "lon", device
+    )
+    mco_copy = lambda device, slot: push(
+        mco_ref, mco_all.at[slot], mco_s.at[device], mco_r.at[slot], "lat", device
+    )
+    greeted()
+    over_lon(lambda device: first(device, me).start())
+    tile_in[me] = tile_out[me]
+
+    zero = north_ref[...] * 0.0
+    zonal_coefs(zw_ref, zs_ref, zr_ref, zco_ref, iw_ref, st_ref, rt_ref, zero)
+    over_lon(lambda device: first(0, device).wait_recv())
+    for lat in range(N_LAT):
+        rows_out[lat] = tile_in[:, lat, :]
+    over_lat(lambda device: second(device, my).start())
+    rows_in[my] = rows_out[my]
+    over_lon(lambda device: zco_copy(device, me).start())
+    zco_all[me] = zco_ref[...]
+    merid_coefs(mw_ref, ms_ref, mr_ref, mco_ref, miw_ref, north_ref[...], zero)
+    over_lat(lambda device: mco_copy(device, my).start())
+    mco_all[my] = mco_ref[...]
+    for field in range(NF):
+        product = lax.dot_general(
+            vert_in[field], vert_in[field], (((1,), (1,)), ((), ())),
+            precision=lax.Precision.HIGHEST, preferred_element_type=F32,
+        )
+        high, low = split(product)
+        vert_ref[field] = jnp.concatenate([high, low, high], axis=1)
+    over_lon(lambda device: zco_copy(0, device).wait_recv())
+    zonal_factor(zco_all, alpha, gamma, minv)
+    over_lat(lambda device: second(0, device).wait_recv())
+    for lat in range(N_LAT):
+        out_ref[N_LON * lat : N_LON * lat + N_LON, :] = rows_in[lat]
+    over_lat(lambda device: mco_copy(0, device).wait_recv())
+    mco_out[...] = mco_all[...]
+    over_lon(lambda device: first(device, me).wait_send())
+    over_lat(lambda device: second(device, my).wait_send())
+    over_lon(lambda device: zco_copy(device, me).wait_send())
+    over_lat(lambda device: mco_copy(device, my).wait_send())
+
+
 def prepare(obs, send_list, zonal_weight, merid_weight, north, vert_inverse):
     shape = lambda *dims: jax.ShapeDtypeStruct(dims, F32)
+    vmem = lambda *dims: pltpu.VMEM(dims, F32)
+    dma = pltpu.SemaphoreType.DMA
     return pl.pallas_call(
         prepare_kernel,
         out_shape=(
-            shape(RANKS, CAP), shape(80, LANES), shape(80, LANES), shape(8, LANES),
-            shape(NF, NLAT, LANES), shape(NF, NLAT, LANES), shape(NF, 8, LANES),
+            shape(RANKS, LANES), shape(80, LANES), shape(80, LANES), shape(8, LANES),
+            shape(NF, NLAT, LANES), shape(NF, NLAT, LANES), shape(N_LAT, NF, 8, LANES),
             jax.ShapeDtypeStruct((NF, ZP, 3 * ZP), BF16),
+            shape(5, N_LON, LANES), shape(5, N_LON, LANES), shape(N_LON, LANES),
         ),
         in_specs=[VMEM_SPEC] * 6,
-        out_specs=(VMEM_SPEC,) * 8,
+        out_specs=(VMEM_SPEC,) * 11,
         scratch_shapes=[
             pltpu.VMEM((RANKS, LANES), jnp.int32),
-            pltpu.VMEM((LANES, LANES), F32),
-            pltpu.VMEM((LANES, LANES), F32),
-            pltpu.VMEM((LANES, LANES), F32),
-            pltpu.VMEM((NF, NLAT, LANES), F32),
+            vmem(LANES, LANES), vmem(LANES, LANES), vmem(LANES, LANES), vmem(NF, NLAT, LANES),
+            vmem(N_LON, 8, LANES), vmem(N_LON, 8, LANES),
+            vmem(N_LAT, N_LON, LANES), vmem(N_LAT, N_LON, LANES),
+            vmem(N_LON, 8, LANES), vmem(NF, 8, LANES), vmem(N_LAT, NF, 8, LANES),
+            dma((N_LON,)), dma((N_LON,)), dma((N_LAT,)), dma((N_LAT,)),
+            dma((N_LON,)), dma((N_LON,)), dma((N_LAT,)), dma((N_LAT,)),
         ],
-        compiler_params=pltpu.CompilerParams(vmem_limit_bytes=16 << 20),
+        compiler_params=pltpu.CompilerParams(
+            collective_id=0, has_side_effects=True, vmem_limit_bytes=4 << 20
+        ),
         name="prepare",
     )(obs, send_list, zonal_weight.reshape(NF * NLAT, LANES), merid_weight, north, vert_inverse)
 
 
-def scatter_kernel(rows_ref, lane_ref, in_ref, depth_ref, norm_ref, field_ref, scale_ref, *scratch):
-    grids = scratch[:GRIDS]
-    value_ref, spread_ref = scratch[GRIDS:]
+def scatter_kernel(
+    rows_ref, lane_ref, in_ref, depth_ref, norm_ref, field_ref, scale_ref, norm_buf, norm_sem,
+    value_ref, even_ref, odd_ref, *grids
+):
+    def norm_copy(field, row):
+        return pltpu.make_async_copy(
+            norm_ref.at[field, :, row, :],
+            norm_buf.at[field, row, pl.ds(0, NZ), :],
+            norm_sem.at[field, row],
+        )
+
+    for field in range(NF):
+
+        def begin(row, _, field=field):
+            norm_copy(field, row).start()
+            return 0
+
+        lax.fori_loop(0, NLAT, begin, 0)
 
     def clear(step, _):
         at = pl.ds(pl.multiple_of(step * 64, 64), 64)
@@ -153,37 +293,44 @@
         return 0
 
     lax.fori_loop(0, ROWS // 64, clear, 0)
-    value_ref[...] = jnp.zeros((RANKS, LANES), F32)
-    value_ref[:, :CAP] = in_ref[...]
-    value_ref[...] = jnp.transpose(value_ref[...])
+    value_ref[...] = jnp.transpose(in_ref[...])
     iota = lane_iota(CAP)
 
-    def sender(q, _):
+    def spread(q):
         index = jnp.full((CAP, LANES), q, jnp.int32)
-        value = lane_pick(value_ref[:CAP, :], index)
         lane = lane_pick(lane_ref[...], index)
-        slot = q & 1
-        spread_ref[slot] = jnp.where(iota == lane, value, 0.0)
+        return jnp.where(iota == lane, lane_pick(value_ref[:CAP, :], index), 0.0)
+
+    def add(q, source):
         for k in range(CAP):
-            row = rows_ref[q * CAP + k]
+            at = pl.ds(rows_ref[q * CAP + k], 1)
             grid = grids[k % GRIDS]
-            at = pl.ds(row, 1)
-            grid[at, :] = grid[at, :] + spread_ref[slot, k : k + 1, :]
+            grid[at, :] = grid[at, :] + source[k : k + 1, :]
+
+    even_ref[...] = spread(0)
+
+    def senders(pair, _):
+        q = 2 * pair
+        odd_ref[...] = spread(q + 1)
+        add(q, even_ref)
+        even_ref[...] = spread(jnp.minimum(q + 2, RANKS - 1))
+        add(q + 1, odd_ref)
         return 0
 
-    lax.fori_loop(0, RANKS, sender, 0)
+    lax.fori_loop(0, RANKS // 2, senders, 0)
     level = lax.broadcasted_iota(jnp.int32, (ZP, LANES), 0)
     for field in range(NF):
 
         def finish(row, _, field=field):
+            norm_copy(field, row).wait()
             at = pl.ds(pl.multiple_of((field * NLAT + row) * ZP, ZP), ZP)
-            total = grids[0][at, :]
-            for grid in grids[1:]:
-                total = total + grid[at, :]
+            total = [grid[at, :] for grid in grids]
+            while len(total) > 1:
+                total = [one + two for one, two in zip(total[::2], total[1::2])]
             wet = level < depth_ref[pl.ds(row, 1), :]
-            scale = jnp.where(wet, norm_ref[field, row], 0.0)
+            scale = jnp.where(wet, norm_buf[field, row], 0.0)
             scale_ref[field, row] = scale
-            field_ref[field, row] = jnp.where(wet, scale * total, 0.0)
+            field_ref[field, row] = jnp.where(wet, scale * total[0], 0.0)
             return 0
 
         lax.fori_loop(0, NLAT, finish, 0)
@@ -194,85 +341,33 @@
     return pl.pallas_call(
         scatter_kernel,
         out_shape=(full, full),
-        in_specs=[SMEM_SPEC] + [VMEM_SPEC] * 4,
+        in_specs=[SMEM_SPEC] + [VMEM_SPEC] * 3 + [ANY_SPEC],
         out_specs=(VMEM_SPEC, VMEM_SPEC),
-        scratch_shapes=[pltpu.VMEM((ROWS, LANES), F32)] * GRIDS
-        + [pltpu.VMEM((RANKS, LANES), F32), pltpu.VMEM((2, CAP, LANES), F32)],
+        scratch_shapes=[
+            pltpu.VMEM((NF, NLAT, ZP, LANES), F32), pltpu.SemaphoreType.DMA((NF, NLAT)),
+            pltpu.VMEM((LANES, LANES), F32), pltpu.VMEM((CAP, LANES), F32), pltpu.VMEM((CAP, LANES), F32),
+        ]
+        + [pltpu.VMEM((ROWS, LANES), F32)] * GRIDS,
         compiler_params=pltpu.CompilerParams(vmem_limit_bytes=40 << 20),
         name="scatter",
     )(rows, lanes, incoming, depth, norm)
 
 
-def push(source, target, send_sem, recv_sem, axis, device):
-    return pltpu.make_async_remote_copy(
-        src_ref=source, dst_ref=target, send_sem=send_sem, recv_sem=recv_sem,
-        device_id={axis: device}, device_id_type=MESH,
-    )
-
-
 def solve_kernel(
-    field_ref, scale_ref, zs_ref, zr_ref, zco_ref, ms_ref, mr_ref, mco_ref, vert_ref, sums_ref,
+    field_ref, scale_ref, zs_ref, zr_ref, zco_ref, ms_ref, mr_ref, mco_all, vert_ref,
+    alpha, gamma, minv, sums_ref,
     x_ref,
-    zco_all, mco_all, alpha, gamma, minv,
     zsend, zrecv, zret, zres, msend, mrecv, mret, mres,
     acc_a, acc_b, ubuf, gbuf, mtot,
-    zco_s, zco_r, mco_s, mco_r, z1s, z1r, z2s, z2r, m1s, m1r, m2s, m2r,
+    z1s, z1r, z2s, z2r, m1s, m1r, m2s, m2r,
 ):
     me = lax.axis_index("lon")
     my = lax.axis_index("lat")
     iota = lane_iota(ZP)
     is_solver = me < SOLVERS
 
-    barrier = pltpu.get_barrier_semaphore()
-
-    def greet_lon(step, _):
-        pl.semaphore_signal(barrier, inc=1, device_id={"lon": (me + step) % N_LON}, device_id_type=MESH)
-        return 0
-
-    def greet_lat(step, _):
-        pl.semaphore_signal(barrier, inc=1, device_id={"lat": (my + step) % N_LAT}, device_id_type=MESH)
-        return 0
-
-    lax.fori_loop(1, N_LON, greet_lon, 0)
-    lax.fori_loop(1, N_LAT, greet_lat, 0)
-    pl.semaphore_wait(barrier, N_LON - 1 + N_LAT - 1)
-
-    def zco_copy(device, slot):
-        return push(zco_ref, zco_all.at[slot], zco_s.at[device], zco_r.at[slot], "lon", device)
-
-    def mco_copy(device, slot):
-        return push(mco_ref, mco_all.at[slot], mco_s.at[device], mco_r.at[slot], "lat", device)
-
-    def over_solvers(action):
-        def body(step, _):
-            device = (me + step) % N_LON
-
-            @pl.when(device < SOLVERS)
-            def _():
-                action(device)
-
-            return 0
-
-        lax.fori_loop(1, N_LON, body, 0)
-
-    def over_lon(action):
-        def body(step, _):
-            action((me + step) % N_LON)
-            return 0
-
-        lax.fori_loop(1, N_LON, body, 0)
-
-    def over_lat(action):
-        def body(step, _):
-            action((my + step) % N_LAT)
-            return 0
-
-        lax.fori_loop(1, N_LAT, body, 0)
-
-    over_solvers(lambda device: zco_copy(device, me).start())
-    over_lat(lambda device: mco_copy(device, my).start())
-    zco_all[me] = zco_ref[...]
-    mco_all[my] = mco_ref[...]
+    greet()
+    over_solvers = lambda action: over_lon(action, SOLVERS)
 
     def zonal_pass(field, chunk, load, field_base):
         lines, left = [], []
@@ -318,26 +413,6 @@
             zret.at[turn, device], zres.at[turn, slot], z2s.at[turn, device], z2r.at[turn, slot], "lon", device
         )
 
-    def zonal_factor():
-        over_lon(lambda device: zco_copy(0, device).wait_recv())
-        coupling = zco_all[:, 0, :]
-        west = jnp.concatenate([coupling[-1:], coupling[:-1]], axis=0)
-        spill = zco_all[:, 2, :]
-        mass = 1.0 + zco_all[:, 1, :] + jnp.concatenate([spill[-1:], spill[:-1]], axis=0)
-        east = coupling
-        for bit in range(5):
-            stride = 1 << bit
-            down = lambda v: jnp.concatenate([v[-stride:], v[:-stride]], axis=0)
-            up = lambda v: jnp.concatenate([v[stride:], v[:stride]], axis=0)
-            inverse = 1.0 / (mass + west + east)
-            left = west * down(inverse)
-            right = east * up(inverse)
-            alpha[bit] = left
-            gamma[bit] = right
-            mass = mass + left * down(mass) + right * up(mass)
-            west, east = left * down(west), right * up(east)
-        minv[...] = 1.0 / mass
-
     def zonal_reduced(turn):
         over_lon(lambda device: zonal_out(turn, 0, device).wait_recv())
         tiles = [zrecv[turn, k] for k in range(N_LON)]
@@ -388,15 +463,15 @@
         )
 
     def vertical_field(field):
-        def body(pair, _):
-            row = pair * 2
-            both = jnp.concatenate([x_ref[field, row], x_ref[field, row + 1]], axis=1)
-            both = vertical(field, both)
-            x_ref[field, row] = both[:, :LANES]
-            x_ref[field, row + 1] = both[:, LANES:]
+        def body(step, _):
+            row = step * CHUNK
+            value = jnp.concatenate([x_ref[field, row + k] for k in range(CHUNK)], axis=1)
+            value = vertical(field, value)
+            for k in range(CHUNK):
+                x_ref[field, row + k] = value[:, k * LANES : (k + 1) * LANES]
             return 0
 
-        lax.fori_loop(0, NLAT // 2, body, 0)
+        lax.fori_loop(0, NLAT // CHUNK, body, 0)
 
     def merid_out(turn, device, slot):
         return push(
@@ -417,7 +492,7 @@
 
     def merid_send(turn, field, tot_a, tot_b):
         mtot[field] = tot_b
-        tot_a = tot_a * mco_ref[field, 0:1, :]
+        tot_a = tot_a * mco_all[my, field, 0:1, :]
         for half in range(2):
             msend[turn, 2 * field + half, 0] = tot_b[40 * half : 40 * half + 40]
             msend[turn, 2 * field + half, 1] = tot_a[40 * half : 40 * half + 40]
@@ -433,8 +508,6 @@
                 mrecv[turn, solver] = msend[turn, solver]
 
     def merid_reduced(turn):
-        if turn == 0:
-            over_lat(lambda device: mco_copy(0, device).wait_recv())
         field = my // 2
         over_lat(lambda device: merid_out(turn, 0, device).wait_recv())
         rows = [mco_all[k, field] for k in range(N_LAT)]
@@ -471,7 +544,7 @@
         own = jnp.concatenate([mres[turn, 2 * field, 0], mres[turn, 2 * field + 1, 0]], axis=0)
         after = jnp.concatenate([mres[turn, 2 * field, 1], mres[turn, 2 * field + 1, 1]], axis=0)
         ubuf[...] = own
-        gbuf[...] = after * mco_ref[field, 0:1, :] + mtot[field]
+        gbuf[...] = after * mco_all[my, field, 0:1, :] + mtot[field]
 
     def merid_value(field, row):
         return (
@@ -491,12 +564,8 @@
             return 0
 
         lax.fori_loop(0, NLAT // CHUNK, first_pass, 0)
+    greeted()
     zonal_send(0)
-
-    @pl.when(is_solver)
-    def _():
-        zonal_factor()
-
     vertical_field(0)
 
     @pl.when(is_solver)
@@ -563,8 +632,6 @@
 
         lax.fori_loop(0, NLAT // CHUNK, last_pass, 0)
 
-    over_solvers(lambda device: zco_copy(device, me).wait_send())
-    over_lat(lambda device: mco_copy(device, my).wait_send())
     for turn in range(2):
         over_solvers(lambda device: zonal_out(turn, device, me).wait_send())
         over_lat(lambda device: merid_out(turn, device, my).wait_send())
@@ -575,78 +642,122 @@
             over_lon(lambda device: zonal_back(turn, device, me).wait_send())
 
 
-def solve(field, scale, coefs, vert, sums):
+def solve(field, scale, coefs, sums):
     dma = pltpu.SemaphoreType.DMA
     vmem = lambda *dims: pltpu.VMEM(dims, F32)
     return pl.pallas_call(
         solve_kernel,
         out_shape=jax.ShapeDtypeStruct((NF, NLAT, ZP, LANES), F32),
-        in_specs=[VMEM_SPEC] * 10,
+        in_specs=[VMEM_SPEC] * 13,
         out_specs=VMEM_SPEC,
         scratch_shapes=[
-            vmem(N_LON, 8, LANES), vmem(N_LAT, NF, 8, LANES),
-            vmem(5, N_LON, LANES), vmem(5, N_LON, LANES), vmem(N_LON, LANES),
             vmem(2, SOLVERS, 8, LANES), vmem(2, N_LON, 8, LANES),
             vmem(2, N_LON, 8, LANES), vmem(2, SOLVERS, 8, LANES),
             vmem(2, N_LAT, 2, 40, LANES), vmem(2, N_LAT, 2, 40, LANES),
             vmem(2, N_LAT, 2, 40, LANES), vmem(2, N_LAT, 2, 40, LANES),
             vmem(ZP, LANES), vmem(ZP, LANES), vmem(ZP, LANES), vmem(ZP, LANES),
             vmem(NF, ZP, LANES),
-            dma((N_LON,)), dma((N_LON,)), dma((N_LAT,)), dma((N_LAT,)),
             dma((2, N_LON)), dma((2, N_LON)), dma((2, N_LON)), dma((2, N_LON)),
             dma((2, N_LAT)), dma((2, N_LAT)), dma((2, N_LAT)), dma((2, N_LAT)),
         ],
         compiler_params=pltpu.CompilerParams(
-            collective_id=1, has_side_effects=True, vmem_limit_bytes=40 << 20
+            collective_id=1, has_side_effects=True, vmem_limit_bytes=18 << 20
         ),
         name="solve",
-    )(field, scale, *coefs, vert, sums)
-
-
-def pick_kernel(rows_ref, lane_ref, x_ref, out_ref, copy_ref):
+    )(field, scale, *coefs, sums)
+
+
+def pick_kernel(rows_ref, lane_ref, x_ref, out_ref, inc_ref, inc_sem, *copies):
     iota = lane_iota(8)
 
-    def sender(q, acc):
-        slot = q & 1
-        for k in range(CAP):
-            row = rows_ref[q * CAP + k]
-            copy_ref[slot, k : k + 1, :] = x_ref[pl.ds(row, 1), :]
-        result = []
-        for part in range(CAP // 8):
-            at = slice(8 * part, 8 * part + 8)
-            found = lane_pick(copy_ref[slot, at, :], lane_ref[at, :])
-            result.append(jnp.where(iota == q, found, acc[part]))
-        return tuple(result)
-
-    acc = lax.fori_loop(0, RANKS, sender, (jnp.zeros((8, LANES), F32),) * (CAP // 8))
+    def inc_copy(field, row):
+        return pltpu.make_async_copy(
+            x_ref.at[pl.ds(pl.multiple_of((field * NLAT + row) * ZP, ZP), NZ), :],
+            inc_ref.at[field, :, row, :],
+            inc_sem.at[field, row],
+        )
+
+    def over_rows(action):
+        for field in range(NF):
+
+            def body(row, _, field=field):
+                action(inc_copy(field, row))
+                return 0
+
+            lax.fori_loop(0, NLAT, body, 0)
+
+    over_rows(lambda copy: copy.start())
+    group = len(copies)
+
+    def senders(step, acc):
+        acc = list(acc)
+        for part in range(group):
+            q = step * group + part
+            for k in range(CAP):
+                copies[part][k : k + 1, :] = x_ref[pl.ds(rows_ref[q * CAP + k], 1), :]
+        for part in range(group):
+            q = step * group + part
+            for tile in range(CAP // 8):
+                at = slice(8 * tile, 8 * tile + 8)
+                found = lane_pick(copies[part][at, :], lane_ref[at, :])
+                acc[tile] = jnp.where(iota == q, found, acc[tile])
+        return tuple(acc)
+
+    acc = lax.fori_loop(0, RANKS // group, senders, (jnp.zeros((8, LANES), F32),) * (CAP // 8))
     whole = jnp.concatenate(list(acc) + [jnp.zeros((LANES - CAP, LANES), F32)], axis=0)
-    out_ref[...] = jnp.transpose(whole)[:, :CAP]
+    out_ref[...] = jnp.transpose(whole)
+    over_rows(lambda copy: copy.wait())
 
 
 def pick(rows, lanes, increment):
     return pl.pallas_call(
         pick_kernel,
-        out_shape=jax.ShapeDtypeStruct((RANKS, CAP), F32),
+        out_shape=(
+            jax.ShapeDtypeStruct((RANKS, LANES), F32),
+            jax.ShapeDtypeStruct((NF, NZ, NLAT, LANES), F32),
+        ),
         in_specs=[SMEM_SPEC, VMEM_SPEC, VMEM_SPEC],
-        out_specs=VMEM_SPEC,
-        scratch_shapes=[pltpu.VMEM((2, CAP, LANES), F32)],
-        compiler_params=pltpu.CompilerParams(vmem_limit_bytes=40 << 20),
+        out_specs=(VMEM_SPEC, ANY_SPEC),
+        scratch_shapes=[pltpu.SemaphoreType.DMA((NF, NLAT))] + [pltpu.VMEM((CAP, LANES), F32)] * 8,
+        compiler_params=pltpu.CompilerParams(vmem_limit_bytes=8 << 20),
         name="pick",
     )(rows, lanes, increment.reshape(ROWS, LANES))
 
 
-def place_kernel(back_ref, send_ref, out_ref, idx_ref, val_ref):
+def place_kernel(
+    picked_ref, send_ref, out_ref, idx_ref, val_ref, rows_in, tile_out, tile_in, b1s, b1r, b2s, b2r
+):
+    me = lax.axis_index("lon")
+    my = lax.axis_index("lat")
+    greet()
     idx_ref[...] = jnp.full((RANKS, LANES), -1, jnp.int32)
     idx_ref[:, :CAP] = send_ref[...]
-    val_ref[...] = jnp.zeros((RANKS, LANES), F32)
-    val_ref[:, :CAP] = back_ref[...]
+    first = lambda device, slot: push(
+        picked_ref.at[device], rows_in.at[slot], b1s.at[device], b1r.at[slot], "lat", device
+    )
+    second = lambda device, slot: push(
+        tile_out.at[device], tile_in.at[slot], b2s.at[device], b2r.at[slot], "lon", device
+    )
+    greeted()
+    over_lat(lambda device: first(device, my).start())
+    rows_in[my] = picked_ref[my]
+    tile_out[...] = jnp.zeros((N_LON, 8, LANES), F32)
+    over_lat(lambda device: first(0, device).wait_recv())
+    for device in range(N_LON):
+        for lat in range(N_LAT):
+            tile_out[device, lat : lat + 1, :] = rows_in[lat, device : device + 1, :]
+    over_lon(lambda device: second(device, me).start())
+    tile_in[me] = tile_out[me]
+    over_lon(lambda device: second(0, device).wait_recv())
+    for device in range(N_LON):
+        val_ref[4 * device : 4 * device + 4, :] = tile_in[device, 0:4, :]
     row_iota = lax.broadcasted_iota(jnp.int32, (CAP, 2 * LANES), 0)
     col_iota = lax.broadcasted_iota(jnp.int32, (LANES, 2 * LANES), 0)
 
     def pair(step, acc):
-        first, second = pl.ds(2 * step, 1), pl.ds(2 * step + 1, 1)
-        index = jnp.concatenate([idx_ref[first, :], idx_ref[second, :]], axis=1)
-        value = jnp.concatenate([val_ref[first, :], val_ref[second, :]], axis=1)
+        left, right = pl.ds(2 * step, 1), pl.ds(2 * step + 1, 1)
+        index = jnp.concatenate([idx_ref[left, :], idx_ref[right, :]], axis=1)
+        value = jnp.concatenate([val_ref[left, :], val_ref[right, :]], axis=1)
         high = value.astype(BF16).astype(F32)
         low = value - high
         rows = jnp.where(row_iota == (index >> 7), 1.0, 0.0).astype(BF16)
@@ -658,24 +769,30 @@
             rows, columns, (((1,), (1,)), ((), ())), preferred_element_type=F32
         )
 
-    acc = lax.fori_loop(0, RANKS // 2, pair, jnp.zeros((CAP, 2 * LANES), F32), unroll=2)
+    acc = lax.fori_loop(0, RANKS // 2, pair, jnp.zeros((CAP, 2 * LANES), F32), unroll=4)
     out_ref[...] = acc[:, :LANES] + acc[:, LANES:]
-
-
-def place(back, send_list):
+    over_lat(lambda device: first(device, my).wait_send())
+    over_lon(lambda device: second(device, me).wait_send())
+
+
+def place(picked, send_list):
+    vmem = lambda *dims: pltpu.VMEM(dims, F32)
+    dma = pltpu.SemaphoreType.DMA
     return pl.pallas_call(
         place_kernel,
         out_shape=jax.ShapeDtypeStruct((CAP, LANES), F32),
         in_specs=[VMEM_SPEC] * 2,
         out_specs=VMEM_SPEC,
-        scratch_shapes=[pltpu.VMEM((RANKS, LANES), jnp.int32), pltpu.VMEM((RANKS, LANES), F32)],
-        compiler_params=pltpu.CompilerParams(vmem_limit_bytes=16 << 20),
+        scratch_shapes=[
+            pltpu.VMEM((RANKS, LANES), jnp.int32), vmem(RANKS, LANES), vmem(N_LAT, N_LON, LANES),
+            vmem(N_LON, 8, LANES), vmem(N_LON, 8, LANES),
+            dma((N_LAT,)), dma((N_LAT,)), dma((N_LON,)), dma((N_LON,)),
+        ],
+        compiler_params=pltpu.CompilerParams(
+            collective_id=2, has_side_effects=True, vmem_limit_bytes=4 << 20
+        ),
         name="place",
-    )(back, send_list)
-
-
-def exchange(values):
-    return lax.all_to_all(values, ("lon", "lat"), split_axis=0, concat_axis=0, tiled=True)
+    )(picked.reshape(N_LAT, N_LON, LANES), send_list)
 
 
 def local(
@@ -684,12 +801,12 @@
     is_north = lax.axis_index("lat") == N_LAT - 1
     north = jnp.full((8, LANES), jnp.where(is_north, 1.0, 0.0), F32)
     padded = jnp.pad(vert_inverse, ((0, 0), (0, ZP - NZ), (0, ZP - NZ)))
-    outgoing, *coefs, vert = prepare(
+    incoming, *coefs = prepare(
         obs_value.reshape(CAP, LANES), send_list, zonal_weight, merid_weight, north, padded
     )
-    incoming = exchange(outgoing)
-
-    cell = jnp.maximum(recv_cell, 0)
+
+    cell = jnp.swapaxes(jnp.maximum(recv_cell, 0).reshape(N_LON, N_LAT, CAP), 0, 1)
+    cell = cell.reshape(RANKS, CAP)
     line = cell >> 7
     lat_row = line % NLAT
     plane = line // NLAT
@@ -697,19 +814,14 @@
     level = plane - field * NZ
     rows = ((field * NLAT + lat_row) * ZP + level).reshape(-1)
     lanes = jnp.transpose(cell & 127)
-
     sums = jnp.where(
         (jnp.arange(2 * LANES)[:, None] % LANES <= jnp.arange(2 * LANES)[None, :]), 1.0, 0.0
     ).astype(BF16)
 
-    norm = jnp.pad(jnp.transpose(norm_scale, (0, 2, 1, 3)), ((0, 0), (0, 0), (0, ZP - NZ), (0, 0)))
-    gridded, scale = scatter(rows, lanes, incoming, column_depth, norm)
-    whole = solve(gridded, scale, coefs, vert, sums)
-    picked = pick(rows, lanes, whole)
-    returned = exchange(picked)
-    result = place(returned, send_list)
-    increment = jnp.transpose(whole[:, :, :NZ], (0, 2, 1, 3))
-    return increment, result.reshape(-1)
+    gridded, scale = scatter(rows, lanes, incoming, column_depth, norm_scale)
+    whole = solve(gridded, scale, coefs, sums)
+    picked, increment = pick(rows, lanes, whole)
+    return increment, place(picked, send_list).reshape(-1)
 
 
 def solution(mesh):

time: 180 us -> 141 us (0.78)
  starting transfers between devices: 17.7 us -> 0 us
  waiting for transfers between devices: 13 us -> 0 us
  local copies, waits for them, and re-layouts: 14.8 us -> 8.61 us
    all_to_all x2 -> x0, starting transfers between devices: 17.7 us -> none  [exchange(): lax.all_to_all(values, ('lon', 'lat'), split_axis=0, concat_axis=0, tiled...]
    pallas_call x1, Pallas kernels: 32.8 us -> 17.8 us  [scatter(): pl.pallas_call(scatter_kernel, out_shape=(full, full), in_specs=[SMEM_SPE...]
    all_to_all x2 -> x0, waiting for transfers between devices: 13 us -> none  [exchange(): lax.all_to_all(values, ('lon', 'lat'), split_axis=0, concat_axis=0, tiled...]
    pallas_call x1, Pallas kernels: 7.64 us -> 20.3 us  [place(): pl.pallas_call(place_kernel, out_shape=jax.ShapeDtypeStruct((CAP, LANES),...]
    pallas_call x2, Pallas kernels: 29.3 us -> 36.7 us  [the longest x1 22.1 us: prepare(): pl.pallas_call(prepare_kernel, out_shape=(shape(RANKS, LANES), shape(80,...]
    unnamed x40 -> x14, local copies, waits for them, and re-layouts: 14.2 us -> 8.17 us
    pallas_call x1, Pallas kernels: 62.1 us -> 56.3 us  [solve(): pl.pallas_call(solve_kernel, out_shape=jax.ShapeDtypeStruct((NF, NLAT, ZP...]
  transfers between devices with their start and end apart: 2 -> 0, of which waited for: 2 -> 0; matrix products, arithmetic and copies ran while one was open for 4% -> 0% of each run, Pallas kernels for 0% -> 0%
where the time goes in v1:
time: 141 us
  Pallas kernels  131 us (93%)
  local copies, waits for them, and re-layouts  8.61 us (6%)
    pallas_call x1, Pallas kernels, solve(): pl.pallas_call(solve_kernel, out_shape=jax.ShapeDtypeStruct((NF, NLAT, ZP...  56.3 us
    pallas_call x1, Pallas kernels, prepare(): pl.pallas_call(prepare_kernel, out_shape=(shape(RANKS, LANES), shape(80,...  22.1 us
    pallas_call x1, Pallas kernels, place(): pl.pallas_call(place_kernel, out_shape=jax.ShapeDtypeStruct((CAP, LANES),...  20.3 us
    pallas_call x1, Pallas kernels, scatter(): pl.pallas_call(scatter_kernel, out_shape=(full, full), in_specs=[SMEM_SPE...  17.8 us
    pallas_call x1, Pallas kernels, pick(): pl.pallas_call(pick_kernel, out_shape=(jax.ShapeDtypeStruct((RANKS, LANES...  14.6 us
    unnamed x14, local copies, waits for them, and re-layouts  8.17 us

profile of v1, /device:TPU:1, one launch (start us, length us, event | category | flops | bytes accessed | tf_op | source)
XLA Modules:
  0.0 140.7 jit_solution(12282178494873049329)
XLA Ops:
  0.7 0.9 copy.21.send_ref
  1.5 0.9 copy.14
  2.5 0.1 ne.63
  2.6 0.9 copy.20
  3.5 0.1 select_convert_fusion.sums_ref
  3.7 0.1 copy.19
  3.8 0.1 rem.48
  3.9 0.1 div.24
  4.0 0.1 fusion.4.rows_ref
  4.0 0.0 copy-start.1
  4.1 0.8 copy-done.1
  4.8 0.0 copy-start.2
  4.8 0.8 copy-done.2
  5.6 0.0 copy-start.3
  5.6 0.8 copy-done.3
  6.4 22.1 %prepare.1 = (f32[128,128]{1,0:T(8,128)S(1)}, f32[80,128]{1,0:T(8,128)S(1)}, f32[80,128]{1,0:T(8,128)S(1)}, f32[8,128]{1,0:T(8,128)S(1)}, f32[2,40,128]{2,1,0:T(...) custom-call(f32[80,128]{1,0:T(8,128)S(1)} %bitcast.24, ...), custom_call_target="tpu_custom_call" | custom-call | tf_op jit(solution)/shard_map/prepare/pallas_call | solution.py:244
  28.5 0.0 copy-start
  28.5 1.9 %copy-done = f32[2,75,40,128]{3,2,1,0:T(8,128)S(1)} copy-done((f32[2,75,40,128]{3,2,1,0:T(8,128)S(1)}, f32[2,75,40,128]{3,2,1,0:T(8,128)}, u32[]{:S(2)}) %copy-start) | copy-done | bytes 3072024
  30.3 0.0 copy-start.4
  30.3 0.7 copy-done.4
  31.1 17.8 %scatter.1 = (f32[2,40,80,128]{3,2,1,0:T(8,128)S(1)}, f32[2,40,80,128]{3,2,1,0:T(8,128)S(1)}) custom-call(s32[10240]{0:T(1024)S(1)} %fusion.4.rows_ref, s32[80,128]{1,0:T(8,128)S(1)} %bitcast.20, f32[128,128]{1,0:T(8,128)S(1)} %get-tuple-element.17.in_ref, s32[40,128]{1,0:T(8,128)S(1)} %copy-done.4, f32[2,75,40,128]{3,2,1,0:T(8,128)S(1)} %copy-done), custom_call_target="tpu_custom_call" | custom-call | tf_op jit(solution)/shard_map/scatter/pallas_call | solution.py:341
  48.9 56.3 %solve.1 = f32[2,40,80,128]{3,2,1,0:T(8,128)S(1)} custom-call(f32[2,40,80,128]{3,2,1,0:T(8,128)S(1)} %get-tuple-element.18.field_ref, f32[2,40,80,128]{3,2,1,0:T(8,128)S(1)} %get-tuple-element.19.scale_ref, f32[80,128]{1,0:T(8,128)S(1)} %get-tuple-element.20.zs_ref, f32[80,128]{1,0:T(8,128)S(1)} %get-tuple-element.21.zr_ref, ...), custom_call_target="tpu_custom_call" | custom-call | tf_op jit(solution)/shard_map/solve/pallas_call | solution.py:648
  105.2 14.6 %pick.1 = (f32[128,128]{1,0:T(8,128)S(1)}, f32[2,75,40,128]{3,2,1,0:T(8,128)}) custom-call(s32[10240]{0:T(1024)S(1)} %fusion.4.rows_ref, s32[80,128]{1,0:T(8,128)S(1)} %bitcast.21, f32[6400,128]{1,0:T(8,128)S(1)} %bitcast.19), custom_call_target="tpu_custom_call" | custom-call | tf_op jit(solution)/shard_map/pick/pallas_call | solution.py:713
  119.8 20.3 %place.1 = f32[80,128]{1,0:T(8,128)S(1)} custom-call(f32[4,32,128]{2,1,0:T(8,128)S(1)} %bitcast.23, s32[128,80]{1,0:T(8,128)S(1)} %copy.21.send_ref), custom_call_target="tpu_custom_call" | custom-call | tf_op jit(solution)/shard_map/place/pallas_call | solution.py:781
  140.1 0.6 copy.24
  (9 shorter events, 0.1 us)
Async XLA Ops:
  4.0 0.8 copy-start.1
  4.8 0.8 copy-start.2
  5.6 0.8 copy-start.3
  28.5 1.9 %copy-start = (f32[2,75,40,128]{3,2,1,0:T(8,128)S(1)}, f32[2,75,40,128]{3,2,1,0:T(8,128)}, u32[]{:S(2)}) copy-start(f32[2,75,40,128]{3,2,1,0:T(8,128)} %norm_ref.1) | copy-start | bytes 9216004
  30.3 0.7 copy-start.4

commit v2 on v1

v2 whole, which is shorter than its diff:
```python
import jax
import jax.numpy as jnp
from jax import lax
from jax.experimental import pallas as pl
from jax.experimental.pallas import tpu as pltpu
from jax.sharding import PartitionSpec as P

F32 = jnp.float32
BF16 = jnp.bfloat16
MESH = pl.DeviceIdType.MESH
NF, NZ, NLAT, NLON = 2, 75, 40, 128
ZP = 80
RANKS, CAP = 128, 80
N_LON, N_LAT = 32, 4
GROUPS = 15
GROUP = 5
SPLIT = 24
LANES = 128
CHUNK = 8
GRIDS = 8
ROWS = NF * NLAT * ZP
VMEM_SPEC = pl.BlockSpec(memory_space=pltpu.VMEM)
SMEM_SPEC = pl.BlockSpec(memory_space=pltpu.SMEM)
ANY_SPEC = pl.BlockSpec(memory_space=pl.ANY)


def lane_iota(rows):
    return lax.broadcasted_iota(jnp.int32, (rows, LANES), 1)


def split(value):
    high = value.astype(BF16)
    return high, (value - high.astype(F32)).astype(BF16)


def lane_pick(table, index):
    return jnp.take_along_axis(table, index, axis=1, mode="promise_in_bounds")


def push(source, target, send_sem, recv_sem, axis, device):
    return pltpu.make_async_remote_copy(
        src_ref=source, dst_ref=target, send_sem=send_sem, recv_sem=recv_sem,
        device_id={axis: device}, device_id_type=MESH,
    )


def over(axis, count, action):
    mine = lax.axis_index(axis)

    def body(step, _):
        action((mine + step) % count)
        return 0

    lax.fori_loop(1, count, body, 0)


def over_lon(action):
    over("lon", N_LON, action)


def over_lat(action):
    over("lat", N_LAT, action)


def greet():
    barrier = pltpu.get_barrier_semaphore()
    over_lon(
        lambda device: pl.semaphore_signal(
            barrier, inc=1, device_id={"lon": device}, device_id_type=MESH
        )
    )
    over_lat(
        lambda device: pl.semaphore_signal(
            barrier, inc=1, device_id={"lat": device}, device_id_type=MESH
        )
    )


def greeted():
    pl.semaphore_wait(pltpu.get_barrier_semaphore(), N_LON - 1 + N_LAT - 1)


def zonal_coefs(zw_ref, zs_ref, zr_ref, zco_ref, iw_ref, st_ref, rt_ref, zero):
    one = zero + 1.0
    iw_ref[...] = jnp.full((LANES, LANES), 1e-3, F32)
    iw_ref[: NF * NLAT, :] = 1.0 / zw_ref[...]
    iw_ref[...] = jnp.transpose(iw_ref[...])

    def zonal_step(step, carry):
        s_val, s_flux, s_sum, r_val, r_flux, r_sum = carry
        back = LANES - 1 - step
        st_ref[pl.ds(step, 1), :] = s_val[0:1]
        s_sum = s_sum + s_val
        s_val = s_val + s_flux * iw_ref[pl.ds(step, 1), :]
        s_flux = s_flux + s_val
        r_sum = r_sum + r_val
        r_val = r_val + r_flux * iw_ref[pl.ds(back, 1), :]
        rt_ref[pl.ds(back, 1), :] = r_val[0:1]
        r_flux = r_flux + r_val
        return s_val, s_flux, s_sum, r_val, r_flux, r_sum

    _, _, s_sum, r_first, _, r_sum = lax.fori_loop(
        0, LANES, zonal_step, (zero, one, zero, zero, one, zero), unroll=8
    )
    coupling = 1.0 / r_first[0:1]
    zco_ref[...] = jnp.zeros((8, LANES), F32)
    zco_ref[0:1, :] = coupling
    zco_ref[1:2, :] = r_sum[0:1] * coupling
    zco_ref[2:3, :] = s_sum[0:1] * coupling
    zs_ref[...] = jnp.transpose(st_ref[...])[: NF * NLAT, :]
    zr_ref[...] = jnp.transpose(rt_ref[...] * coupling)[: NF * NLAT, :]


def merid_coefs(mw_ref, ms_ref, mr_ref, mss_ref, mrr_ref, mco_ref, miw_ref, north, zero):
    one = zero + 1.0
    miw_ref[...] = 1.0 / mw_ref[...]
    mco_ref[...] = jnp.zeros((NF, 8, LANES), F32)
    for field in range(NF):
        s_val, s_flux, s_sum = zero, one, zero
        for row in range(NLAT):
            ms_ref[field, row : row + 1, :] = s_val[0:1]
            s_sum = s_sum + s_val
            s_val = s_val + s_flux * miw_ref[field, row : row + 1, :]
            s_flux = s_flux + s_val
        r_val = jnp.where(north > 0.5, 1.0, miw_ref[field, NLAT - 1 : NLAT, :] + zero)
        r_flux = jnp.where(north > 0.5, 0.0, one)
        r_sum = zero
        mr_ref[field, NLAT - 1 : NLAT, :] = r_val[0:1]
        for row in range(NLAT - 2, -1, -1):
            r_sum = r_sum + r_val
            r_flux = r_flux + r_val
            r_val = r_val + r_flux * miw_ref[field, row : row + 1, :]
            mr_ref[field, row : row + 1, :] = r_val[0:1]
        inverse = 1.0 / r_val[0:1]
        coupling = jnp.where(north[0:1] > 0.5, 0.0, inverse)
        mr_ref[field] = mr_ref[field] * inverse
        sum_rr, sum_rs = zero, zero
        for row in range(NLAT - 1, -1, -1):
            at = slice(row, row + 1)
            s_row, r_row = ms_ref[field, at, :], mr_ref[field, at, :]
            mrr_ref[field, at, :] = s_row * sum_rr[0:1]
            mss_ref[field, at, :] = s_row * sum_rs[0:1]
            sum_rr = sum_rr + r_row * r_row
            sum_rs = sum_rs + r_row * s_row
        sum_sr, sum_ss = zero, zero
        for row in range(NLAT):
            at = slice(row, row + 1)
            s_row, r_row = ms_ref[field, at, :], mr_ref[field, at, :]
            sum_sr = sum_sr + s_row * r_row
            sum_ss = sum_ss + s_row * s_row
            mrr_ref[field, at, :] = mrr_ref[field, at, :] + r_row * sum_sr[0:1]
            mss_ref[field, at, :] = mss_ref[field, at, :] + r_row * sum_ss[0:1]
        mco_ref[field, 0:1, :] = coupling
        mco_ref[field, 1:2, :] = r_sum[0:1] * inverse
        mco_ref[field, 2:3, :] = s_sum[0:1] * coupling
        mco_ref[field, 3:4, :] = sum_rr[0:1]
        mco_ref[field, 4:5, :] = sum_rs[0:1] * coupling
        mco_ref[field, 5:6, :] = sum_ss[0:1] * coupling * coupling


def zonal_factor(zco_all, alpha, gamma, minv):
    coupling = zco_all[:, 0, :]
    west = jnp.concatenate([coupling[-1:], coupling[:-1]], axis=0)
    spill = zco_all[:, 2, :]
    mass = 1.0 + zco_all[:, 1, :] + jnp.concatenate([spill[-1:], spill[:-1]], axis=0)
    east = coupling
    for bit in range(5):
        stride = 1 << bit
        down = lambda v: jnp.concatenate([v[-stride:], v[:-stride]], axis=0)
        up = lambda v: jnp.concatenate([v[stride:], v[:stride]], axis=0)
        inverse = 1.0 / (mass + west + east)
        left = west * down(inverse)
        right = east * up(inverse)
        for field in range(NF):
            alpha[field, bit] = to_field(left, field)
            gamma[field, bit] = to_field(right, field)
        mass = mass + left * down(mass) + right * up(mass)
        west, east = left * down(west), right * up(east)
    for field in range(NF):
        minv[field] = to_field(1.0 / mass, field)


def to_field(rows, field):
    return rows if field == 0 else pltpu.roll(rows, LANES - field * NLAT, 1)


def gather_lines(table_ref, count, high, low, base):
    def step(row, acc):
        line = jnp.broadcast_to(table_ref[pl.ds(row, 1), :], (ZP, LANES))
        return jnp.where(high == row + base, lane_pick(line, low), acc)

    return lax.fori_loop(0, count, step, jnp.zeros((ZP, LANES), F32), unroll=8)


def two_phase(tile_out, tile_in, rows_out, rows_in, sems):
    me = lax.axis_index("lon")
    my = lax.axis_index("lat")
    s1, r1, s2, r2 = sems
    first = lambda device, slot: push(
        tile_out.at[device], tile_in.at[slot], s1.at[device], r1.at[slot], "lon", device
    )
    second = lambda device, slot: push(
        rows_out.at[device], rows_in.at[slot], s2.at[device], r2.at[slot], "lat", device
    )

    def begin():
        over_lon(lambda device: first(device, me).start())
        tile_in[me] = tile_out[me]

    def middle():
        over_lon(lambda device: first(0, device).wait_recv())
        for lat in range(N_LAT):
            rows_out[lat] = tile_in[:, lat, :]
        over_lat(lambda device: second(device, my).start())
        rows_in[my] = rows_out[my]

    def end():
        over_lat(lambda device: second(0, device).wait_recv())

    def sent():
        over_lon(lambda device: first(device, me).wait_send())
        over_lat(lambda device: second(device, my).wait_send())

    return begin, middle, end, sent


def prepare_kernel(
    obs_ref, send_ref, zw_ref, mw_ref, north_ref, vert_in,
    out_ref, zs_ref, zr_ref, zco_out, ms_ref, mr_ref, mss_ref, mrr_ref, mco_out, vert_ref,
    alpha, gamma, minv, sums_ref,
    iw_ref, st_ref, rt_ref, miw_ref, prod_ref,
    tile_out, tile_in, rows_out, rows_in, zco_ref, zco_all, mco_ref, mco_all,
    o1s, o1r, o2s, o2r, zco_s, zco_r, mco_s, mco_r,
):
    me = lax.axis_index("lon")
    my = lax.axis_index("lat")
    greet()
    index = send_ref[...]
    picked = gather_lines(obs_ref, CAP, index >> 7, index & 127, 0)
    picked = jnp.transpose(
        jnp.concatenate([picked, jnp.zeros((LANES - CAP, LANES), F32)], axis=0)
    )
    for device in range(N_LON):
        tile_out[device, 0:4, :] = picked[4 * device : 4 * device + 4]
        tile_out[device, 4:8, :] = jnp.zeros((4, LANES), F32)

    begin, middle, end, sent = two_phase(tile_out, tile_in, rows_out, rows_in, (o1s, o1r, o2s, o2r))
    zco_copy = lambda device, slot: push(
        zco_ref, zco_all.at[slot], zco_s.at[device], zco_r.at[slot], "lon", device
    )
    mco_copy = lambda device, slot: push(
        mco_ref, mco_all.at[slot], mco_s.at[device], mco_r.at[slot], "lat", device
    )
    greeted()
    begin()
    zero = north_ref[...] * 0.0
    zonal_coefs(zw_ref, zs_ref, zr_ref, zco_ref, iw_ref, st_ref, rt_ref, zero)
    middle()
    over_lon(lambda device: zco_copy(device, me).start())
    zco_all[me] = zco_ref[...]
    for field in range(NF):
        zco_out[field] = to_field(zco_ref[...], field)
    merid_coefs(mw_ref, ms_ref, mr_ref, mss_ref, mrr_ref, mco_ref, miw_ref, north_ref[...], zero)
    over_lat(lambda device: mco_copy(device, my).start())
    mco_all[my] = mco_ref[...]
    prod_ref[...] = jnp.zeros((ZP, LANES), F32)
    for field in range(NF):
        matrix = vert_in[:, field, :]
        prod_ref[:NZ, :NZ] = lax.dot_general(
            matrix, matrix, (((1,), (1,)), ((), ())),
            precision=lax.Precision.HIGHEST, preferred_element_type=F32,
        )
        high, low = split(prod_ref[:, :ZP])
        vert_ref[field] = jnp.concatenate([high, low, high], axis=1)
    source = lax.broadcasted_iota(jnp.int32, (2 * LANES, 2 * LANES), 0) & 127
    target = lax.broadcasted_iota(jnp.int32, (2 * LANES, 2 * LANES), 1)
    sums_ref[...] = jnp.where(source <= target, 1.0, 0.0).astype(BF16)
    end()
    for lat in range(N_LAT):
        out_ref[N_LON * lat : N_LON * lat + N_LON, :] = rows_in[lat]
    over_lon(lambda device: zco_copy(0, device).wait_recv())
    zonal_factor(zco_all, alpha, gamma, minv)
    over_lat(lambda device: mco_copy(0, device).wait_recv())
    mco_out[...] = mco_all[...]
    sent()
    over_lon(lambda device: zco_copy(device, me).wait_send())
    over_lat(lambda device: mco_copy(device, my).wait_send())


def prepare(obs, send_list, zonal_weight, merid_weight, north, vert_inverse):
    shape = lambda *dims: jax.ShapeDtypeStruct(dims, F32)
    vmem = lambda *dims: pltpu.VMEM(dims, F32)
    dma = pltpu.SemaphoreType.DMA
    return pl.pallas_call(
        prepare_kernel,
        out_shape=(
            shape(RANKS, LANES), shape(80, LANES), shape(80, LANES), shape(NF, 8, LANES),
            shape(NF, NLAT, LANES), shape(NF, NLAT, LANES),
            shape(NF, NLAT, LANES), shape(NF, NLAT, LANES), shape(N_LAT, NF, 8, LANES),
            jax.ShapeDtypeStruct((NF, ZP, 3 * ZP), BF16),
            shape(NF, 5, N_LON, LANES), shape(NF, 5, N_LON, LANES), shape(NF, N_LON, LANES),
            jax.ShapeDtypeStruct((2 * LANES, 2 * LANES), BF16),
        ),
        in_specs=[VMEM_SPEC] * 6,
        out_specs=(VMEM_SPEC,) * 14,
        scratch_shapes=[
            vmem(LANES, LANES), vmem(LANES, LANES), vmem(LANES, LANES), vmem(NF, NLAT, LANES),
            vmem(ZP, LANES),
            vmem(N_LON, 8, LANES), vmem(N_LON, 8, LANES),
            vmem(N_LAT, N_LON, LANES), vmem(N_LAT, N_LON, LANES),
            vmem(8, LANES), vmem(N_LON, 8, LANES), vmem(NF, 8, LANES), vmem(N_LAT, NF, 8, LANES),
            dma((N_LON,)), dma((N_LON,)), dma((N_LAT,)), dma((N_LAT,)),
            dma((N_LON,)), dma((N_LON,)), dma((N_LAT,)), dma((N_LAT,)),
        ],
        compiler_params=pltpu.CompilerParams(
            collective_id=0, has_side_effects=True, vmem_limit_bytes=6 << 20
        ),
        name="prepare",
    )(obs, send_list, zonal_weight.reshape(NF * NLAT, LANES), merid_weight, north, vert_inverse)


def scatter_kernel(
    rows_ref, lane_ref, in_ref, depth_ref, norm_ref, field_ref, scale_ref, norm_buf, norm_sem,
    value_ref, even_ref, odd_ref, *grids
):
    def norm_copy(field, row):
        return pltpu.make_async_copy(
            norm_ref.at[field, :, row, :],
            norm_buf.at[field, row, pl.ds(0, NZ), :],
            norm_sem.at[field, row],
        )

    for field in range(NF):

        def begin(row, _, field=field):
            norm_copy(field, row).start()
            return 0

        lax.fori_loop(0, NLAT, begin, 0)

    def clear(step, _):
        at = pl.ds(pl.multiple_of(step * 64, 64), 64)
        for grid in grids:
            grid[at, :] = jnp.zeros((64, LANES), F32)
        return 0

    lax.fori_loop(0, ROWS // 64, clear, 0)
    value_ref[...] = jnp.transpose(in_ref[...])
    iota = lane_iota(CAP)

    def spread(q):
        index = jnp.full((CAP, LANES), q, jnp.int32)
        place = jnp.full((CAP, LANES), (q % N_LAT) * N_LON + q // N_LAT, jnp.int32)
        lane = lane_pick(lane_ref[...], index)
        return jnp.where(iota == lane, lane_pick(value_ref[:CAP, :], place), 0.0)

    def add(q, source):
        for k in range(CAP):
            at = pl.ds(rows_ref[k * RANKS + q], 1)
            grid = grids[k % GRIDS]
            grid[at, :] = grid[at, :] + source[k : k + 1, :]

    even_ref[...] = spread(0)

    def senders(pair, _):
        q = 2 * pair
        odd_ref[...] = spread(q + 1)
        add(q, even_ref)
        even_ref[...] = spread(jnp.minimum(q + 2, RANKS - 1))
        add(q + 1, odd_ref)
        return 0

    lax.fori_loop(0, RANKS // 2, senders, 0)
    level = lax.broadcasted_iota(jnp.int32, (ZP, LANES), 0)
    for field in range(NF):

        def finish(row, _, field=field):
            norm_copy(field, row).wait()
            at = pl.ds(pl.multiple_of((field * NLAT + row) * ZP, ZP), ZP)
            total = [grid[at, :] for grid in grids]
            while len(total) > 1:
                total = [one + two for one, two in zip(total[::2], total[1::2])]
            wet = level < depth_ref[pl.ds(row, 1), :]
            scale = jnp.where(wet, norm_buf[field, row], 0.0)
            scale_ref[field, row] = scale
            field_ref[field, row] = jnp.where(wet, scale * total[0], 0.0)
            return 0

        lax.fori_loop(0, NLAT, finish, 0)


def scatter(rows, lanes, incoming, depth, norm):
    full = jax.ShapeDtypeStruct((NF, NLAT, ZP, LANES), F32)
    return pl.pallas_call(
        scatter_kernel,
        out_shape=(full, full),
        in_specs=[SMEM_SPEC] + [VMEM_SPEC] * 3 + [pl.BlockSpec(memory_space=pltpu.HBM)],
        out_specs=(VMEM_SPEC, VMEM_SPEC),
        scratch_shapes=[
            pltpu.VMEM((NF, NLAT, ZP, LANES), F32), pltpu.SemaphoreType.DMA((NF, NLAT)),
            pltpu.VMEM((LANES, LANES), F32), pltpu.VMEM((CAP, LANES), F32), pltpu.VMEM((CAP, LANES), F32),
        ]
        + [pltpu.VMEM((ROWS, LANES), F32)] * GRIDS,
        compiler_params=pltpu.CompilerParams(vmem_limit_bytes=40 << 20),
        name="scatter",
    )(rows, lanes, incoming, depth, norm)


def solve_kernel(
    field_ref, scale_ref, zs_ref, zr_ref, zco_ref, ms_ref, mr_ref, mss_ref, mrr_ref, mco_all,
    vert_ref, alpha, gamma, minv, sums_ref,
    x_ref,
    zsend, zrecv, zret, zres, msend, mrecv, mret, mres,
    acc_a, acc_b, ubuf, gbuf, mtot, mbuf,
    z1s, z1r, z2s, z2r, m1s, m1r, m2s, m2r,
):
    me = lax.axis_index("lon")
    my = lax.axis_index("lat")
    iota = lane_iota(ZP)
    half = N_LON // NF
    my_field = me // half
    is_solver = me % half < GROUPS
    nothing = jnp.zeros((ZP, LANES), F32)
    greet()


    def zonal_out(turn, field, group, slot):
        return push(
            zsend.at[turn, field, group], zrecv.at[turn, slot],
            z1s.at[turn, field, group], z1r.at[turn, slot], "lon", field * half + group,
        )

    def zonal_back(turn, device, field, group):
        return push(
            zret.at[turn, device], zres.at[turn, field, group],
            z2s.at[turn, device], z2r.at[turn, field, group], "lon", device,
        )

    def others(field, action):
        for group in range(GROUPS):
            pl.when(me != field * half + group)(lambda group=group: action(group))

    def zonal_pass(turn, field, load):
        def chunk_pass(chunk, _):
            lines, left = [], []
            for step in range(CHUNK):
                row = chunk * CHUNK + step
                at = pl.ds(field * NLAT + row, 1)
                s_row, r_row = zs_ref[at, :], zr_ref[at, :]
                value = load(row)
                for coef in (s_row, r_row):
                    high, low = split(coef * value)
                    left.append(jnp.concatenate([high, low], axis=1))
                lines.append((row, s_row, r_row))
            sums = jnp.dot(
                jnp.concatenate(left, axis=0), sums_ref[...], preferred_element_type=F32
            )
            tot_a, tot_b = acc_a[...], acc_b[field]
            for step, (row, s_row, r_row) in enumerate(lines):
                a_part = sums[2 * step * ZP : (2 * step + 1) * ZP]
                b_part = sums[(2 * step + 1) * ZP : (2 * step + 2) * ZP]
                x_ref[field, row] = r_row * a_part[:, :LANES] - s_row * b_part[:, :LANES]
                mine = iota == row
                tot_a = jnp.where(mine, a_part[:, LANES:], tot_a)
                tot_b = jnp.where(mine, b_part[:, LANES:], tot_b)
            acc_a[...] = tot_a
            acc_b[field] = tot_b
            return 0

        acc_a[...] = nothing
        acc_b[field] = nothing
        lax.fori_loop(0, NLAT // CHUNK, chunk_pass, 0)
        acc_a[...] = acc_a[...] * zco_ref[field, 0:1, :]
        for group in range(GROUPS):
            at = slice(GROUP * group, GROUP * group + GROUP)
            zsend[turn, field, group, 0:GROUP, :] = acc_b[field, at, :]
            zsend[turn, field, group, 8 : 8 + GROUP, :] = acc_a[at, :]

    def zonal_send(turn, field):
        others(field, lambda group: zonal_out(turn, field, group, me).start())

        @pl.when(is_solver & (my_field == field))
        def _():
            zrecv[turn, me] = zsend[turn, field, me % half]

    def zonal_reduced(turn):
        mine = me % half
        over_lon(lambda device: zonal_out(turn, 0, 0, device).wait_recv())
        right_side = [
            zrecv[turn, k, 0:8, :] + zrecv[turn, (k - 1) % N_LON, 8:16, :] for k in range(N_LON)
        ]
        for bit in range(5):
            stride = 1 << bit
            right_side = [
                right_side[k]
                + alpha[my_field, bit, k : k + 1, :] * right_side[(k - stride) % N_LON]
                + gamma[my_field, bit, k : k + 1, :] * right_side[(k + stride) % N_LON]
                for k in range(N_LON)
            ]
        values = [right_side[k] * minv[my_field, k : k + 1, :] for k in range(N_LON)]
        for k in range(N_LON):
            zret[turn, k, 0:8, :] = values[k]
            zret[turn, k, 8:16, :] = values[(k + 1) % N_LON]
        over_lon(lambda device: zonal_back(turn, device, my_field, mine).start())
        zres[turn, my_field, mine] = zret[turn, me]

    def zonal_receive(turn, field):
        others(field, lambda group: zonal_back(turn, 0, field, group).wait_recv())
        ubuf[72:80, :] = jnp.zeros((8, LANES), F32)
        gbuf[72:80, :] = jnp.zeros((8, LANES), F32)
        for group in range(GROUPS):
            at = slice(GROUP * group, GROUP * group + GROUP)
            ubuf[at, :] = zres[turn, field, group, 0:GROUP, :]
            gbuf[at, :] = zres[turn, field, group, 8 : 8 + GROUP, :]
        gbuf[...] = gbuf[...] * zco_ref[field, 0:1, :] + acc_b[field]

    def zonal_values(field, chunk):
        u_all, g_all = ubuf[...], gbuf[...]
        found = []
        for step in range(CHUNK):
            row = chunk * CHUNK + step
            at = pl.ds(field * NLAT + row, 1)
            found.append(
                x_ref[field, row]
                + zr_ref[at, :] * jnp.broadcast_to(u_all[:, step : step + 1], (ZP, LANES))
                + zs_ref[at, :] * jnp.broadcast_to(g_all[:, step : step + 1], (ZP, LANES))
            )
        ubuf[...] = pltpu.roll(u_all, LANES - CHUNK, 1)
        gbuf[...] = pltpu.roll(g_all, LANES - CHUNK, 1)
        return found


    def vertical(field, value):
        high, low = split(value)
        return jnp.dot(
            vert_ref[field], jnp.concatenate([high, high, low], axis=0), preferred_element_type=F32
        )

    def vertical_field(field):
        def body(step, _):
            row = step * CHUNK
            value = jnp.concatenate([x_ref[field, row + k] for k in range(CHUNK)], axis=1)
            value = vertical(field, value)
            for k in range(CHUNK):
                x_ref[field, row + k] = value[:, k * LANES : (k + 1) * LANES]
            return 0

        lax.fori_loop(0, NLAT // CHUNK, body, 0)


    def merid_out(field, device, slot):
        return push(
            msend.at[field, device], mrecv.at[field, slot],
            m1s.at[field, device], m1r.at[field, slot], "lat", device,
        )

    def merid_back(field, device, slot):
        return push(
            mret.at[field, device], mres.at[field, slot],
            m2s.at[field, device], m2r.at[field, slot], "lat", device,
        )

    def merid_pass(field):
        def one(chunk, carry):
            tot_a, tot_b = carry
            found = zonal_values(field, chunk)
            for step in range(CHUNK):
                row = chunk * CHUNK + step
                s_row, r_row = ms_ref[field, pl.ds(row, 1), :], mr_ref[field, pl.ds(row, 1), :]
                tot_a = tot_a + s_row * found[step]
                tot_b = tot_b + r_row * found[step]
                x_ref[field, row] = r_row * tot_a - s_row * tot_b
            return tot_a, tot_b

        a_one, b_one = lax.fori_loop(0, NLAT // CHUNK, one, (nothing, nothing))
        ubuf[...] = b_one

        def two(row, carry):
            tot_a, tot_b = carry
            s_row, r_row = ms_ref[field, pl.ds(row, 1), :], mr_ref[field, pl.ds(row, 1), :]
            value = x_ref[field, row] + s_row * ubuf[...]
            tot_a = tot_a + s_row * value
            tot_b = tot_b + r_row * value
            x_ref[field, row] = r_row * tot_a - s_row * tot_b
            return tot_a, tot_b

        a_two, b_two = lax.fori_loop(0, NLAT, two, (nothing, nothing), unroll=4)
        mtot[field] = b_two
        coupling = mco_all[my, field, 0:1, :]
        for part, value in enumerate((b_one, a_one * coupling, b_two, a_two * coupling)):
            for solver in range(N_LAT):
                count = min(SPLIT, ZP - SPLIT * solver)
                msend[field, solver, part, 0:count, :] = value[SPLIT * solver : SPLIT * solver + count]
                if count < SPLIT:
                    msend[field, solver, part, count:SPLIT, :] = jnp.zeros(
                        (SPLIT - count, LANES), F32
                    )
        over_lat(lambda device: merid_out(field, device, my).start())
        mrecv[field, my] = msend[field, my]

    def merid_reduced(field):
        over_lat(lambda device: merid_out(field, 0, device).wait_recv())
        coef = lambda k, row: mco_all[k, field, row : row + 1, :]
        part = lambda k, index: mrecv[field, k, index]

        def solve_four(right_side):
            mass = 1.0 + coef(0, 1)
            reduced = right_side[0]
            kept, inverses, values = [], [], [None] * N_LAT
            for k in range(N_LAT):
                inverse = 1.0 / (mass + coef(k, 0))
                kept.append(reduced)
                inverses.append(inverse)
                if k + 1 < N_LAT:
                    factor = coef(k, 0) * inverse
                    mass = 1.0 + coef(k + 1, 1) + coef(k, 2) + factor * mass
                    reduced = right_side[k + 1] + factor * reduced
            values[-1] = kept[-1] * inverses[-1]
            for k in range(N_LAT - 2, -1, -1):
                values[k] = (kept[k] + coef(k, 0) * values[k + 1]) * inverses[k]
            return values

        none = jnp.zeros((SPLIT, LANES), F32)
        u = solve_four([part(k, 0) + (part(k - 1, 1) if k else none) for k in range(N_LAT)]) + [none]
        second = []
        for k in range(N_LAT):
            value = part(k, 2) + coef(k, 3) * u[k] + coef(k, 4) * u[k + 1]
            if k:
                value = value + part(k - 1, 3) + coef(k - 1, 4) * u[k - 1] + coef(k - 1, 5) * u[k]
            second.append(value)
        v = solve_four(second) + [none]
        for k in range(N_LAT):
            for index, value in enumerate((u[k], u[k + 1], v[k], v[k + 1])):
                mret[field, k, index] = value
        over_lat(lambda device: merid_back(field, device, my).start())
        mres[field, my] = mret[field, my]

    def merid_receive(field):
        over_lat(lambda device: merid_back(field, 0, device).wait_recv())
        for index in range(4):
            for solver in range(N_LAT):
                count = min(SPLIT, ZP - SPLIT * solver)
                mbuf[index, SPLIT * solver : SPLIT * solver + count, :] = mres[
                    field, solver, index, 0:count, :
                ]
        coupling = mco_all[my, field, 0:1, :]
        mbuf[1] = mbuf[1] * coupling
        mbuf[3] = mbuf[3] * coupling + mtot[field]

    def merid_value(field, row):
        at = pl.ds(row, 1)
        return (
            x_ref[field, row]
            + mrr_ref[field, at, :] * mbuf[0]
            + mss_ref[field, at, :] * mbuf[1]
            + mr_ref[field, at, :] * mbuf[2]
            + ms_ref[field, at, :] * mbuf[3]
        )

    zonal_pass(0, 0, lambda row: field_ref[0, row])
    greeted()
    zonal_send(0, 0)
    zonal_pass(0, 1, lambda row: field_ref[1, row])
    zonal_send(0, 1)
    vertical_field(0)
    pl.when(is_solver & (my_field == 0))(lambda: zonal_reduced(0))
    vertical_field(1)
    pl.when(is_solver & (my_field == 1))(lambda: zonal_reduced(0))

    for field in range(NF):
        zonal_receive(0, field)
        both = vertical(field, jnp.concatenate([ubuf[...], gbuf[...]], axis=1))
        ubuf[...] = both[:, :LANES]
        gbuf[...] = both[:, LANES:]
        merid_pass(field)
    for field in range(NF):
        merid_reduced(field)

    for field in range(NF):
        merid_receive(field)
        zonal_pass(1, field, lambda row, field=field: merid_value(field, row))
        zonal_send(1, field)
    pl.when(is_solver)(lambda: zonal_reduced(1))
    for field in range(NF):
        zonal_receive(1, field)

        def last_pass(chunk, _, field=field):
            found = zonal_values(field, chunk)
            for step in range(CHUNK):
                row = chunk * CHUNK + step
                x_ref[field, row] = found[step] * scale_ref[field, row]
            return 0

        lax.fori_loop(0, NLAT // CHUNK, last_pass, 0)

    for field in range(NF):
        over_lat(lambda device, field=field: merid_out(field, device, my).wait_send())
        over_lat(lambda device, field=field: merid_back(field, device, my).wait_send())
        for turn in range(2):
            others(
                field,
                lambda group, turn=turn, field=field: zonal_out(turn, field, group, me).wait_send(),
            )

    @pl.when(is_solver)
    def _():
        for turn in range(2):
            over_lon(lambda device, turn=turn: zonal_back(turn, device, 0, 0).wait_send())


def solve(field, scale, coefs):
    dma = pltpu.SemaphoreType.DMA
    vmem = lambda *dims: pltpu.VMEM(dims, F32)
    return pl.pallas_call(
        solve_kernel,
        out_shape=jax.ShapeDtypeStruct((NF, NLAT, ZP, LANES), F32),
        in_specs=[VMEM_SPEC] * 15,
        out_specs=VMEM_SPEC,
        scratch_shapes=[
            vmem(2, NF, GROUPS, 16, LANES), vmem(2, N_LON, 16, LANES),
            vmem(2, N_LON, 16, LANES), vmem(2, NF, GROUPS, 16, LANES),
            vmem(NF, N_LAT, 4, SPLIT, LANES), vmem(NF, N_LAT, 4, SPLIT, LANES),
            vmem(NF, N_LAT, 4, SPLIT, LANES), vmem(NF, N_LAT, 4, SPLIT, LANES),
            vmem(ZP, LANES), vmem(NF, ZP, LANES), vmem(ZP, LANES), vmem(ZP, LANES),
            vmem(NF, ZP, LANES), vmem(4, ZP, LANES),
            dma((2, NF, GROUPS)), dma((2, N_LON)), dma((2, N_LON)), dma((2, NF, GROUPS)),
            dma((NF, N_LAT)), dma((NF, N_LAT)), dma((NF, N_LAT)), dma((NF, N_LAT)),
        ],
        compiler_params=pltpu.CompilerParams(
            collective_id=1, has_side_effects=True, vmem_limit_bytes=20 << 20
        ),
        name="solve",
    )(field, scale, *coefs)


def pick_kernel(rows_ref, lane_ref, x_ref, out_ref, inc_ref, inc_sem, *copies):
    iota = lane_iota(8)

    def inc_copy(field, row):
        return pltpu.make_async_copy(
            x_ref.at[pl.ds(pl.multiple_of((field * NLAT + row) * ZP, ZP), NZ), :],
            inc_ref.at[field, :, row, :],
            inc_sem.at[field, row],
        )

    def over_rows(action):
        for field in range(NF):

            def body(row, _, field=field):
                action(inc_copy(field, row))
                return 0

            lax.fori_loop(0, NLAT, body, 0)

    over_rows(lambda copy: copy.start())
    group = len(copies)

    def senders(step, acc):
        acc = list(acc)
        for part in range(group):
            q = step * group + part
            for k in range(CAP):
                copies[part][k : k + 1, :] = x_ref[pl.ds(rows_ref[k * RANKS + q], 1), :]
        for part in range(group):
            q = step * group + part
            for tile in range(CAP // 8):
                at = slice(8 * tile, 8 * tile + 8)
                found = lane_pick(copies[part][at, :], lane_ref[at, :])
                acc[tile] = jnp.where(iota == q, found, acc[tile])
        return tuple(acc)

    acc = lax.fori_loop(0, RANKS // group, senders, (jnp.zeros((8, LANES), F32),) * (CAP // 8))
    whole = jnp.concatenate(list(acc) + [jnp.zeros((LANES - CAP, LANES), F32)], axis=0)
    whole = jnp.transpose(whole)
    for device in range(N_LON):
        out_ref[device, 0:4, :] = whole[4 * device : 4 * device + 4]
        out_ref[device, 4:8, :] = jnp.zeros((4, LANES), F32)
    over_rows(lambda copy: copy.wait())


def pick(rows, lanes, increment):
    return pl.pallas_call(
        pick_kernel,
        out_shape=(
            jax.ShapeDtypeStruct((N_LON, 8, LANES), F32),
            jax.ShapeDtypeStruct((NF, NZ, NLAT, LANES), F32),
        ),
        in_specs=[SMEM_SPEC, VMEM_SPEC, VMEM_SPEC],
        out_specs=(VMEM_SPEC, ANY_SPEC),
        scratch_shapes=[pltpu.SemaphoreType.DMA((NF, NLAT))] + [pltpu.VMEM((CAP, LANES), F32)] * 8,
        compiler_params=pltpu.CompilerParams(vmem_limit_bytes=8 << 20),
        name="pick",
    )(rows, lanes, increment.reshape(ROWS, LANES))


def place_kernel(
    tile_out, send_ref, out_ref, idx_ref, val_ref, tile_in, rows_out, rows_in, b1s, b1r, b2s, b2r
):
    greet()
    none = jnp.full((LANES - CAP, LANES), -1, jnp.int32)
    idx_ref[...] = jnp.transpose(jnp.concatenate([send_ref[...], none], axis=0))
    begin, middle, end, sent = two_phase(tile_out, tile_in, rows_out, rows_in, (b1s, b1r, b2s, b2r))
    row_iota = lax.broadcasted_iota(jnp.int32, (CAP, 2 * LANES), 0)
    col_iota = lax.broadcasted_iota(jnp.int32, (LANES, 2 * LANES), 0)
    lane = lax.broadcasted_iota(jnp.int32, (LANES, 2 * LANES), 1)
    slot = (lane & 127).astype(F32)
    second_half = lane >> 7

    def pair(step, acc):
        left, right = pl.ds(2 * step, 1), pl.ds(2 * step + 1, 1)
        index = jnp.concatenate([idx_ref[left, :], idx_ref[right, :]], axis=1)
        rows = jnp.where(row_iota == (index >> 7), 1.0, 0.0).astype(BF16)
        here = col_iota == (index & 127)
        number = 2 * step + second_half
        number = ((number % N_LAT) * N_LON + number // N_LAT + 1).astype(F32)
        columns = jnp.concatenate(
            [jnp.where(here, number, 0.0).astype(BF16), jnp.where(here, slot, 0.0).astype(BF16)],
            axis=0,
        )
        return acc + lax.dot_general(
            rows, columns, (((1,), (1,)), ((), ())), preferred_element_type=F32
        )

    def pairs(start, stop, acc):
        return lax.fori_loop(start, stop, pair, acc, unroll=4)

    acc = jnp.zeros((CAP, 2 * LANES), F32)
    greeted()
    begin()
    acc = pairs(0, RANKS // 4, acc)
    middle()
    acc = pairs(RANKS // 4, RANKS // 2, acc)
    high = acc[:, :LANES].astype(jnp.int32)
    low = acc[:, LANES:].astype(jnp.int32)
    end()
    for lat in range(N_LAT):
        val_ref[N_LON * lat : N_LON * lat + N_LON, :] = rows_in[lat]
    out_ref[...] = gather_lines(val_ref, RANKS, high, low, 1)
    sent()


def place(tiles, send_list):
    vmem = lambda *dims: pltpu.VMEM(dims, F32)
    dma = pltpu.SemaphoreType.DMA
    return pl.pallas_call(
        place_kernel,
        out_shape=jax.ShapeDtypeStruct((CAP, LANES), F32),
        in_specs=[VMEM_SPEC] * 2,
        out_specs=VMEM_SPEC,
        scratch_shapes=[
            pltpu.VMEM((RANKS, LANES), jnp.int32), vmem(RANKS, LANES),
            vmem(N_LON, 8, LANES), vmem(N_LAT, N_LON, LANES), vmem(N_LAT, N_LON, LANES),
            dma((N_LON,)), dma((N_LON,)), dma((N_LAT,)), dma((N_LAT,)),
        ],
        compiler_params=pltpu.CompilerParams(
            collective_id=2, has_side_effects=True, vmem_limit_bytes=6 << 20
        ),
        name="place",
    )(tiles, send_list)


def local(
    obs_value, send_list, recv_cell, column_depth, zonal_weight, merid_weight, vert_inverse, norm_scale
):
    is_north = lax.axis_index("lat") == N_LAT - 1
    north = jnp.full((8, LANES), jnp.where(is_north, 1.0, 0.0), F32)
    sends = jnp.transpose(send_list)
    incoming, *coefs = prepare(
        obs_value.reshape(CAP, LANES), sends, zonal_weight, merid_weight, north,
        jnp.transpose(vert_inverse, (1, 0, 2)),
    )
    cell = jnp.maximum(jnp.transpose(recv_cell), 0)
    line = cell >> 7
    plane = line // NLAT
    lat_row = line - plane * NLAT
    field = (plane >= NZ).astype(jnp.int32)
    level = plane - field * NZ
    rows = ((field * NLAT + lat_row) * ZP + level).reshape(-1)

    gridded, scale = scatter(rows, cell & 127, incoming, column_depth, norm_scale)
    whole = solve(gridded, scale, coefs)
    tiles, increment = pick(rows, cell & 127, whole)
    return increment, place(tiles, sends).reshape(-1)


def solution(mesh):
    in_specs = (
        P(("lon", "lat")),
        P(("lon", "lat"), None),
        P(("lon", "lat"), None),
        P("lat", "lon"),
        P(None, "lat", "lon"),
        P(None, "lat", "lon"),
        P(),
        P(None, None, "lat", "lon"),
    )
    out_specs = (P(None, None, "lat", "lon"), P(("lon", "lat")))
    return jax.shard_map(local, mesh=mesh, in_specs=in_specs, out_specs=out_specs, check_vma=False)
```

time: 141 us -> 132 us (0.936)
  Pallas kernels: 131 us -> 122 us
    pallas_call x1, Pallas kernels: 56.3 us -> 49.2 us  [solve(): pl.pallas_call(solve_kernel, out_shape=jax.ShapeDtypeStruct((NF, NLAT, ZP...]
    pallas_call x1, Pallas kernels: 20.3 us -> 17.7 us  [place(): pl.pallas_call(place_kernel, out_shape=jax.ShapeDtypeStruct((CAP, LANES),...]
    pallas_call x1, Pallas kernels: 17.8 us -> 20.3 us  [scatter(): pl.pallas_call(scatter_kernel, out_shape=(full, full), in_specs=[SMEM_SPE...]
    pallas_call x1, Pallas kernels: 22.1 us -> 20.5 us  [prepare(): pl.pallas_call(prepare_kernel, out_shape=(shape(RANKS, LANES), shape(80,...]
    unnamed x14 -> x17, local copies, waits for them, and re-layouts: 8.17 us -> 7.21 us
where the time goes in v2:
time: 132 us
  Pallas kernels  122 us (92%)
  local copies, waits for them, and re-layouts  7.21 us (5%)
  other arithmetic  1.61 us (1%)
    pallas_call x1, Pallas kernels, solve(): pl.pallas_call(solve_kernel, out_shape=jax.ShapeDtypeStruct((NF, NLAT, ZP...  49.2 us
    pallas_call x1, Pallas kernels, prepare(): pl.pallas_call(prepare_kernel, out_shape=(shape(RANKS, LANES), shape(80,...  20.5 us
    pallas_call x1, Pallas kernels, scatter(): pl.pallas_call(scatter_kernel, out_shape=(full, full), in_specs=[SMEM_SPE...  20.3 us
    pallas_call x1, Pallas kernels, place(): pl.pallas_call(place_kernel, out_shape=jax.ShapeDtypeStruct((CAP, LANES),...  17.7 us
    pallas_call x1, Pallas kernels, pick(): pl.pallas_call(pick_kernel, out_shape=(jax.ShapeDtypeStruct((N_LON, 8, LA...  14.5 us
    unnamed x17, local copies, waits for them, and re-layouts  7.21 us

profile of v2, /device:TPU:1, one launch (start us, length us, event | category | flops | bytes accessed | tf_op | source)
XLA Modules:
  0.0 131.8 jit_solution(5217973507955320012)
XLA Ops:
  0.6 0.8 and_bitcast_fusion.lane_ref
  1.4 0.8 fusion.5.rows_ref
  2.3 0.0 copy-start.1
  2.3 0.8 copy-done.1
  3.0 0.0 copy-start.3
  3.0 0.9 copy-done.3
  3.9 0.0 copy-start.4
  3.9 0.8 copy-done.4
  4.7 0.0 copy-start.5
  4.7 0.8 copy-done.5
  5.5 0.0 copy-start.6
  5.5 0.8 copy-done.6
  6.3 20.5 %prepare.1 = (f32[128,128]{1,0:T(8,128)S(1)}, f32[80,128]{1,0:T(8,128)S(1)}, f32[80,128]{1,0:T(8,128)S(1)}, f32[2,8,128]{2,1,0:T(8,128)S(1)}, f32[2,40,128]{2,1,...) custom-call(f32[80,128]{1,0:T(8,128)S(1)} %bitcast.42, ...), custom_call_target="tpu_custom_call" | custom-call | tf_op jit(solution)/shard_map/prepare/pallas_call | solution.py:294
  26.8 0.0 copy-start
  26.8 1.9 %copy-done = f32[2,75,40,128]{3,2,1,0:T(8,128)S(1)} copy-done((f32[2,75,40,128]{3,2,1,0:T(8,128)S(1)}, f32[2,75,40,128]{3,2,1,0:T(8,128)}, u32[]{:S(2)}) %copy-start) | copy-done | bytes 3072024
  28.6 0.0 copy-start.7
  28.6 0.7 copy-done.7
  29.4 20.3 %scatter.1 = (f32[2,40,80,128]{3,2,1,0:T(8,128)S(1)}, f32[2,40,80,128]{3,2,1,0:T(8,128)S(1)}) custom-call(s32[10240]{0:T(1024)S(1)} %fusion.5.rows_ref, s32[80,128]{1,0:T(8,128)S(1)} %and_bitcast_fusion.lane_ref, f32[128,128]{1,0:T(8,128)S(1)} %get-tuple-element.20.in_ref, s32[40,128]{1,0:T(8,128)S(1)} %copy-done.7, f32[2,75,40,128]{3,2,1,0:T(8,128)S(1)} %copy-done), custom_call_target="tpu_custom_call" | custom-call | tf_op jit(solution)/shard_map/scatter/pallas_call | solution.py:394
  49.7 49.2 %solve.1 = f32[2,40,80,128]{3,2,1,0:T(8,128)S(1)} custom-call(f32[2,40,80,128]{3,2,1,0:T(8,128)S(1)} %get-tuple-element.21.field_ref, f32[2,40,80,128]{3,2,1,0:T(8,128)S(1)} %get-tuple-element.22.scale_ref, f32[80,128]{1,0:T(8,128)S(1)} %get-tuple-element.23.zs_ref, f32[80,128]{1,0:T(8,128)S(1)} %get-tuple-element.24.zr_ref, ...), custom_call_target="tpu_custom_call" | custom-call | tf_op jit(solution)/shard_map/solve/pallas_call | solution.py:714
  98.9 0.0 copy-start.2
  98.9 14.5 %pick.1 = (f32[32,8,128]{2,1,0:T(8,128)S(1)}, f32[2,75,40,128]{3,2,1,0:T(8,128)}) custom-call(s32[10240]{0:T(1024)S(1)} %fusion.5.rows_ref, s32[80,128]{1,0:T(8,128)S(1)} %and_bitcast_fusion.lane_ref, f32[6400,128]{1,0:T(8,128)S(1)} %bitcast.37), custom_call_target="tpu_custom_call" | custom-call | tf_op jit(solution)/shard_map/pick/pallas_call | solution.py:782
  113.5 0.0 copy-done.2
  113.5 17.7 %place.1 = f32[80,128]{1,0:T(8,128)S(1)} custom-call(f32[32,8,128]{2,1,0:T(8,128)S(1)} %get-tuple-element.37.tile_out, s32[80,128]{1,0:T(8,128)S(1)} %bitcast.40), custom_call_target="tpu_custom_call" | custom-call | tf_op jit(solution)/shard_map/place/pallas_call | solution.py:845
  131.2 0.6 copy.11
  (1 shorter events, 0.0 us)
Async XLA Ops:
  2.3 0.8 copy-start.1
  3.0 0.9 copy-start.3
  3.9 0.8 copy-start.4
  4.7 0.8 copy-start.5
  5.5 0.8 copy-start.6
  26.8 1.9 %copy-start = (f32[2,75,40,128]{3,2,1,0:T(8,128)S(1)}, f32[2,75,40,128]{3,2,1,0:T(8,128)}, u32[]{:S(2)}) copy-start(f32[2,75,40,128]{3,2,1,0:T(8,128)} %norm_ref.1) | copy-start | bytes 9216004
  28.6 0.7 copy-start.7
  98.9 14.6 %copy-start.2 = (s32[128,80]{0,1:T(8,128)S(1)}, s32[128,80]{0,1:T(8,128)}, u32[]{:S(2)}) copy-start(s32[128,80]{0,1:T(8,128)} %param.9) | copy-start | bytes 122884

commit v3 on v2

--- a/solution.py
+++ b/solution.py
@@ -14,14 +14,20 @@
 N_LON, N_LAT = 32, 4
 GROUPS = 15
 GROUP = 5
-SPLIT = 24
 LANES = 128
 CHUNK = 8
+HALF = 64
 GRIDS = 8
 ROWS = NF * NLAT * ZP
+ZW_AT, MW_AT, VERT_AT = 80, 160, 240
+DEPTH_AT = 160
 VMEM_SPEC = pl.BlockSpec(memory_space=pltpu.VMEM)
 SMEM_SPEC = pl.BlockSpec(memory_space=pltpu.SMEM)
 ANY_SPEC = pl.BlockSpec(memory_space=pl.ANY)
+
+
+def cost(micros):
+    return pl.CostEstimate(flops=0, bytes_accessed=int(micros * 3.6e6), transcendentals=0)
 
 
 def lane_iota(rows):
@@ -80,10 +86,10 @@
     pl.semaphore_wait(pltpu.get_barrier_semaphore(), N_LON - 1 + N_LAT - 1)
 
 
-def zonal_coefs(zw_ref, zs_ref, zr_ref, zco_ref, iw_ref, st_ref, rt_ref, zero):
+def zonal_coefs(floats_ref, zs_ref, zr_ref, zco_ref, iw_ref, st_ref, rt_ref, zero):
     one = zero + 1.0
     iw_ref[...] = jnp.full((LANES, LANES), 1e-3, F32)
-    iw_ref[: NF * NLAT, :] = 1.0 / zw_ref[...]
+    iw_ref[: NF * NLAT, :] = 1.0 / floats_ref[ZW_AT : ZW_AT + NF * NLAT, :]
     iw_ref[...] = jnp.transpose(iw_ref[...])
 
     def zonal_step(step, carry):
@@ -111,9 +117,11 @@
     zr_ref[...] = jnp.transpose(rt_ref[...] * coupling)[: NF * NLAT, :]
 
 
-def merid_coefs(mw_ref, ms_ref, mr_ref, mss_ref, mrr_ref, mco_ref, miw_ref, north, zero):
+def merid_coefs(floats_ref, ms_ref, mr_ref, mss_ref, mrr_ref, mco_ref, miw_ref, north, zero):
     one = zero + 1.0
-    miw_ref[...] = 1.0 / mw_ref[...]
+    for field in range(NF):
+        at = MW_AT + field * NLAT
+        miw_ref[field] = 1.0 / floats_ref[at : at + NLAT, :]
     mco_ref[...] = jnp.zeros((NF, 8, LANES), F32)
     for field in range(NF):
         s_val, s_flux, s_sum = zero, one, zero
@@ -225,9 +233,21 @@
 
 
 def prepare_kernel(
-    obs_ref, send_ref, zw_ref, mw_ref, north_ref, vert_in,
+    ints_ref, floats_ref, north_ref,
     out_ref, zs_ref, zr_ref, zco_out, ms_ref, mr_ref, mss_ref, mrr_ref, mco_out, vert_ref,
-    alpha, gamma, minv, sums_ref,
+    alpha, gamma, minv, sums_ref, *rest
+):
+    grids, rest = rest[:GRIDS], rest[GRIDS:]
+    prepare_body(
+        ints_ref, floats_ref, north_ref, out_ref, zs_ref, zr_ref, zco_out, ms_ref, mr_ref, mss_ref,
+        mrr_ref, mco_out, vert_ref, alpha, gamma, minv, sums_ref, grids, *rest,
+    )
+
+
+def prepare_body(
+    ints_ref, floats_ref, north_ref,
+    out_ref, zs_ref, zr_ref, zco_out, ms_ref, mr_ref, mss_ref, mrr_ref, mco_out, vert_ref,
+    alpha, gamma, minv, sums_ref, grids,
     iw_ref, st_ref, rt_ref, miw_ref, prod_ref,
     tile_out, tile_in, rows_out, rows_in, zco_ref, zco_all, mco_ref, mco_all,
     o1s, o1r, o2s, o2r, zco_s, zco_r, mco_s, mco_r,
@@ -235,8 +255,8 @@
     me = lax.axis_index("lon")
     my = lax.axis_index("lat")
     greet()
-    index = send_ref[...]
-    picked = gather_lines(obs_ref, CAP, index >> 7, index & 127, 0)
+    index = ints_ref[0:CAP, :]
+    picked = gather_lines(floats_ref, CAP, index >> 7, index & 127, 0)
     picked = jnp.transpose(
         jnp.concatenate([picked, jnp.zeros((LANES - CAP, LANES), F32)], axis=0)
     )
@@ -254,18 +274,18 @@
     greeted()
     begin()
     zero = north_ref[...] * 0.0
-    zonal_coefs(zw_ref, zs_ref, zr_ref, zco_ref, iw_ref, st_ref, rt_ref, zero)
+    zonal_coefs(floats_ref, zs_ref, zr_ref, zco_ref, iw_ref, st_ref, rt_ref, zero)
     middle()
     over_lon(lambda device: zco_copy(device, me).start())
     zco_all[me] = zco_ref[...]
     for field in range(NF):
         zco_out[field] = to_field(zco_ref[...], field)
-    merid_coefs(mw_ref, ms_ref, mr_ref, mss_ref, mrr_ref, mco_ref, miw_ref, north_ref[...], zero)
+    merid_coefs(floats_ref, ms_ref, mr_ref, mss_ref, mrr_ref, mco_ref, miw_ref, north_ref[...], zero)
     over_lat(lambda device: mco_copy(device, my).start())
     mco_all[my] = mco_ref[...]
     prod_ref[...] = jnp.zeros((ZP, LANES), F32)
     for field in range(NF):
-        matrix = vert_in[:, field, :]
+        matrix = floats_ref[pl.ds(VERT_AT + field, NZ, stride=NF), :]
         prod_ref[:NZ, :NZ] = lax.dot_general(
             matrix, matrix, (((1,), (1,)), ((), ())),
             precision=lax.Precision.HIGHEST, preferred_element_type=F32,
@@ -275,6 +295,13 @@
     source = lax.broadcasted_iota(jnp.int32, (2 * LANES, 2 * LANES), 0) & 127
     target = lax.broadcasted_iota(jnp.int32, (2 * LANES, 2 * LANES), 1)
     sums_ref[...] = jnp.where(source <= target, 1.0, 0.0).astype(BF16)
+    def clear(step, _):
+        at = pl.ds(pl.multiple_of(step * 64, 64), 64)
+        for grid in grids:
+            grid[at, :] = jnp.zeros((64, LANES), F32)
+        return 0
+
+    lax.fori_loop(0, ROWS // 64, clear, 0)
     end()
     for lat in range(N_LAT):
         out_ref[N_LON * lat : N_LON * lat + N_LON, :] = rows_in[lat]
@@ -287,7 +314,7 @@
     over_lat(lambda device: mco_copy(device, my).wait_send())
 
 
-def prepare(obs, send_list, zonal_weight, merid_weight, north, vert_inverse):
+def prepare(ints, floats, north):
     shape = lambda *dims: jax.ShapeDtypeStruct(dims, F32)
     vmem = lambda *dims: pltpu.VMEM(dims, F32)
     dma = pltpu.SemaphoreType.DMA
@@ -300,9 +327,10 @@
             jax.ShapeDtypeStruct((NF, ZP, 3 * ZP), BF16),
             shape(NF, 5, N_LON, LANES), shape(NF, 5, N_LON, LANES), shape(NF, N_LON, LANES),
             jax.ShapeDtypeStruct((2 * LANES, 2 * LANES), BF16),
-        ),
-        in_specs=[VMEM_SPEC] * 6,
-        out_specs=(VMEM_SPEC,) * 14,
+        )
+        + (shape(ROWS, LANES),) * GRIDS,
+        in_specs=[VMEM_SPEC] * 3,
+        out_specs=(VMEM_SPEC,) * (14 + GRIDS),
         scratch_shapes=[
             vmem(LANES, LANES), vmem(LANES, LANES), vmem(LANES, LANES), vmem(NF, NLAT, LANES),
             vmem(ZP, LANES),
@@ -315,14 +343,15 @@
         compiler_params=pltpu.CompilerParams(
             collective_id=0, has_side_effects=True, vmem_limit_bytes=6 << 20
         ),
+        cost_estimate=cost(15),
         name="prepare",
-    )(obs, send_list, zonal_weight.reshape(NF * NLAT, LANES), merid_weight, north, vert_inverse)
-
-
-def scatter_kernel(
-    rows_ref, lane_ref, in_ref, depth_ref, norm_ref, field_ref, scale_ref, norm_buf, norm_sem,
-    value_ref, even_ref, odd_ref, *grids
-):
+    )(ints, floats, north)
+
+
+def scatter_kernel(rows_ref, ints_ref, in_ref, norm_ref, *refs):
+    grids = refs[GRIDS : 2 * GRIDS]
+    norm_buf, norm_sem, value_ref, even_ref, odd_ref = refs[2 * GRIDS :]
+
     def norm_copy(field, row):
         return pltpu.make_async_copy(
             norm_ref.at[field, :, row, :],
@@ -330,33 +359,28 @@
             norm_sem.at[field, row],
         )
 
-    for field in range(NF):
-
-        def begin(row, _, field=field):
-            norm_copy(field, row).start()
-            return 0
-
-        lax.fori_loop(0, NLAT, begin, 0)
-
-    def clear(step, _):
-        at = pl.ds(pl.multiple_of(step * 64, 64), 64)
-        for grid in grids:
-            grid[at, :] = jnp.zeros((64, LANES), F32)
-        return 0
-
-    lax.fori_loop(0, ROWS // 64, clear, 0)
+    def over_rows(action):
+        for field in range(NF):
+
+            def body(row, _, field=field):
+                action(norm_copy(field, row))
+                return 0
+
+            lax.fori_loop(0, NLAT, body, 0)
+
+    over_rows(lambda copy: copy.start())
     value_ref[...] = jnp.transpose(in_ref[...])
     iota = lane_iota(CAP)
 
     def spread(q):
         index = jnp.full((CAP, LANES), q, jnp.int32)
         place = jnp.full((CAP, LANES), (q % N_LAT) * N_LON + q // N_LAT, jnp.int32)
-        lane = lane_pick(lane_ref[...], index)
+        lane = lane_pick(ints_ref[CAP : 2 * CAP, :], index)
         return jnp.where(iota == lane, lane_pick(value_ref[:CAP, :], place), 0.0)
 
     def add(q, source):
         for k in range(CAP):
-            at = pl.ds(rows_ref[k * RANKS + q], 1)
+            at = pl.ds(rows_ref[k, q], 1)
             grid = grids[k % GRIDS]
             grid[at, :] = grid[at, :] + source[k : k + 1, :]
 
@@ -371,48 +395,38 @@
         return 0
 
     lax.fori_loop(0, RANKS // 2, senders, 0)
-    level = lax.broadcasted_iota(jnp.int32, (ZP, LANES), 0)
-    for field in range(NF):
-
-        def finish(row, _, field=field):
-            norm_copy(field, row).wait()
-            at = pl.ds(pl.multiple_of((field * NLAT + row) * ZP, ZP), ZP)
-            total = [grid[at, :] for grid in grids]
-            while len(total) > 1:
-                total = [one + two for one, two in zip(total[::2], total[1::2])]
-            wet = level < depth_ref[pl.ds(row, 1), :]
-            scale = jnp.where(wet, norm_buf[field, row], 0.0)
-            scale_ref[field, row] = scale
-            field_ref[field, row] = jnp.where(wet, scale * total[0], 0.0)
-            return 0
-
-        lax.fori_loop(0, NLAT, finish, 0)
-
-
-def scatter(rows, lanes, incoming, depth, norm):
-    full = jax.ShapeDtypeStruct((NF, NLAT, ZP, LANES), F32)
+    over_rows(lambda copy: copy.wait())
+
+
+def scatter(rows, ints, incoming, norm, grids):
+    grid = jax.ShapeDtypeStruct((ROWS, LANES), F32)
     return pl.pallas_call(
         scatter_kernel,
-        out_shape=(full, full),
-        in_specs=[SMEM_SPEC] + [VMEM_SPEC] * 3 + [pl.BlockSpec(memory_space=pltpu.HBM)],
-        out_specs=(VMEM_SPEC, VMEM_SPEC),
+        out_shape=(grid,) * GRIDS + (jax.ShapeDtypeStruct((NF, NLAT, ZP, LANES), F32),),
+        in_specs=[SMEM_SPEC] + [VMEM_SPEC] * 2 + [ANY_SPEC] + [VMEM_SPEC] * GRIDS,
+        out_specs=(VMEM_SPEC,) * (GRIDS + 1),
+        input_output_aliases={4 + index: index for index in range(GRIDS)},
         scratch_shapes=[
-            pltpu.VMEM((NF, NLAT, ZP, LANES), F32), pltpu.SemaphoreType.DMA((NF, NLAT)),
+            pltpu.SemaphoreType.DMA((NF, NLAT)),
             pltpu.VMEM((LANES, LANES), F32), pltpu.VMEM((CAP, LANES), F32), pltpu.VMEM((CAP, LANES), F32),
-        ]
-        + [pltpu.VMEM((ROWS, LANES), F32)] * GRIDS,
-        compiler_params=pltpu.CompilerParams(vmem_limit_bytes=40 << 20),
+        ],
+        compiler_params=pltpu.CompilerParams(vmem_limit_bytes=6 << 20),
+        cost_estimate=cost(12),
         name="scatter",
-    )(rows, lanes, incoming, depth, norm)
-
-
-def solve_kernel(
-    field_ref, scale_ref, zs_ref, zr_ref, zco_ref, ms_ref, mr_ref, mss_ref, mrr_ref, mco_all,
+    )(rows, ints, incoming, norm, *grids)
+
+
+def solve_kernel(*refs):
+    solve_body(refs[:GRIDS], *refs[GRIDS:])
+
+
+def solve_body(
+    grids, norm_ref, ints_ref, zs_ref, zr_ref, zco_ref, ms_ref, mr_ref, mss_ref, mrr_ref, mco_all,
     vert_ref, alpha, gamma, minv, sums_ref,
     x_ref,
-    zsend, zrecv, zret, zres, msend, mrecv, mret, mres,
+    zsend, zrecv, zret, zres, msend, mrecv, mval,
     acc_a, acc_b, ubuf, gbuf, mtot, mbuf,
-    z1s, z1r, z2s, z2r, m1s, m1r, m2s, m2r,
+    z1s, z1r, z2s, z2r, m1s, m1r,
 ):
     me = lax.axis_index("lon")
     my = lax.axis_index("lat")
@@ -470,11 +484,10 @@
         acc_a[...] = nothing
         acc_b[field] = nothing
         lax.fori_loop(0, NLAT // CHUNK, chunk_pass, 0)
-        acc_a[...] = acc_a[...] * zco_ref[field, 0:1, :]
+        acc_a[...] = acc_b[field] + pltpu.roll(acc_a[...] * zco_ref[field, 0:1, :], HALF, 1)
         for group in range(GROUPS):
             at = slice(GROUP * group, GROUP * group + GROUP)
-            zsend[turn, field, group, 0:GROUP, :] = acc_b[field, at, :]
-            zsend[turn, field, group, 8 : 8 + GROUP, :] = acc_a[at, :]
+            zsend[turn, field, group, 0:GROUP, :] = acc_a[at, :]
 
     def zonal_send(turn, field):
         others(field, lambda group: zonal_out(turn, field, group, me).start())
@@ -487,7 +500,7 @@
         mine = me % half
         over_lon(lambda device: zonal_out(turn, 0, 0, device).wait_recv())
         right_side = [
-            zrecv[turn, k, 0:8, :] + zrecv[turn, (k - 1) % N_LON, 8:16, :] for k in range(N_LON)
+            zrecv[turn, k] + pltpu.roll(zrecv[turn, (k - 1) % N_LON], HALF, 1) for k in range(N_LON)
         ]
         for bit in range(5):
             stride = 1 << bit
@@ -499,20 +512,19 @@
             ]
         values = [right_side[k] * minv[my_field, k : k + 1, :] for k in range(N_LON)]
         for k in range(N_LON):
-            zret[turn, k, 0:8, :] = values[k]
-            zret[turn, k, 8:16, :] = values[(k + 1) % N_LON]
+            zret[turn, k] = jnp.where(
+                iota[0:8] < HALF, values[k], pltpu.roll(values[(k + 1) % N_LON], HALF, 1)
+            )
         over_lon(lambda device: zonal_back(turn, device, my_field, mine).start())
         zres[turn, my_field, mine] = zret[turn, me]
 
     def zonal_receive(turn, field):
         others(field, lambda group: zonal_back(turn, 0, field, group).wait_recv())
         ubuf[72:80, :] = jnp.zeros((8, LANES), F32)
-        gbuf[72:80, :] = jnp.zeros((8, LANES), F32)
         for group in range(GROUPS):
             at = slice(GROUP * group, GROUP * group + GROUP)
             ubuf[at, :] = zres[turn, field, group, 0:GROUP, :]
-            gbuf[at, :] = zres[turn, field, group, 8 : 8 + GROUP, :]
-        gbuf[...] = gbuf[...] * zco_ref[field, 0:1, :] + acc_b[field]
+        gbuf[...] = pltpu.roll(ubuf[...], HALF, 1) * zco_ref[field, 0:1, :] + acc_b[field]
 
     def zonal_values(field, chunk):
         u_all, g_all = ubuf[...], gbuf[...]
@@ -550,14 +562,8 @@
 
     def merid_out(field, device, slot):
         return push(
-            msend.at[field, device], mrecv.at[field, slot],
+            msend.at[field], mrecv.at[field, slot],
             m1s.at[field, device], m1r.at[field, slot], "lat", device,
-        )
-
-    def merid_back(field, device, slot):
-        return push(
-            mret.at[field, device], mres.at[field, slot],
-            m2s.at[field, device], m2r.at[field, slot], "lat", device,
         )
 
     def merid_pass(field):
@@ -588,64 +594,56 @@
         mtot[field] = b_two
         coupling = mco_all[my, field, 0:1, :]
         for part, value in enumerate((b_one, a_one * coupling, b_two, a_two * coupling)):
-            for solver in range(N_LAT):
-                count = min(SPLIT, ZP - SPLIT * solver)
-                msend[field, solver, part, 0:count, :] = value[SPLIT * solver : SPLIT * solver + count]
-                if count < SPLIT:
-                    msend[field, solver, part, count:SPLIT, :] = jnp.zeros(
-                        (SPLIT - count, LANES), F32
-                    )
+            msend[field, part] = value
         over_lat(lambda device: merid_out(field, device, my).start())
-        mrecv[field, my] = msend[field, my]
+        mrecv[field, my] = msend[field]
 
     def merid_reduced(field):
         over_lat(lambda device: merid_out(field, 0, device).wait_recv())
         coef = lambda k, row: mco_all[k, field, row : row + 1, :]
-        part = lambda k, index: mrecv[field, k, index]
-
-        def solve_four(right_side):
-            mass = 1.0 + coef(0, 1)
-            reduced = right_side[0]
-            kept, inverses, values = [], [], [None] * N_LAT
+
+        def tile(step, _):
+            at = pl.ds(pl.multiple_of(step * 8, 8), 8)
+            part = lambda k, index: mrecv[field, k, index, at, :]
+
+            def solve_four(right_side):
+                mass = 1.0 + coef(0, 1)
+                reduced = right_side[0]
+                kept, inverses, values = [], [], [None] * N_LAT
+                for k in range(N_LAT):
+                    inverse = 1.0 / (mass + coef(k, 0))
+                    kept.append(reduced)
+                    inverses.append(inverse)
+                    if k + 1 < N_LAT:
+                        factor = coef(k, 0) * inverse
+                        mass = 1.0 + coef(k + 1, 1) + coef(k, 2) + factor * mass
+                        reduced = right_side[k + 1] + factor * reduced
+                values[-1] = kept[-1] * inverses[-1]
+                for k in range(N_LAT - 2, -1, -1):
+                    values[k] = (kept[k] + coef(k, 0) * values[k + 1]) * inverses[k]
+                return values
+
+            none = jnp.zeros((8, LANES), F32)
+            u = solve_four([part(k, 0) + (part(k - 1, 1) if k else none) for k in range(N_LAT)])
+            u = u + [none]
+            second = []
             for k in range(N_LAT):
-                inverse = 1.0 / (mass + coef(k, 0))
-                kept.append(reduced)
-                inverses.append(inverse)
-                if k + 1 < N_LAT:
-                    factor = coef(k, 0) * inverse
-                    mass = 1.0 + coef(k + 1, 1) + coef(k, 2) + factor * mass
-                    reduced = right_side[k + 1] + factor * reduced
-            values[-1] = kept[-1] * inverses[-1]
-            for k in range(N_LAT - 2, -1, -1):
-                values[k] = (kept[k] + coef(k, 0) * values[k + 1]) * inverses[k]
-            return values
-
-        none = jnp.zeros((SPLIT, LANES), F32)
-        u = solve_four([part(k, 0) + (part(k - 1, 1) if k else none) for k in range(N_LAT)]) + [none]
-        second = []
-        for k in range(N_LAT):
-            value = part(k, 2) + coef(k, 3) * u[k] + coef(k, 4) * u[k + 1]
-            if k:
-                value = value + part(k - 1, 3) + coef(k - 1, 4) * u[k - 1] + coef(k - 1, 5) * u[k]
-            second.append(value)
-        v = solve_four(second) + [none]
-        for k in range(N_LAT):
-            for index, value in enumerate((u[k], u[k + 1], v[k], v[k + 1])):
-                mret[field, k, index] = value
-        over_lat(lambda device: merid_back(field, device, my).start())
-        mres[field, my] = mret[field, my]
-
-    def merid_receive(field):
-        over_lat(lambda device: merid_back(field, 0, device).wait_recv())
-        for index in range(4):
-            for solver in range(N_LAT):
-                count = min(SPLIT, ZP - SPLIT * solver)
-                mbuf[index, SPLIT * solver : SPLIT * solver + count, :] = mres[
-                    field, solver, index, 0:count, :
-                ]
+                value = part(k, 2) + coef(k, 3) * u[k] + coef(k, 4) * u[k + 1]
+                if k:
+                    value = value + part(k - 1, 3) + coef(k - 1, 4) * u[k - 1] + coef(k - 1, 5) * u[k]
+                second.append(value)
+            v = solve_four(second) + [none]
+            for k in range(N_LAT + 1):
+                mval[0, k, at, :] = u[k]
+                mval[1, k, at, :] = v[k]
+            return 0
+
+        lax.fori_loop(0, ZP // 8, tile, 0)
         coupling = mco_all[my, field, 0:1, :]
-        mbuf[1] = mbuf[1] * coupling
-        mbuf[3] = mbuf[3] * coupling + mtot[field]
+        mbuf[0] = mval[0, my]
+        mbuf[1] = mval[0, my + 1] * coupling
+        mbuf[2] = mval[1, my]
+        mbuf[3] = mval[1, my + 1] * coupling + mtot[field]
 
     def merid_value(field, row):
         at = pl.ds(row, 1)
@@ -657,10 +655,26 @@
             + ms_ref[field, at, :] * mbuf[3]
         )
 
-    zonal_pass(0, 0, lambda row: field_ref[0, row])
+    level = lax.broadcasted_iota(jnp.int32, (ZP, LANES), 0)
+
+    def scale(field, row):
+        wet = level < ints_ref[pl.ds(DEPTH_AT + row, 1), :]
+        return jnp.where(wet, norm_ref[field, row], 0.0)
+
+    def scaled_grid(field):
+        def load(row):
+            at = pl.ds(pl.multiple_of((field * NLAT + row) * ZP, ZP), ZP)
+            total = [grid[at, :] for grid in grids]
+            while len(total) > 1:
+                total = [one + two for one, two in zip(total[::2], total[1::2])]
+            return scale(field, row) * total[0]
+
+        return load
+
+    zonal_pass(0, 0, scaled_grid(0))
     greeted()
     zonal_send(0, 0)
-    zonal_pass(0, 1, lambda row: field_ref[1, row])
+    zonal_pass(0, 1, scaled_grid(1))
     zonal_send(0, 1)
     vertical_field(0)
     pl.when(is_solver & (my_field == 0))(lambda: zonal_reduced(0))
@@ -673,11 +687,9 @@
         ubuf[...] = both[:, :LANES]
         gbuf[...] = both[:, LANES:]
         merid_pass(field)
+
     for field in range(NF):
         merid_reduced(field)
-
-    for field in range(NF):
-        merid_receive(field)
         zonal_pass(1, field, lambda row, field=field: merid_value(field, row))
         zonal_send(1, field)
     pl.when(is_solver)(lambda: zonal_reduced(1))
@@ -688,14 +700,13 @@
             found = zonal_values(field, chunk)
             for step in range(CHUNK):
                 row = chunk * CHUNK + step
-                x_ref[field, row] = found[step] * scale_ref[field, row]
+                x_ref[field, row] = found[step] * scale(field, row)
             return 0
 
         lax.fori_loop(0, NLAT // CHUNK, last_pass, 0)
 
     for field in range(NF):
         over_lat(lambda device, field=field: merid_out(field, device, my).wait_send())
-        over_lat(lambda device, field=field: merid_back(field, device, my).wait_send())
         for turn in range(2):
             others(
                 field,
@@ -708,32 +719,32 @@
             over_lon(lambda device, turn=turn: zonal_back(turn, device, 0, 0).wait_send())
 
 
-def solve(field, scale, coefs):
+def solve(grids, norm, ints, coefs):
     dma = pltpu.SemaphoreType.DMA
     vmem = lambda *dims: pltpu.VMEM(dims, F32)
     return pl.pallas_call(
         solve_kernel,
         out_shape=jax.ShapeDtypeStruct((NF, NLAT, ZP, LANES), F32),
-        in_specs=[VMEM_SPEC] * 15,
+        in_specs=[VMEM_SPEC] * (15 + GRIDS),
         out_specs=VMEM_SPEC,
         scratch_shapes=[
-            vmem(2, NF, GROUPS, 16, LANES), vmem(2, N_LON, 16, LANES),
-            vmem(2, N_LON, 16, LANES), vmem(2, NF, GROUPS, 16, LANES),
-            vmem(NF, N_LAT, 4, SPLIT, LANES), vmem(NF, N_LAT, 4, SPLIT, LANES),
-            vmem(NF, N_LAT, 4, SPLIT, LANES), vmem(NF, N_LAT, 4, SPLIT, LANES),
+            vmem(2, NF, GROUPS, 8, LANES), vmem(2, N_LON, 8, LANES),
+            vmem(2, N_LON, 8, LANES), vmem(2, NF, GROUPS, 8, LANES),
+            vmem(NF, 4, ZP, LANES), vmem(NF, N_LAT, 4, ZP, LANES), vmem(2, N_LAT + 1, ZP, LANES),
             vmem(ZP, LANES), vmem(NF, ZP, LANES), vmem(ZP, LANES), vmem(ZP, LANES),
             vmem(NF, ZP, LANES), vmem(4, ZP, LANES),
             dma((2, NF, GROUPS)), dma((2, N_LON)), dma((2, N_LON)), dma((2, NF, GROUPS)),
-            dma((NF, N_LAT)), dma((NF, N_LAT)), dma((NF, N_LAT)), dma((NF, N_LAT)),
+            dma((NF, N_LAT)), dma((NF, N_LAT)),
         ],
         compiler_params=pltpu.CompilerParams(
-            collective_id=1, has_side_effects=True, vmem_limit_bytes=20 << 20
+            collective_id=1, has_side_effects=True, vmem_limit_bytes=10 << 20
         ),
+        cost_estimate=cost(40),
         name="solve",
-    )(field, scale, *coefs)
-
-
-def pick_kernel(rows_ref, lane_ref, x_ref, out_ref, inc_ref, inc_sem, *copies):
+    )(*grids, norm, ints, *coefs)
+
+
+def pick_kernel(rows_ref, ints_ref, x_ref, out_ref, inc_ref, inc_sem, *copies):
     iota = lane_iota(8)
 
     def inc_copy(field, row):
@@ -760,12 +771,14 @@
         for part in range(group):
             q = step * group + part
             for k in range(CAP):
-                copies[part][k : k + 1, :] = x_ref[pl.ds(rows_ref[k * RANKS + q], 1), :]
+                copies[part][k : k + 1, :] = x_ref[pl.ds(rows_ref[k, q], 1), :]
         for part in range(group):
             q = step * group + part
             for tile in range(CAP // 8):
                 at = slice(8 * tile, 8 * tile + 8)
-                found = lane_pick(copies[part][at, :], lane_ref[at, :])
+                found = lane_pick(
+                    copies[part][at, :], ints_ref[CAP + 8 * tile : CAP + 8 * tile + 8, :]
+                )
                 acc[tile] = jnp.where(iota == q, found, acc[tile])
         return tuple(acc)
 
@@ -778,7 +791,7 @@
     over_rows(lambda copy: copy.wait())
 
 
-def pick(rows, lanes, increment):
+def pick(rows, ints, increment):
     return pl.pallas_call(
         pick_kernel,
         out_shape=(
@@ -789,57 +802,57 @@
         out_specs=(VMEM_SPEC, ANY_SPEC),
         scratch_shapes=[pltpu.SemaphoreType.DMA((NF, NLAT))] + [pltpu.VMEM((CAP, LANES), F32)] * 8,
         compiler_params=pltpu.CompilerParams(vmem_limit_bytes=8 << 20),
+        cost_estimate=cost(14),
         name="pick",
-    )(rows, lanes, increment.reshape(ROWS, LANES))
+    )(rows, ints, increment.reshape(ROWS, LANES))
 
 
 def place_kernel(
-    tile_out, send_ref, out_ref, idx_ref, val_ref, tile_in, rows_out, rows_in, b1s, b1r, b2s, b2r
+    tile_out, ints_ref, out_ref,
+    idx_ref, val_ref, rows_oh, cols_oh, tile_in, rows_out, rows_in, b1s, b1r, b2s, b2r,
 ):
     greet()
     none = jnp.full((LANES - CAP, LANES), -1, jnp.int32)
-    idx_ref[...] = jnp.transpose(jnp.concatenate([send_ref[...], none], axis=0))
+    idx_ref[...] = jnp.transpose(jnp.concatenate([ints_ref[0:CAP, :], none], axis=0))
     begin, middle, end, sent = two_phase(tile_out, tile_in, rows_out, rows_in, (b1s, b1r, b2s, b2r))
     row_iota = lax.broadcasted_iota(jnp.int32, (CAP, 2 * LANES), 0)
     col_iota = lax.broadcasted_iota(jnp.int32, (LANES, 2 * LANES), 0)
-    lane = lax.broadcasted_iota(jnp.int32, (LANES, 2 * LANES), 1)
-    slot = (lane & 127).astype(F32)
-    second_half = lane >> 7
-
-    def pair(step, acc):
-        left, right = pl.ds(2 * step, 1), pl.ds(2 * step + 1, 1)
-        index = jnp.concatenate([idx_ref[left, :], idx_ref[right, :]], axis=1)
-        rows = jnp.where(row_iota == (index >> 7), 1.0, 0.0).astype(BF16)
-        here = col_iota == (index & 127)
-        number = 2 * step + second_half
-        number = ((number % N_LAT) * N_LON + number // N_LAT + 1).astype(F32)
-        columns = jnp.concatenate(
-            [jnp.where(here, number, 0.0).astype(BF16), jnp.where(here, slot, 0.0).astype(BF16)],
-            axis=0,
-        )
+
+    def build(step, _):
+        lat = step // (N_LON // 2)
+        left = (step % (N_LON // 2)) * 2 * N_LAT + lat
+        index = jnp.concatenate(
+            [idx_ref[pl.ds(left, 1), :], idx_ref[pl.ds(left + N_LAT, 1), :]], axis=1
+        )
+        rows_oh[step] = jnp.where(row_iota == (index >> 7), 1.0, 0.0).astype(BF16)
+        cols_oh[step] = jnp.where(col_iota == (index & 127), 1.0, 0.0).astype(BF16)
+        return 0
+
+    def add(step, acc):
+        value = jnp.concatenate(
+            [val_ref[pl.ds(2 * step, 1), :], val_ref[pl.ds(2 * step + 1, 1), :]], axis=1
+        )
+        high, low = split(value)
+        rows = rows_oh[step]
         return acc + lax.dot_general(
-            rows, columns, (((1,), (1,)), ((), ())), preferred_element_type=F32
-        )
-
-    def pairs(start, stop, acc):
-        return lax.fori_loop(start, stop, pair, acc, unroll=4)
-
-    acc = jnp.zeros((CAP, 2 * LANES), F32)
+            jnp.concatenate([rows * high, rows * low], axis=0), cols_oh[step],
+            (((1,), (1,)), ((), ())), preferred_element_type=F32,
+        )
+
     greeted()
     begin()
-    acc = pairs(0, RANKS // 4, acc)
+    lax.fori_loop(0, RANKS // 4, build, 0, unroll=2)
     middle()
-    acc = pairs(RANKS // 4, RANKS // 2, acc)
-    high = acc[:, :LANES].astype(jnp.int32)
-    low = acc[:, LANES:].astype(jnp.int32)
+    lax.fori_loop(RANKS // 4, RANKS // 2, build, 0, unroll=2)
     end()
     for lat in range(N_LAT):
         val_ref[N_LON * lat : N_LON * lat + N_LON, :] = rows_in[lat]
-    out_ref[...] = gather_lines(val_ref, RANKS, high, low, 1)
+    acc = lax.fori_loop(0, RANKS // 2, add, jnp.zeros((2 * CAP, LANES), F32), unroll=8)
+    out_ref[...] = acc[:CAP] + acc[CAP:]
     sent()
 
 
-def place(tiles, send_list):
+def place(tiles, ints):
     vmem = lambda *dims: pltpu.VMEM(dims, F32)
     dma = pltpu.SemaphoreType.DMA
     return pl.pallas_call(
@@ -849,14 +862,17 @@
         out_specs=VMEM_SPEC,
         scratch_shapes=[
             pltpu.VMEM((RANKS, LANES), jnp.int32), vmem(RANKS, LANES),
+            pltpu.VMEM((RANKS // 2, CAP, 2 * LANES), BF16),
+            pltpu.VMEM((RANKS // 2, LANES, 2 * LANES), BF16),
             vmem(N_LON, 8, LANES), vmem(N_LAT, N_LON, LANES), vmem(N_LAT, N_LON, LANES),
             dma((N_LON,)), dma((N_LON,)), dma((N_LAT,)), dma((N_LAT,)),
         ],
         compiler_params=pltpu.CompilerParams(
-            collective_id=2, has_side_effects=True, vmem_limit_bytes=6 << 20
+            collective_id=2, has_side_effects=True, vmem_limit_bytes=10 << 20
         ),
+        cost_estimate=cost(15),
         name="place",
-    )(tiles, send_list)
+    )(tiles, ints)
 
 
 def local(
@@ -864,23 +880,30 @@
 ):
     is_north = lax.axis_index("lat") == N_LAT - 1
     north = jnp.full((8, LANES), jnp.where(is_north, 1.0, 0.0), F32)
-    sends = jnp.transpose(send_list)
-    incoming, *coefs = prepare(
-        obs_value.reshape(CAP, LANES), sends, zonal_weight, merid_weight, north,
-        jnp.transpose(vert_inverse, (1, 0, 2)),
-    )
     cell = jnp.maximum(jnp.transpose(recv_cell), 0)
     line = cell >> 7
     plane = line // NLAT
     lat_row = line - plane * NLAT
     field = (plane >= NZ).astype(jnp.int32)
     level = plane - field * NZ
-    rows = ((field * NLAT + lat_row) * ZP + level).reshape(-1)
-
-    gridded, scale = scatter(rows, cell & 127, incoming, column_depth, norm_scale)
-    whole = solve(gridded, scale, coefs)
-    tiles, increment = pick(rows, cell & 127, whole)
-    return increment, place(tiles, sends).reshape(-1)
+    rows = (field * NLAT + lat_row) * ZP + level
+    ints = jnp.concatenate([jnp.transpose(send_list), cell & 127, column_depth], axis=0)
+    vert = jnp.transpose(vert_inverse, (1, 0, 2)).reshape(NF * NZ, NZ)
+    floats = jnp.concatenate(
+        [
+            obs_value.reshape(CAP, LANES),
+            zonal_weight.reshape(NF * NLAT, LANES),
+            merid_weight.reshape(NF * NLAT, LANES),
+            jnp.pad(vert, ((0, 0), (0, LANES - NZ))),
+        ],
+        axis=0,
+    )
+    made = prepare(ints, floats, north)
+    incoming, coefs, grids = made[0], made[1:14], made[14:]
+    *grids, norm = scatter(rows, ints, incoming, norm_scale, grids)
+    whole = solve(grids, norm, ints, coefs)
+    tiles, increment = pick(rows, ints, whole)
+    return increment, place(tiles, ints).reshape(-1)
 
 
 def solution(mesh):

time: 132 us -> 129 us (0.977)
  local copies, waits for them, and re-layouts: 7.21 us -> 3.43 us
  other arithmetic: 1.61 us -> 3.26 us
    unnamed x17 -> x3, local copies, waits for them, and re-layouts: 7.21 us -> 2.48 us
    pallas_call x1, Pallas kernels: 17.7 us -> 14.7 us  [place(): pl.pallas_call(place_kernel, out_shape=jax.ShapeDtypeStruct((CAP, LANES),...]
    pallas_call x1, Pallas kernels: 20.3 us -> 17.7 us  [scatter(): pl.pallas_call(scatter_kernel, out_shape=(grid,) * GRIDS + (jax.ShapeDtyp...]
    pallas_call x1, Pallas kernels: 14.5 us -> 17 us  [pick(): pl.pallas_call(pick_kernel, out_shape=(jax.ShapeDtypeStruct((N_LON, 8, LA...]
    pallas_call x1, Pallas kernels: 49.2 us -> 51.4 us  [solve(): pl.pallas_call(solve_kernel, out_shape=jax.ShapeDtypeStruct((NF, NLAT, ZP...]
    concatenate x0 -> x2, other arithmetic: none -> 1.64 us  [the longest x1 0.84 us: local(): jnp.concatenate([obs_value.reshape(CAP, LANES), zonal_weight.reshape(NF *...]
where the time goes in v3:
time: 129 us
  Pallas kernels  122 us (95%)
  local copies, waits for them, and re-layouts  3.43 us (3%)
  other arithmetic  3.26 us (3%)
    pallas_call x1, Pallas kernels, solve(): pl.pallas_call(solve_kernel, out_shape=jax.ShapeDtypeStruct((NF, NLAT, ZP...  51.4 us
    pallas_call x1, Pallas kernels, prepare(): pl.pallas_call(prepare_kernel, out_shape=(shape(RANKS, LANES), shape(80,...  20.8 us
    pallas_call x1, Pallas kernels, scatter(): pl.pallas_call(scatter_kernel, out_shape=(grid,) * GRIDS + (jax.ShapeDtyp...  17.7 us
    pallas_call x1, Pallas kernels, pick(): pl.pallas_call(pick_kernel, out_shape=(jax.ShapeDtypeStruct((N_LON, 8, LA...  17 us
    pallas_call x1, Pallas kernels, place(): pl.pallas_call(place_kernel, out_shape=jax.ShapeDtypeStruct((CAP, LANES),...  14.7 us

profile of v3, /device:TPU:1, one launch (start us, length us, event | category | flops | bytes accessed | tf_op | source)
XLA Modules:
  0.0 129.1 jit_solution(12600929460876369238)
XLA Ops:
  0.6 0.8 fusion.4.rows_ref
  1.5 0.8 and_bitcast_fusion
  2.3 0.8 pad_add_fusion.ints_ref.refs_9_
  3.1 0.9 reshape.25
  4.0 0.8 select_maximum_fusion.floats_ref
  4.9 20.8 %prepare.1 = (f32[128,128]{1,0:T(8,128)S(1)}, f32[80,128]{1,0:T(8,128)S(1)}, f32[80,128]{1,0:T(8,128)S(1)}, f32[2,8,128]{2,1,0:T(8,128)S(1)}, f32[2,40,128]{2,1,...) custom-call(s32[200,128]{1,0:T(8,128)S(1)} %pad_add_fusion.ints_ref., ...), custom_call_target="tpu_custom_call" | custom-call | bytes 54000000 | tf_op jit(solution)/shard_map/prepare/pallas_call | solution.py:321
  25.6 0.0 copy-start
  25.7 1.9 %copy-done = f32[2,75,40,128]{3,2,1,0:T(8,128)S(1)} copy-done((f32[2,75,40,128]{3,2,1,0:T(8,128)S(1)}, f32[2,75,40,128]{3,2,1,0:T(8,128)}, u32[]{:S(2)}) %copy-start) | copy-done | bytes 3072024
  27.5 17.7 %scatter.1 = (f32[6400,128]{1,0:T(8,128)S(1)}, f32[6400,128]{1,0:T(8,128)S(1)}, f32[6400,128]{1,0:T(8,128)S(1)}, f32[6400,128]{1,0:T(8,128)S(1)}, f32[6400,128]{...) custom-call(s32[80,128]{1,0:T(8,128)S(1)} %fusion.4.rows_ref, ...), custom_call_target="tpu_custom_call", output_to_operand_aliasing={{0}: (4, {}), {1}: (5, {}), {2}: (6, {}), {3}: (7, {}), {4}... | custom-call | bytes 43200000 | tf_op jit(solution)/shard_map/scatter/pallas_call | solution.py:403
  45.3 51.4 %solve.1 = f32[2,40,80,128]{3,2,1,0:T(8,128)S(1)} custom-call(f32[6400,128]{1,0:T(8,128)S(1)} %get-tuple-element.44.refs_0_, f32[6400,128]{1,0:T(8,128)S(1)} %get-tuple-element.45.refs_1_, f32[6400,128]{1,0:T(8,128)S(1)} %get-tuple-element.46.refs_2_, f32[6400,128]{1,0:T(8,128)S(1)} %get-tuple-element.47.refs_3_, f32[6400,128]{1,0:T(8,128)S(1)} %get-tuple-element.48.refs_4_, ...), custom_call_target="tpu_custom_call" | custom-call | bytes 144000000 | tf_op jit(solution)/shard_map/solve/pallas_call | solution.py:725
  96.7 17.0 %pick.1 = (f32[32,8,128]{2,1,0:T(8,128)S(1)}, f32[2,75,40,128]{3,2,1,0:T(8,128)}) custom-call(s32[80,128]{1,0:T(8,128)S(1)} %fusion.4.rows_ref, s32[200,128]{1,0:T(8,128)S(1)} %pad_add_fusion.ints_ref.refs_9_, f32[6400,128]{1,0:T(8,128)S(1)} %bitcast.34), custom_call_target="tpu_custom_call" | custom-call | bytes 50400000 | tf_op jit(solution)/shard_map/pick/pallas_call | solution.py:795
  113.7 14.7 %place.1 = f32[80,128]{1,0:T(8,128)S(1)} custom-call(f32[32,8,128]{2,1,0:T(8,128)S(1)} %get-tuple-element.67.tile_out, s32[200,128]{1,0:T(8,128)S(1)} %pad_add_fusion.ints_ref.refs_9_), custom_call_target="tpu_custom_call" | custom-call | bytes 54000000 | tf_op jit(solution)/shard_map/place/pallas_call | solution.py:858
  128.4 0.6 copy.27
  (1 shorter events, 0.0 us)
Async XLA Ops:
  25.6 1.9 %copy-start = (f32[2,75,40,128]{3,2,1,0:T(8,128)S(1)}, f32[2,75,40,128]{3,2,1,0:T(8,128)}, u32[]{:S(2)}) copy-start(f32[2,75,40,128]{3,2,1,0:T(8,128)} %norm_ref.1) | copy-start | bytes 9216004

commit v4 on v3

--- a/solution.py
+++ b/solution.py
@@ -15,8 +15,9 @@
 GROUPS = 15
 GROUP = 5
 LANES = 128
-CHUNK = 8
+CHUNK = 20
 HALF = 64
+VERT_CHUNK = 10
 GRIDS = 8
 ROWS = NF * NLAT * ZP
 ZW_AT, MW_AT, VERT_AT = 80, 160, 240
@@ -235,19 +236,19 @@
 def prepare_kernel(
     ints_ref, floats_ref, north_ref,
     out_ref, zs_ref, zr_ref, zco_out, ms_ref, mr_ref, mss_ref, mrr_ref, mco_out, vert_ref,
-    alpha, gamma, minv, sums_ref, *rest
+    alpha, gamma, minv, sums_ref, row_ref, *rest
 ):
     grids, rest = rest[:GRIDS], rest[GRIDS:]
     prepare_body(
         ints_ref, floats_ref, north_ref, out_ref, zs_ref, zr_ref, zco_out, ms_ref, mr_ref, mss_ref,
-        mrr_ref, mco_out, vert_ref, alpha, gamma, minv, sums_ref, grids, *rest,
+        mrr_ref, mco_out, vert_ref, alpha, gamma, minv, sums_ref, row_ref, grids, *rest,
     )
 
 
 def prepare_body(
     ints_ref, floats_ref, north_ref,
     out_ref, zs_ref, zr_ref, zco_out, ms_ref, mr_ref, mss_ref, mrr_ref, mco_out, vert_ref,
-    alpha, gamma, minv, sums_ref, grids,
+    alpha, gamma, minv, sums_ref, row_ref, grids,
     iw_ref, st_ref, rt_ref, miw_ref, prod_ref,
     tile_out, tile_in, rows_out, rows_in, zco_ref, zco_all, mco_ref, mco_all,
     o1s, o1r, o2s, o2r, zco_s, zco_r, mco_s, mco_r,
@@ -275,14 +276,19 @@
     begin()
     zero = north_ref[...] * 0.0
     zonal_coefs(floats_ref, zs_ref, zr_ref, zco_ref, iw_ref, st_ref, rt_ref, zero)
-    middle()
     over_lon(lambda device: zco_copy(device, me).start())
     zco_all[me] = zco_ref[...]
-    for field in range(NF):
-        zco_out[field] = to_field(zco_ref[...], field)
     merid_coefs(floats_ref, ms_ref, mr_ref, mss_ref, mrr_ref, mco_ref, miw_ref, north_ref[...], zero)
     over_lat(lambda device: mco_copy(device, my).start())
     mco_all[my] = mco_ref[...]
+    middle()
+    for field in range(NF):
+        zco_out[field] = to_field(zco_ref[...], field)
+    cell = jnp.maximum(ints_ref[CAP : 2 * CAP, :], 0)
+    line = cell >> 7
+    plane = line // NLAT
+    second_field = (plane >= NZ).astype(jnp.int32)
+    row_ref[...] = (second_field * NLAT + line - plane * NLAT) * ZP + plane - second_field * NZ
     prod_ref[...] = jnp.zeros((ZP, LANES), F32)
     for field in range(NF):
         matrix = floats_ref[pl.ds(VERT_AT + field, NZ, stride=NF), :]
@@ -327,10 +333,11 @@
             jax.ShapeDtypeStruct((NF, ZP, 3 * ZP), BF16),
             shape(NF, 5, N_LON, LANES), shape(NF, 5, N_LON, LANES), shape(NF, N_LON, LANES),
             jax.ShapeDtypeStruct((2 * LANES, 2 * LANES), BF16),
+            jax.ShapeDtypeStruct((CAP, LANES), jnp.int32),
         )
         + (shape(ROWS, LANES),) * GRIDS,
         in_specs=[VMEM_SPEC] * 3,
-        out_specs=(VMEM_SPEC,) * (14 + GRIDS),
+        out_specs=(VMEM_SPEC,) * (15 + GRIDS),
         scratch_shapes=[
             vmem(LANES, LANES), vmem(LANES, LANES), vmem(LANES, LANES), vmem(NF, NLAT, LANES),
             vmem(ZP, LANES),
@@ -375,12 +382,12 @@
     def spread(q):
         index = jnp.full((CAP, LANES), q, jnp.int32)
         place = jnp.full((CAP, LANES), (q % N_LAT) * N_LON + q // N_LAT, jnp.int32)
-        lane = lane_pick(ints_ref[CAP : 2 * CAP, :], index)
+        lane = lane_pick(ints_ref[CAP : 2 * CAP, :] & 127, index)
         return jnp.where(iota == lane, lane_pick(value_ref[:CAP, :], place), 0.0)
 
     def add(q, source):
         for k in range(CAP):
-            at = pl.ds(rows_ref[k, q], 1)
+            at = pl.ds(rows_ref[k * RANKS + q], 1)
             grid = grids[k % GRIDS]
             grid[at, :] = grid[at, :] + source[k : k + 1, :]
 
@@ -550,14 +557,14 @@
 
     def vertical_field(field):
         def body(step, _):
-            row = step * CHUNK
-            value = jnp.concatenate([x_ref[field, row + k] for k in range(CHUNK)], axis=1)
+            row = step * VERT_CHUNK
+            value = jnp.concatenate([x_ref[field, row + k] for k in range(VERT_CHUNK)], axis=1)
             value = vertical(field, value)
-            for k in range(CHUNK):
+            for k in range(VERT_CHUNK):
                 x_ref[field, row + k] = value[:, k * LANES : (k + 1) * LANES]
             return 0
 
-        lax.fori_loop(0, NLAT // CHUNK, body, 0)
+        lax.fori_loop(0, NLAT // VERT_CHUNK, body, 0)
 
 
     def merid_out(field, device, slot):
@@ -771,13 +778,13 @@
         for part in range(group):
             q = step * group + part
             for k in range(CAP):
-                copies[part][k : k + 1, :] = x_ref[pl.ds(rows_ref[k, q], 1), :]
+                copies[part][k : k + 1, :] = x_ref[pl.ds(rows_ref[k * RANKS + q], 1), :]
         for part in range(group):
             q = step * group + part
             for tile in range(CAP // 8):
                 at = slice(8 * tile, 8 * tile + 8)
                 found = lane_pick(
-                    copies[part][at, :], ints_ref[CAP + 8 * tile : CAP + 8 * tile + 8, :]
+                    copies[part][at, :], ints_ref[CAP + 8 * tile : CAP + 8 * tile + 8, :] & 127
                 )
                 acc[tile] = jnp.where(iota == q, found, acc[tile])
         return tuple(acc)
@@ -800,7 +807,7 @@
         ),
         in_specs=[SMEM_SPEC, VMEM_SPEC, VMEM_SPEC],
         out_specs=(VMEM_SPEC, ANY_SPEC),
-        scratch_shapes=[pltpu.SemaphoreType.DMA((NF, NLAT))] + [pltpu.VMEM((CAP, LANES), F32)] * 8,
+        scratch_shapes=[pltpu.SemaphoreType.DMA((NF, NLAT))] + [pltpu.VMEM((CAP, LANES), F32)] * 16,
         compiler_params=pltpu.CompilerParams(vmem_limit_bytes=8 << 20),
         cost_estimate=cost(14),
         name="pick",
@@ -880,14 +887,9 @@
 ):
     is_north = lax.axis_index("lat") == N_LAT - 1
     north = jnp.full((8, LANES), jnp.where(is_north, 1.0, 0.0), F32)
-    cell = jnp.maximum(jnp.transpose(recv_cell), 0)
-    line = cell >> 7
-    plane = line // NLAT
-    lat_row = line - plane * NLAT
-    field = (plane >= NZ).astype(jnp.int32)
-    level = plane - field * NZ
-    rows = (field * NLAT + lat_row) * ZP + level
-    ints = jnp.concatenate([jnp.transpose(send_list), cell & 127, column_depth], axis=0)
+    ints = jnp.concatenate(
+        [jnp.transpose(send_list), jnp.transpose(recv_cell), column_depth], axis=0
+    )
     vert = jnp.transpose(vert_inverse, (1, 0, 2)).reshape(NF * NZ, NZ)
     floats = jnp.concatenate(
         [
@@ -899,7 +901,7 @@
         axis=0,
     )
     made = prepare(ints, floats, north)
-    incoming, coefs, grids = made[0], made[1:14], made[14:]
+    incoming, coefs, rows, grids = made[0], made[1:14], made[14].reshape(-1), made[15:]
     *grids, norm = scatter(rows, ints, incoming, norm_scale, grids)
     whole = solve(grids, norm, ints, coefs)
     tiles, increment = pick(rows, ints, whole)

time: 129 us -> 123 us (0.953)
  Pallas kernels: 122 us -> 117 us
  other arithmetic: 3.26 us -> 1.66 us
    pallas_call x1, Pallas kernels: 17 us -> 14 us  [pick(): pl.pallas_call(pick_kernel, out_shape=(jax.ShapeDtypeStruct((N_LON, 8, LA...]
where the time goes in v4:
time: 123 us
  Pallas kernels  117 us (95%)
  local copies, waits for them, and re-layouts  3.43 us (3%)
  other arithmetic  1.66 us (1%)
    pallas_call x1, Pallas kernels, solve(): pl.pallas_call(solve_kernel, out_shape=jax.ShapeDtypeStruct((NF, NLAT, ZP...  50.5 us
    pallas_call x1, Pallas kernels, prepare(): pl.pallas_call(prepare_kernel, out_shape=(shape(RANKS, LANES), shape(80,...  20.4 us
    pallas_call x1, Pallas kernels, scatter(): pl.pallas_call(scatter_kernel, out_shape=(grid,) * GRIDS + (jax.ShapeDtyp...  16.6 us
    pallas_call x1, Pallas kernels, place(): pl.pallas_call(place_kernel, out_shape=jax.ShapeDtypeStruct((CAP, LANES),...  15.5 us
    pallas_call x1, Pallas kernels, pick(): pl.pallas_call(pick_kernel, out_shape=(jax.ShapeDtypeStruct((N_LON, 8, LA...  14 us
    unnamed x3, local copies, waits for them, and re-layouts  2.48 us

profile of v4, /device:TPU:1, one launch (start us, length us, event | category | flops | bytes accessed | tf_op | source)
XLA Modules:
  0.0 122.8 jit_solution(1039259699143890538)
XLA Ops:
  0.6 0.9 reshape.28
  1.6 0.8 pad_add_fusion.ints_ref.refs_9_
  2.4 0.8 select_maximum_fusion.floats_ref
  3.3 20.4 %prepare.1 = (f32[128,128]{1,0:T(8,128)S(1)}, f32[80,128]{1,0:T(8,128)S(1)}, f32[80,128]{1,0:T(8,128)S(1)}, f32[2,8,128]{2,1,0:T(8,128)S(1)}, f32[2,40,128]{2,1,...) custom-call(s32[200,128]{1,0:T(8,128)S(1)} %pad_add_fusion.ints_ref., ...), custom_call_target="tpu_custom_call" | custom-call | bytes 54000000 | tf_op jit(solution)/shard_map/prepare/pallas_call | solution.py:327
  23.7 0.0 copy-start
  23.7 1.9 %copy-done = f32[2,75,40,128]{3,2,1,0:T(8,128)S(1)} copy-done((f32[2,75,40,128]{3,2,1,0:T(8,128)S(1)}, f32[2,75,40,128]{3,2,1,0:T(8,128)}, u32[]{:S(2)}) %copy-start) | copy-done | bytes 3072024
  25.5 16.6 %scatter.1 = (f32[6400,128]{1,0:T(8,128)S(1)}, f32[6400,128]{1,0:T(8,128)S(1)}, f32[6400,128]{1,0:T(8,128)S(1)}, f32[6400,128]{1,0:T(8,128)S(1)}, f32[6400,128]{...) custom-call(s32[10240]{0:T(1024)S(1)} %bitcast.11, ...), custom_call_target="tpu_custom_call", output_to_operand_aliasing={{0}: (4, {}), {1}: (5, {}), {2}: (6, {}), {3}: (7, {}), {4}... | custom-call | bytes 43200000 | tf_op jit(solution)/shard_map/scatter/pallas_call | solution.py:410
  42.2 50.5 %solve.1 = f32[2,40,80,128]{3,2,1,0:T(8,128)S(1)} custom-call(f32[6400,128]{1,0:T(8,128)S(1)} %get-tuple-element.46.refs_0_, f32[6400,128]{1,0:T(8,128)S(1)} %get-tuple-element.47.refs_1_, f32[6400,128]{1,0:T(8,128)S(1)} %get-tuple-element.48.refs_2_, f32[6400,128]{1,0:T(8,128)S(1)} %get-tuple-element.49.refs_3_, f32[6400,128]{1,0:T(8,128)S(1)} %get-tuple-element.50.refs_4_, ...), custom_call_target="tpu_custom_call" | custom-call | bytes 144000000 | tf_op jit(solution)/shard_map/solve/pallas_call | solution.py:732
  92.7 14.0 %pick.1 = (f32[32,8,128]{2,1,0:T(8,128)S(1)}, f32[2,75,40,128]{3,2,1,0:T(8,128)}) custom-call(s32[10240]{0:T(1024)S(1)} %bitcast.12, s32[200,128]{1,0:T(8,128)S(1)} %pad_add_fusion.ints_ref.refs_9_, f32[6400,128]{1,0:T(8,128)S(1)} %bitcast.9), custom_call_target="tpu_custom_call" | custom-call | bytes 50400000 | tf_op jit(solution)/shard_map/pick/pallas_call | solution.py:802
  106.7 15.5 %place.1 = f32[80,128]{1,0:T(8,128)S(1)} custom-call(f32[32,8,128]{2,1,0:T(8,128)S(1)} %get-tuple-element.69.tile_out, s32[200,128]{1,0:T(8,128)S(1)} %pad_add_fusion.ints_ref.refs_9_), custom_call_target="tpu_custom_call" | custom-call | bytes 54000000 | tf_op jit(solution)/shard_map/place/pallas_call | solution.py:865
  122.2 0.6 copy.27
  (1 shorter events, 0.0 us)
Async XLA Ops:
  23.7 1.9 %copy-start = (f32[2,75,40,128]{3,2,1,0:T(8,128)S(1)}, f32[2,75,40,128]{3,2,1,0:T(8,128)}, u32[]{:S(2)}) copy-start(f32[2,75,40,128]{3,2,1,0:T(8,128)} %norm_ref.1) | copy-start | bytes 9216004

commit v5 on v4

--- a/solution.py
+++ b/solution.py
@@ -17,6 +17,7 @@
 LANES = 128
 CHUNK = 20
 HALF = 64
+SPLIT = 24
 VERT_CHUNK = 10
 GRIDS = 8
 ROWS = NF * NLAT * ZP
@@ -284,11 +285,13 @@
     middle()
     for field in range(NF):
         zco_out[field] = to_field(zco_ref[...], field)
-    cell = jnp.maximum(ints_ref[CAP : 2 * CAP, :], 0)
+    cell = ints_ref[CAP : 2 * CAP, :]
     line = cell >> 7
     plane = line // NLAT
     second_field = (plane >= NZ).astype(jnp.int32)
-    row_ref[...] = (second_field * NLAT + line - plane * NLAT) * ZP + plane - second_field * NZ
+    live_row = (second_field * NLAT + line - plane * NLAT) * ZP + plane - second_field * NZ
+    dead_row = lax.broadcasted_iota(jnp.int32, (CAP, LANES), 0) * ZP + NZ
+    row_ref[...] = jnp.where(cell >= 0, live_row, dead_row)
     prod_ref[...] = jnp.zeros((ZP, LANES), F32)
     for field in range(NF):
         matrix = floats_ref[pl.ds(VERT_AT + field, NZ, stride=NF), :]
@@ -431,9 +434,9 @@
     grids, norm_ref, ints_ref, zs_ref, zr_ref, zco_ref, ms_ref, mr_ref, mss_ref, mrr_ref, mco_all,
     vert_ref, alpha, gamma, minv, sums_ref,
     x_ref,
-    zsend, zrecv, zret, zres, msend, mrecv, mval,
+    zsend, zrecv, zret, zres, msend, mrecv, mret, mres,
     acc_a, acc_b, ubuf, gbuf, mtot, mbuf,
-    z1s, z1r, z2s, z2r, m1s, m1r,
+    z1s, z1r, z2s, z2r, m1s, m1r, m2s, m2r,
 ):
     me = lax.axis_index("lon")
     my = lax.axis_index("lat")
@@ -569,8 +572,14 @@
 
     def merid_out(field, device, slot):
         return push(
-            msend.at[field], mrecv.at[field, slot],
+            msend.at[field, device], mrecv.at[field, slot],
             m1s.at[field, device], m1r.at[field, slot], "lat", device,
+        )
+
+    def merid_back(field, device, slot):
+        return push(
+            mret.at[field, device], mres.at[field, slot],
+            m2s.at[field, device], m2r.at[field, slot], "lat", device,
         )
 
     def merid_pass(field):
@@ -601,56 +610,64 @@
         mtot[field] = b_two
         coupling = mco_all[my, field, 0:1, :]
         for part, value in enumerate((b_one, a_one * coupling, b_two, a_two * coupling)):
-            msend[field, part] = value
+            for solver in range(N_LAT):
+                count = min(SPLIT, ZP - SPLIT * solver)
+                msend[field, solver, part, 0:count, :] = value[SPLIT * solver : SPLIT * solver + count]
+                if count < SPLIT:
+                    msend[field, solver, part, count:SPLIT, :] = jnp.zeros(
+                        (SPLIT - count, LANES), F32
+                    )
         over_lat(lambda device: merid_out(field, device, my).start())
-        mrecv[field, my] = msend[field]
+        mrecv[field, my] = msend[field, my]
 
     def merid_reduced(field):
         over_lat(lambda device: merid_out(field, 0, device).wait_recv())
         coef = lambda k, row: mco_all[k, field, row : row + 1, :]
-
-        def tile(step, _):
-            at = pl.ds(pl.multiple_of(step * 8, 8), 8)
-            part = lambda k, index: mrecv[field, k, index, at, :]
-
-            def solve_four(right_side):
-                mass = 1.0 + coef(0, 1)
-                reduced = right_side[0]
-                kept, inverses, values = [], [], [None] * N_LAT
-                for k in range(N_LAT):
-                    inverse = 1.0 / (mass + coef(k, 0))
-                    kept.append(reduced)
-                    inverses.append(inverse)
-                    if k + 1 < N_LAT:
-                        factor = coef(k, 0) * inverse
-                        mass = 1.0 + coef(k + 1, 1) + coef(k, 2) + factor * mass
-                        reduced = right_side[k + 1] + factor * reduced
-                values[-1] = kept[-1] * inverses[-1]
-                for k in range(N_LAT - 2, -1, -1):
-                    values[k] = (kept[k] + coef(k, 0) * values[k + 1]) * inverses[k]
-                return values
-
-            none = jnp.zeros((8, LANES), F32)
-            u = solve_four([part(k, 0) + (part(k - 1, 1) if k else none) for k in range(N_LAT)])
-            u = u + [none]
-            second = []
+        part = lambda k, index: mrecv[field, k, index]
+
+        def solve_four(right_side):
+            mass = 1.0 + coef(0, 1)
+            reduced = right_side[0]
+            kept, inverses, values = [], [], [None] * N_LAT
             for k in range(N_LAT):
-                value = part(k, 2) + coef(k, 3) * u[k] + coef(k, 4) * u[k + 1]
-                if k:
-                    value = value + part(k - 1, 3) + coef(k - 1, 4) * u[k - 1] + coef(k - 1, 5) * u[k]
-                second.append(value)
-            v = solve_four(second) + [none]
-            for k in range(N_LAT + 1):
-                mval[0, k, at, :] = u[k]
-                mval[1, k, at, :] = v[k]
-            return 0
-
-        lax.fori_loop(0, ZP // 8, tile, 0)
+                inverse = 1.0 / (mass + coef(k, 0))
+                kept.append(reduced)
+                inverses.append(inverse)
+                if k + 1 < N_LAT:
+                    factor = coef(k, 0) * inverse
+                    mass = 1.0 + coef(k + 1, 1) + coef(k, 2) + factor * mass
+                    reduced = right_side[k + 1] + factor * reduced
+            values[-1] = kept[-1] * inverses[-1]
+            for k in range(N_LAT - 2, -1, -1):
+                values[k] = (kept[k] + coef(k, 0) * values[k + 1]) * inverses[k]
+            return values
+
+        none = jnp.zeros((SPLIT, LANES), F32)
+        u = solve_four([part(k, 0) + (part(k - 1, 1) if k else none) for k in range(N_LAT)]) + [none]
+        second = []
+        for k in range(N_LAT):
+            value = part(k, 2) + coef(k, 3) * u[k] + coef(k, 4) * u[k + 1]
+            if k:
+                value = value + part(k - 1, 3) + coef(k - 1, 4) * u[k - 1] + coef(k - 1, 5) * u[k]
+            second.append(value)
+        v = solve_four(second) + [none]
+        for k in range(N_LAT):
+            for index, value in enumerate((u[k], u[k + 1], v[k], v[k + 1])):
+                mret[field, k, index] = value
+        over_lat(lambda device: merid_back(field, device, my).start())
+        mres[field, my] = mret[field, my]
+
+    def merid_receive(field):
+        over_lat(lambda device: merid_back(field, 0, device).wait_recv())
+        for index in range(4):
+            for solver in range(N_LAT):
+                count = min(SPLIT, ZP - SPLIT * solver)
+                mbuf[index, SPLIT * solver : SPLIT * solver + count, :] = mres[
+                    field, solver, index, 0:count, :
+                ]
         coupling = mco_all[my, field, 0:1, :]
-        mbuf[0] = mval[0, my]
-        mbuf[1] = mval[0, my + 1] * coupling
-        mbuf[2] = mval[1, my]
-        mbuf[3] = mval[1, my + 1] * coupling + mtot[field]
+        mbuf[1] = mbuf[1] * coupling
+        mbuf[3] = mbuf[3] * coupling + mtot[field]
 
     def merid_value(field, row):
         at = pl.ds(row, 1)
@@ -694,9 +711,11 @@
         ubuf[...] = both[:, :LANES]
         gbuf[...] = both[:, LANES:]
         merid_pass(field)
-
     for field in range(NF):
         merid_reduced(field)
+
+    for field in range(NF):
+        merid_receive(field)
         zonal_pass(1, field, lambda row, field=field: merid_value(field, row))
         zonal_send(1, field)
     pl.when(is_solver)(lambda: zonal_reduced(1))
@@ -714,6 +733,7 @@
 
     for field in range(NF):
         over_lat(lambda device, field=field: merid_out(field, device, my).wait_send())
+        over_lat(lambda device, field=field: merid_back(field, device, my).wait_send())
         for turn in range(2):
             others(
                 field,
@@ -737,11 +757,12 @@
         scratch_shapes=[
             vmem(2, NF, GROUPS, 8, LANES), vmem(2, N_LON, 8, LANES),
             vmem(2, N_LON, 8, LANES), vmem(2, NF, GROUPS, 8, LANES),
-            vmem(NF, 4, ZP, LANES), vmem(NF, N_LAT, 4, ZP, LANES), vmem(2, N_LAT + 1, ZP, LANES),
+            vmem(NF, N_LAT, 4, SPLIT, LANES), vmem(NF, N_LAT, 4, SPLIT, LANES),
+            vmem(NF, N_LAT, 4, SPLIT, LANES), vmem(NF, N_LAT, 4, SPLIT, LANES),
             vmem(ZP, LANES), vmem(NF, ZP, LANES), vmem(ZP, LANES), vmem(ZP, LANES),
             vmem(NF, ZP, LANES), vmem(4, ZP, LANES),
             dma((2, NF, GROUPS)), dma((2, N_LON)), dma((2, N_LON)), dma((2, NF, GROUPS)),
-            dma((NF, N_LAT)), dma((NF, N_LAT)),
+            dma((NF, N_LAT)), dma((NF, N_LAT)), dma((NF, N_LAT)), dma((NF, N_LAT)),
         ],
         compiler_params=pltpu.CompilerParams(
             collective_id=1, has_side_effects=True, vmem_limit_bytes=10 << 20

time: 123 us -> 116 us (0.943)
  Pallas kernels: 117 us -> 109 us
    pallas_call x1, Pallas kernels: 50.5 us -> 45.2 us  [solve(): pl.pallas_call(solve_kernel, out_shape=jax.ShapeDtypeStruct((NF, NLAT, ZP...]
    pallas_call x1, Pallas kernels: 16.6 us -> 15.2 us  [scatter(): pl.pallas_call(scatter_kernel, out_shape=(grid,) * GRIDS + (jax.ShapeDtyp...]
where the time goes in v5:
time: 116 us; the launch traced here: 115 us
  Pallas kernels  109 us (94%)
  local copies, waits for them, and re-layouts  3.43 us (3%)
  other arithmetic  1.66 us (1%)
    pallas_call x1, Pallas kernels, solve(): pl.pallas_call(solve_kernel, out_shape=jax.ShapeDtypeStruct((NF, NLAT, ZP...  45.2 us
    pallas_call x1, Pallas kernels, prepare(): pl.pallas_call(prepare_kernel, out_shape=(shape(RANKS, LANES), shape(80,...  20.4 us
    pallas_call x1, Pallas kernels, scatter(): pl.pallas_call(scatter_kernel, out_shape=(grid,) * GRIDS + (jax.ShapeDtyp...  15.2 us
    pallas_call x1, Pallas kernels, place(): pl.pallas_call(place_kernel, out_shape=jax.ShapeDtypeStruct((CAP, LANES),...  14.7 us
    pallas_call x1, Pallas kernels, pick(): pl.pallas_call(pick_kernel, out_shape=(jax.ShapeDtypeStruct((N_LON, 8, LA...  14 us
    unnamed x3, local copies, waits for them, and re-layouts  2.48 us

profile of v5, /device:TPU:1, one launch (start us, length us, event | category | flops | bytes accessed | tf_op | source)
XLA Modules:
  0.0 115.3 jit_solution(13993142506505995783)
XLA Ops:
  0.6 0.9 reshape.28
  1.6 0.8 pad_add_fusion.ints_ref.refs_9_
  2.4 0.8 select_maximum_fusion.floats_ref
  3.3 20.4 %prepare.1 = (f32[128,128]{1,0:T(8,128)S(1)}, f32[80,128]{1,0:T(8,128)S(1)}, f32[80,128]{1,0:T(8,128)S(1)}, f32[2,8,128]{2,1,0:T(8,128)S(1)}, f32[2,40,128]{2,1,...) custom-call(s32[200,128]{1,0:T(8,128)S(1)} %pad_add_fusion.ints_ref., ...), custom_call_target="tpu_custom_call" | custom-call | bytes 54000000 | tf_op jit(solution)/shard_map/prepare/pallas_call | solution.py:330
  23.7 0.0 copy-start
  23.7 1.9 %copy-done = f32[2,75,40,128]{3,2,1,0:T(8,128)S(1)} copy-done((f32[2,75,40,128]{3,2,1,0:T(8,128)S(1)}, f32[2,75,40,128]{3,2,1,0:T(8,128)}, u32[]{:S(2)}) %copy-start) | copy-done | bytes 3072024
  25.5 15.2 %scatter.1 = (f32[6400,128]{1,0:T(8,128)S(1)}, f32[6400,128]{1,0:T(8,128)S(1)}, f32[6400,128]{1,0:T(8,128)S(1)}, f32[6400,128]{1,0:T(8,128)S(1)}, f32[6400,128]{...) custom-call(s32[10240]{0:T(1024)S(1)} %bitcast.11, ...), custom_call_target="tpu_custom_call", output_to_operand_aliasing={{0}: (4, {}), {1}: (5, {}), {2}: (6, {}), {3}: (7, {}), {4}... | custom-call | bytes 43200000 | tf_op jit(solution)/shard_map/scatter/pallas_call | solution.py:413
  40.8 45.2 %solve.1 = f32[2,40,80,128]{3,2,1,0:T(8,128)S(1)} custom-call(f32[6400,128]{1,0:T(8,128)S(1)} %get-tuple-element.46.refs_0_, f32[6400,128]{1,0:T(8,128)S(1)} %get-tuple-element.47.refs_1_, f32[6400,128]{1,0:T(8,128)S(1)} %get-tuple-element.48.refs_2_, f32[6400,128]{1,0:T(8,128)S(1)} %get-tuple-element.49.refs_3_, f32[6400,128]{1,0:T(8,128)S(1)} %get-tuple-element.50.refs_4_, ...), custom_call_target="tpu_custom_call" | custom-call | bytes 144000000 | tf_op jit(solution)/shard_map/solve/pallas_call | solution.py:752
  86.0 14.0 %pick.1 = (f32[32,8,128]{2,1,0:T(8,128)S(1)}, f32[2,75,40,128]{3,2,1,0:T(8,128)}) custom-call(s32[10240]{0:T(1024)S(1)} %bitcast.12, s32[200,128]{1,0:T(8,128)S(1)} %pad_add_fusion.ints_ref.refs_9_, f32[6400,128]{1,0:T(8,128)S(1)} %bitcast.9), custom_call_target="tpu_custom_call" | custom-call | bytes 50400000 | tf_op jit(solution)/shard_map/pick/pallas_call | solution.py:823
  99.9 14.7 %place.1 = f32[80,128]{1,0:T(8,128)S(1)} custom-call(f32[32,8,128]{2,1,0:T(8,128)S(1)} %get-tuple-element.69.tile_out, s32[200,128]{1,0:T(8,128)S(1)} %pad_add_fusion.ints_ref.refs_9_), custom_call_target="tpu_custom_call" | custom-call | bytes 54000000 | tf_op jit(solution)/shard_map/place/pallas_call | solution.py:886
  114.7 0.6 copy.27
  (1 shorter events, 0.0 us)
Async XLA Ops:
  23.7 1.9 %copy-start = (f32[2,75,40,128]{3,2,1,0:T(8,128)S(1)}, f32[2,75,40,128]{3,2,1,0:T(8,128)}, u32[]{:S(2)}) copy-start(f32[2,75,40,128]{3,2,1,0:T(8,128)} %norm_ref.1) | copy-start | bytes 9216004

commit v6 on v5

--- a/solution.py
+++ b/solution.py
@@ -194,10 +194,11 @@
     return rows if field == 0 else pltpu.roll(rows, LANES - field * NLAT, 1)
 
 
-def gather_lines(table_ref, count, high, low, base):
+def gather_lines(table_ref, count, high, low, beside):
     def step(row, acc):
+        beside(row)
         line = jnp.broadcast_to(table_ref[pl.ds(row, 1), :], (ZP, LANES))
-        return jnp.where(high == row + base, lane_pick(line, low), acc)
+        return jnp.where(high == row, lane_pick(line, low), acc)
 
     return lax.fori_loop(0, count, step, jnp.zeros((ZP, LANES), F32), unroll=8)
 
@@ -235,30 +236,38 @@
 
 
 def prepare_kernel(
-    ints_ref, floats_ref, north_ref,
+    ints_ref, floats_ref, north_ref, norm_ref,
     out_ref, zs_ref, zr_ref, zco_out, ms_ref, mr_ref, mss_ref, mrr_ref, mco_out, vert_ref,
-    alpha, gamma, minv, sums_ref, row_ref, *rest
+    alpha, gamma, minv, sums_ref, row_ref, norm_buf, *rest
 ):
     grids, rest = rest[:GRIDS], rest[GRIDS:]
     prepare_body(
-        ints_ref, floats_ref, north_ref, out_ref, zs_ref, zr_ref, zco_out, ms_ref, mr_ref, mss_ref,
-        mrr_ref, mco_out, vert_ref, alpha, gamma, minv, sums_ref, row_ref, grids, *rest,
+        ints_ref, floats_ref, north_ref, norm_ref, out_ref, zs_ref, zr_ref, zco_out, ms_ref, mr_ref, mss_ref,
+        mrr_ref, mco_out, vert_ref, alpha, gamma, minv, sums_ref, row_ref, norm_buf,
+        grids, *rest,
     )
 
 
 def prepare_body(
-    ints_ref, floats_ref, north_ref,
+    ints_ref, floats_ref, north_ref, norm_ref,
     out_ref, zs_ref, zr_ref, zco_out, ms_ref, mr_ref, mss_ref, mrr_ref, mco_out, vert_ref,
-    alpha, gamma, minv, sums_ref, row_ref, grids,
+    alpha, gamma, minv, sums_ref, row_ref, norm_buf, grids,
     iw_ref, st_ref, rt_ref, miw_ref, prod_ref,
     tile_out, tile_in, rows_out, rows_in, zco_ref, zco_all, mco_ref, mco_all,
-    o1s, o1r, o2s, o2r, zco_s, zco_r, mco_s, mco_r,
+    o1s, o1r, o2s, o2r, zco_s, zco_r, mco_s, mco_r, norm_sem,
 ):
     me = lax.axis_index("lon")
     my = lax.axis_index("lat")
     greet()
     index = ints_ref[0:CAP, :]
-    picked = gather_lines(floats_ref, CAP, index >> 7, index & 127, 0)
+
+    def norm_copy(line):
+        field, row = line // NLAT, line % NLAT
+        pltpu.make_async_copy(
+            norm_ref.at[field, :, row, :], norm_buf.at[field, row, pl.ds(0, NZ), :], norm_sem
+        ).start()
+
+    picked = gather_lines(floats_ref, CAP, index >> 7, index & 127, norm_copy)
     picked = jnp.transpose(
         jnp.concatenate([picked, jnp.zeros((LANES - CAP, LANES), F32)], axis=0)
     )
@@ -318,12 +327,14 @@
     zonal_factor(zco_all, alpha, gamma, minv)
     over_lat(lambda device: mco_copy(0, device).wait_recv())
     mco_out[...] = mco_all[...]
+    whole = norm_buf.at[:, :, pl.ds(0, NZ), :]
+    pltpu.make_async_copy(whole, whole, norm_sem).wait()
     sent()
     over_lon(lambda device: zco_copy(device, me).wait_send())
     over_lat(lambda device: mco_copy(device, my).wait_send())
 
 
-def prepare(ints, floats, north):
+def prepare(ints, floats, north, norm):
     shape = lambda *dims: jax.ShapeDtypeStruct(dims, F32)
     vmem = lambda *dims: pltpu.VMEM(dims, F32)
     dma = pltpu.SemaphoreType.DMA
@@ -337,10 +348,11 @@
             shape(NF, 5, N_LON, LANES), shape(NF, 5, N_LON, LANES), shape(NF, N_LON, LANES),
             jax.ShapeDtypeStruct((2 * LANES, 2 * LANES), BF16),
             jax.ShapeDtypeStruct((CAP, LANES), jnp.int32),
+            shape(NF, NLAT, ZP, LANES),
         )
         + (shape(ROWS, LANES),) * GRIDS,
-        in_specs=[VMEM_SPEC] * 3,
-        out_specs=(VMEM_SPEC,) * (15 + GRIDS),
+        in_specs=[VMEM_SPEC] * 3 + [ANY_SPEC],
+        out_specs=(VMEM_SPEC,) * (16 + GRIDS),
         scratch_shapes=[
             vmem(LANES, LANES), vmem(LANES, LANES), vmem(LANES, LANES), vmem(NF, NLAT, LANES),
             vmem(ZP, LANES),
@@ -348,37 +360,19 @@
             vmem(N_LAT, N_LON, LANES), vmem(N_LAT, N_LON, LANES),
             vmem(8, LANES), vmem(N_LON, 8, LANES), vmem(NF, 8, LANES), vmem(N_LAT, NF, 8, LANES),
             dma((N_LON,)), dma((N_LON,)), dma((N_LAT,)), dma((N_LAT,)),
-            dma((N_LON,)), dma((N_LON,)), dma((N_LAT,)), dma((N_LAT,)),
+            dma((N_LON,)), dma((N_LON,)), dma((N_LAT,)), dma((N_LAT,)), dma,
         ],
         compiler_params=pltpu.CompilerParams(
             collective_id=0, has_side_effects=True, vmem_limit_bytes=6 << 20
         ),
         cost_estimate=cost(15),
         name="prepare",
-    )(ints, floats, north)
-
-
-def scatter_kernel(rows_ref, ints_ref, in_ref, norm_ref, *refs):
+    )(ints, floats, north, norm)
+
+
+def scatter_kernel(rows_ref, ints_ref, in_ref, *refs):
     grids = refs[GRIDS : 2 * GRIDS]
-    norm_buf, norm_sem, value_ref, even_ref, odd_ref = refs[2 * GRIDS :]
-
-    def norm_copy(field, row):
-        return pltpu.make_async_copy(
-            norm_ref.at[field, :, row, :],
-            norm_buf.at[field, row, pl.ds(0, NZ), :],
-            norm_sem.at[field, row],
-        )
-
-    def over_rows(action):
-        for field in range(NF):
-
-            def body(row, _, field=field):
-                action(norm_copy(field, row))
-                return 0
-
-            lax.fori_loop(0, NLAT, body, 0)
-
-    over_rows(lambda copy: copy.start())
+    value_ref, even_ref, odd_ref = refs[2 * GRIDS :]
     value_ref[...] = jnp.transpose(in_ref[...])
     iota = lane_iota(CAP)
 
@@ -405,25 +399,23 @@
         return 0
 
     lax.fori_loop(0, RANKS // 2, senders, 0)
-    over_rows(lambda copy: copy.wait())
-
-
-def scatter(rows, ints, incoming, norm, grids):
+
+
+def scatter(rows, ints, incoming, grids):
     grid = jax.ShapeDtypeStruct((ROWS, LANES), F32)
     return pl.pallas_call(
         scatter_kernel,
-        out_shape=(grid,) * GRIDS + (jax.ShapeDtypeStruct((NF, NLAT, ZP, LANES), F32),),
-        in_specs=[SMEM_SPEC] + [VMEM_SPEC] * 2 + [ANY_SPEC] + [VMEM_SPEC] * GRIDS,
-        out_specs=(VMEM_SPEC,) * (GRIDS + 1),
-        input_output_aliases={4 + index: index for index in range(GRIDS)},
+        out_shape=(grid,) * GRIDS,
+        in_specs=[SMEM_SPEC] + [VMEM_SPEC] * (2 + GRIDS),
+        out_specs=(VMEM_SPEC,) * GRIDS,
+        input_output_aliases={3 + index: index for index in range(GRIDS)},
         scratch_shapes=[
-            pltpu.SemaphoreType.DMA((NF, NLAT)),
             pltpu.VMEM((LANES, LANES), F32), pltpu.VMEM((CAP, LANES), F32), pltpu.VMEM((CAP, LANES), F32),
         ],
         compiler_params=pltpu.CompilerParams(vmem_limit_bytes=6 << 20),
         cost_estimate=cost(12),
         name="scatter",
-    )(rows, ints, incoming, norm, *grids)
+    )(rows, ints, incoming, *grids)
 
 
 def solve_kernel(*refs):
@@ -772,41 +764,28 @@
     )(*grids, norm, ints, *coefs)
 
 
-def pick_kernel(rows_ref, ints_ref, x_ref, out_ref, inc_ref, inc_sem, *copies):
+def pick_kernel(rows_ref, ints_ref, x_ref, out_ref, inc_ref, inc_sem):
     iota = lane_iota(8)
-
-    def inc_copy(field, row):
-        return pltpu.make_async_copy(
-            x_ref.at[pl.ds(pl.multiple_of((field * NLAT + row) * ZP, ZP), NZ), :],
-            inc_ref.at[field, :, row, :],
-            inc_sem.at[field, row],
-        )
-
-    def over_rows(action):
-        for field in range(NF):
-
-            def body(row, _, field=field):
-                action(inc_copy(field, row))
-                return 0
-
-            lax.fori_loop(0, NLAT, body, 0)
-
-    over_rows(lambda copy: copy.start())
-    group = len(copies)
+    group = 16
+    for field in range(NF):
+
+        def begin(row, _, field=field):
+            at = pl.ds(pl.multiple_of((field * NLAT + row) * ZP, ZP), NZ)
+            pltpu.make_async_copy(x_ref.at[at, :], inc_ref.at[field, :, row, :], inc_sem).start()
+            return 0
+
+        lax.fori_loop(0, NLAT, begin, 0)
 
     def senders(step, acc):
         acc = list(acc)
         for part in range(group):
             q = step * group + part
-            for k in range(CAP):
-                copies[part][k : k + 1, :] = x_ref[pl.ds(rows_ref[k * RANKS + q], 1), :]
-        for part in range(group):
-            q = step * group + part
             for tile in range(CAP // 8):
-                at = slice(8 * tile, 8 * tile + 8)
-                found = lane_pick(
-                    copies[part][at, :], ints_ref[CAP + 8 * tile : CAP + 8 * tile + 8, :] & 127
-                )
+                lines = [
+                    x_ref[pl.ds(rows_ref[k * RANKS + q], 1), :] for k in range(8 * tile, 8 * tile + 8)
+                ]
+                lane = ints_ref[CAP + 8 * tile : CAP + 8 * tile + 8, :] & 127
+                found = lane_pick(jnp.concatenate(lines, axis=0), lane)
                 acc[tile] = jnp.where(iota == q, found, acc[tile])
         return tuple(acc)
 
@@ -816,7 +795,7 @@
     for device in range(N_LON):
         out_ref[device, 0:4, :] = whole[4 * device : 4 * device + 4]
         out_ref[device, 4:8, :] = jnp.zeros((4, LANES), F32)
-    over_rows(lambda copy: copy.wait())
+    pltpu.make_async_copy(inc_ref, inc_ref, inc_sem).wait()
 
 
 def pick(rows, ints, increment):
@@ -828,7 +807,7 @@
         ),
         in_specs=[SMEM_SPEC, VMEM_SPEC, VMEM_SPEC],
         out_specs=(VMEM_SPEC, ANY_SPEC),
-        scratch_shapes=[pltpu.SemaphoreType.DMA((NF, NLAT))] + [pltpu.VMEM((CAP, LANES), F32)] * 16,
+        scratch_shapes=[pltpu.SemaphoreType.DMA],
         compiler_params=pltpu.CompilerParams(vmem_limit_bytes=8 << 20),
         cost_estimate=cost(14),
         name="pick",
@@ -921,9 +900,9 @@
         ],
         axis=0,
     )
-    made = prepare(ints, floats, north)
-    incoming, coefs, rows, grids = made[0], made[1:14], made[14].reshape(-1), made[15:]
-    *grids, norm = scatter(rows, ints, incoming, norm_scale, grids)
+    made = prepare(ints, floats, north, norm_scale)
+    incoming, coefs, rows, norm = made[0], made[1:14], made[14].reshape(-1), made[15]
+    grids = scatter(rows, ints, incoming, made[16:])
     whole = solve(grids, norm, ints, coefs)
     tiles, increment = pick(rows, ints, whole)
     return increment, place(tiles, ints).reshape(-1)

time: 116 us -> 112 us (0.966)
  Pallas kernels: 109 us -> 106 us
    pallas_call x1, Pallas kernels: 20.4 us -> 24.7 us  [prepare(): pl.pallas_call(prepare_kernel, out_shape=(shape(RANKS, LANES), shape(80,...]
    pallas_call x1, Pallas kernels: 15.2 us -> 11 us  [scatter(): pl.pallas_call(scatter_kernel, out_shape=(grid,) * GRIDS, in_specs=[SMEM_...]
    pallas_call x1, Pallas kernels: 14 us -> 10.7 us  [pick(): pl.pallas_call(pick_kernel, out_shape=(jax.ShapeDtypeStruct((N_LON, 8, LA...]
where the time goes in v6:
time: 112 us
  Pallas kernels  106 us (95%)
  local copies, waits for them, and re-layouts  3.43 us (3%)
  other arithmetic  1.66 us (1%)
    pallas_call x1, Pallas kernels, solve(): pl.pallas_call(solve_kernel, out_shape=jax.ShapeDtypeStruct((NF, NLAT, ZP...  44.6 us
    pallas_call x1, Pallas kernels, prepare(): pl.pallas_call(prepare_kernel, out_shape=(shape(RANKS, LANES), shape(80,...  24.7 us
    pallas_call x1, Pallas kernels, place(): pl.pallas_call(place_kernel, out_shape=jax.ShapeDtypeStruct((CAP, LANES),...  14.9 us
    pallas_call x1, Pallas kernels, scatter(): pl.pallas_call(scatter_kernel, out_shape=(grid,) * GRIDS, in_specs=[SMEM_...  11 us
    pallas_call x1, Pallas kernels, pick(): pl.pallas_call(pick_kernel, out_shape=(jax.ShapeDtypeStruct((N_LON, 8, LA...  10.7 us
    unnamed x3, local copies, waits for them, and re-layouts  2.48 us

profile of v6, /device:TPU:1, one launch (start us, length us, event | category | flops | bytes accessed | tf_op | source)
XLA Modules:
  0.0 111.6 jit_solution(8637390062071970542)
XLA Ops:
  0.6 0.9 reshape.28
  1.6 0.8 pad_add_fusion.ints_ref.refs_9_
  2.4 0.8 select_maximum_fusion.floats_ref
  3.3 0.0 copy-start
  3.3 1.9 %copy-done = f32[2,75,40,128]{3,2,1,0:T(8,128)S(1)} copy-done((f32[2,75,40,128]{3,2,1,0:T(8,128)S(1)}, f32[2,75,40,128]{3,2,1,0:T(8,128)}, u32[]{:S(2)}) %copy-start) | copy-done | bytes 3072024
  5.1 24.7 %prepare.1 = (f32[128,128]{1,0:T(8,128)S(1)}, f32[80,128]{1,0:T(8,128)S(1)}, f32[80,128]{1,0:T(8,128)S(1)}, f32[2,8,128]{2,1,0:T(8,128)S(1)}, f32[2,40,128]{2,1,...) custom-call(s32[200,128]{1,0:T(8,128)S(1)} %pad_add_fusion.ints_ref., ...), custom_call_target="tpu_custom_call" | custom-call | bytes 54000000 | tf_op jit(solution)/shard_map/prepare/pallas_call | solution.py:341
  29.8 11.0 %scatter.1 = (f32[6400,128]{1,0:T(8,128)S(1)}, f32[6400,128]{1,0:T(8,128)S(1)}, f32[6400,128]{1,0:T(8,128)S(1)}, f32[6400,128]{1,0:T(8,128)S(1)}, f32[6400,128]{...) custom-call(s32[10240]{0:T(1024)S(1)} %bitcast.10, ...), custom_call_target="tpu_custom_call", output_to_operand_aliasing={{0}: (3, {}), {1}: (4, {}), {2}: (5, {}), {3}: (6, {}), {4}... | custom-call | bytes 43200000 | tf_op jit(solution)/shard_map/scatter/pallas_call | solution.py:406
  40.8 44.6 %solve.1 = f32[2,40,80,128]{3,2,1,0:T(8,128)S(1)} custom-call(f32[6400,128]{1,0:T(8,128)S(1)} %get-tuple-element.46.refs_0_, f32[6400,128]{1,0:T(8,128)S(1)} %get-tuple-element.47.refs_1_, f32[6400,128]{1,0:T(8,128)S(1)} %get-tuple-element.48.refs_2_, f32[6400,128]{1,0:T(8,128)S(1)} %get-tuple-element.49.refs_3_, f32[6400,128]{1,0:T(8,128)S(1)} %get-tuple-element.50.refs_4_, ...), custom_call_target="tpu_custom_call" | custom-call | bytes 144000000 | tf_op jit(solution)/shard_map/solve/pallas_call | solution.py:744
  85.4 10.7 %pick.1 = (f32[32,8,128]{2,1,0:T(8,128)S(1)}, f32[2,75,40,128]{3,2,1,0:T(8,128)}) custom-call(s32[10240]{0:T(1024)S(1)} %bitcast.11, s32[200,128]{1,0:T(8,128)S(1)} %pad_add_fusion.ints_ref.refs_9_, f32[6400,128]{1,0:T(8,128)S(1)} %bitcast.9), custom_call_target="tpu_custom_call" | custom-call | bytes 50400000 | tf_op jit(solution)/shard_map/pick/pallas_call | solution.py:802
  96.1 14.9 %place.1 = f32[80,128]{1,0:T(8,128)S(1)} custom-call(f32[32,8,128]{2,1,0:T(8,128)S(1)} %get-tuple-element.69.tile_out, s32[200,128]{1,0:T(8,128)S(1)} %pad_add_fusion.ints_ref.refs_9_), custom_call_target="tpu_custom_call" | custom-call | bytes 54000000 | tf_op jit(solution)/shard_map/place/pallas_call | solution.py:865
  111.0 0.6 copy.27
  (1 shorter events, 0.0 us)
Async XLA Ops:
  3.3 1.9 %copy-start = (f32[2,75,40,128]{3,2,1,0:T(8,128)S(1)}, f32[2,75,40,128]{3,2,1,0:T(8,128)}, u32[]{:S(2)}) copy-start(f32[2,75,40,128]{3,2,1,0:T(8,128)} %norm_ref.1) | copy-start | bytes 9216004

commit v7 on v6

--- a/solution.py
+++ b/solution.py
@@ -236,38 +236,36 @@
 
 
 def prepare_kernel(
-    ints_ref, floats_ref, north_ref, norm_ref,
+    ints_ref, floats_ref, north_ref,
     out_ref, zs_ref, zr_ref, zco_out, ms_ref, mr_ref, mss_ref, mrr_ref, mco_out, vert_ref,
-    alpha, gamma, minv, sums_ref, row_ref, norm_buf, *rest
+    alpha, gamma, minv, sums_ref, row_ref, *rest
 ):
     grids, rest = rest[:GRIDS], rest[GRIDS:]
     prepare_body(
-        ints_ref, floats_ref, north_ref, norm_ref, out_ref, zs_ref, zr_ref, zco_out, ms_ref, mr_ref, mss_ref,
-        mrr_ref, mco_out, vert_ref, alpha, gamma, minv, sums_ref, row_ref, norm_buf,
-        grids, *rest,
+        ints_ref, floats_ref, north_ref, out_ref, zs_ref, zr_ref, zco_out, ms_ref, mr_ref, mss_ref,
+        mrr_ref, mco_out, vert_ref, alpha, gamma, minv, sums_ref, row_ref, grids, *rest,
     )
 
 
 def prepare_body(
-    ints_ref, floats_ref, north_ref, norm_ref,
+    ints_ref, floats_ref, north_ref,
     out_ref, zs_ref, zr_ref, zco_out, ms_ref, mr_ref, mss_ref, mrr_ref, mco_out, vert_ref,
-    alpha, gamma, minv, sums_ref, row_ref, norm_buf, grids,
+    alpha, gamma, minv, sums_ref, row_ref, grids,
     iw_ref, st_ref, rt_ref, miw_ref, prod_ref,
     tile_out, tile_in, rows_out, rows_in, zco_ref, zco_all, mco_ref, mco_all,
-    o1s, o1r, o2s, o2r, zco_s, zco_r, mco_s, mco_r, norm_sem,
+    o1s, o1r, o2s, o2r, zco_s, zco_r, mco_s, mco_r,
 ):
     me = lax.axis_index("lon")
     my = lax.axis_index("lat")
     greet()
     index = ints_ref[0:CAP, :]
 
-    def norm_copy(line):
-        field, row = line // NLAT, line % NLAT
-        pltpu.make_async_copy(
-            norm_ref.at[field, :, row, :], norm_buf.at[field, row, pl.ds(0, NZ), :], norm_sem
-        ).start()
-
-    picked = gather_lines(floats_ref, CAP, index >> 7, index & 127, norm_copy)
+    def clear(line):
+        at = pl.ds(pl.multiple_of(line * ZP, ZP), ZP)
+        for grid in grids:
+            grid[at, :] = jnp.zeros((ZP, LANES), F32)
+
+    picked = gather_lines(floats_ref, CAP, index >> 7, index & 127, clear)
     picked = jnp.transpose(
         jnp.concatenate([picked, jnp.zeros((LANES - CAP, LANES), F32)], axis=0)
     )
@@ -313,13 +311,6 @@
     source = lax.broadcasted_iota(jnp.int32, (2 * LANES, 2 * LANES), 0) & 127
     target = lax.broadcasted_iota(jnp.int32, (2 * LANES, 2 * LANES), 1)
     sums_ref[...] = jnp.where(source <= target, 1.0, 0.0).astype(BF16)
-    def clear(step, _):
-        at = pl.ds(pl.multiple_of(step * 64, 64), 64)
-        for grid in grids:
-            grid[at, :] = jnp.zeros((64, LANES), F32)
-        return 0
-
-    lax.fori_loop(0, ROWS // 64, clear, 0)
     end()
     for lat in range(N_LAT):
         out_ref[N_LON * lat : N_LON * lat + N_LON, :] = rows_in[lat]
@@ -327,14 +318,12 @@
     zonal_factor(zco_all, alpha, gamma, minv)
     over_lat(lambda device: mco_copy(0, device).wait_recv())
     mco_out[...] = mco_all[...]
-    whole = norm_buf.at[:, :, pl.ds(0, NZ), :]
-    pltpu.make_async_copy(whole, whole, norm_sem).wait()
     sent()
     over_lon(lambda device: zco_copy(device, me).wait_send())
     over_lat(lambda device: mco_copy(device, my).wait_send())
 
 
-def prepare(ints, floats, north, norm):
+def prepare(ints, floats, north):
     shape = lambda *dims: jax.ShapeDtypeStruct(dims, F32)
     vmem = lambda *dims: pltpu.VMEM(dims, F32)
     dma = pltpu.SemaphoreType.DMA
@@ -348,11 +337,10 @@
             shape(NF, 5, N_LON, LANES), shape(NF, 5, N_LON, LANES), shape(NF, N_LON, LANES),
             jax.ShapeDtypeStruct((2 * LANES, 2 * LANES), BF16),
             jax.ShapeDtypeStruct((CAP, LANES), jnp.int32),
-            shape(NF, NLAT, ZP, LANES),
         )
         + (shape(ROWS, LANES),) * GRIDS,
-        in_specs=[VMEM_SPEC] * 3 + [ANY_SPEC],
-        out_specs=(VMEM_SPEC,) * (16 + GRIDS),
+        in_specs=[VMEM_SPEC] * 3,
+        out_specs=(VMEM_SPEC,) * (15 + GRIDS),
         scratch_shapes=[
             vmem(LANES, LANES), vmem(LANES, LANES), vmem(LANES, LANES), vmem(NF, NLAT, LANES),
             vmem(ZP, LANES),
@@ -360,14 +348,14 @@
             vmem(N_LAT, N_LON, LANES), vmem(N_LAT, N_LON, LANES),
             vmem(8, LANES), vmem(N_LON, 8, LANES), vmem(NF, 8, LANES), vmem(N_LAT, NF, 8, LANES),
             dma((N_LON,)), dma((N_LON,)), dma((N_LAT,)), dma((N_LAT,)),
-            dma((N_LON,)), dma((N_LON,)), dma((N_LAT,)), dma((N_LAT,)), dma,
+            dma((N_LON,)), dma((N_LON,)), dma((N_LAT,)), dma((N_LAT,)),
         ],
         compiler_params=pltpu.CompilerParams(
             collective_id=0, has_side_effects=True, vmem_limit_bytes=6 << 20
         ),
         cost_estimate=cost(15),
         name="prepare",
-    )(ints, floats, north, norm)
+    )(ints, floats, north)
 
 
 def scatter_kernel(rows_ref, ints_ref, in_ref, *refs):
@@ -675,7 +663,8 @@
 
     def scale(field, row):
         wet = level < ints_ref[pl.ds(DEPTH_AT + row, 1), :]
-        return jnp.where(wet, norm_ref[field, row], 0.0)
+        line = jnp.concatenate([norm_ref[field, row], jnp.zeros((ZP - NZ, LANES), F32)], axis=0)
+        return jnp.where(wet, line, 0.0)
 
     def scaled_grid(field):
         def load(row):
@@ -900,9 +889,10 @@
         ],
         axis=0,
     )
-    made = prepare(ints, floats, north, norm_scale)
-    incoming, coefs, rows, norm = made[0], made[1:14], made[14].reshape(-1), made[15]
-    grids = scatter(rows, ints, incoming, made[16:])
+    made = prepare(ints, floats, north)
+    incoming, coefs, rows = made[0], made[1:14], made[14].reshape(-1)
+    grids = scatter(rows, ints, incoming, made[15:])
+    norm = jnp.transpose(norm_scale, (0, 2, 1, 3))
     whole = solve(grids, norm, ints, coefs)
     tiles, increment = pick(rows, ints, whole)
     return increment, place(tiles, ints).reshape(-1)

time: 112 us -> 107 us (0.955)
  Pallas kernels: 106 us -> 102 us
  local copies, waits for them, and re-layouts: 3.43 us -> 2.18 us
    pallas_call x1, Pallas kernels: 24.7 us -> 21.3 us  [prepare(): pl.pallas_call(prepare_kernel, out_shape=(shape(RANKS, LANES), shape(80,...]
    unnamed x3 -> x4, local copies, waits for them, and re-layouts: 2.48 us -> 1.24 us
where the time goes in v7:
time: 107 us
  Pallas kernels  102 us (95%)
  local copies, waits for them, and re-layouts  2.18 us (2%)
  other arithmetic  1.66 us (2%)
    pallas_call x1, Pallas kernels, solve(): pl.pallas_call(solve_kernel, out_shape=jax.ShapeDtypeStruct((NF, NLAT, ZP...  44.7 us
    pallas_call x1, Pallas kernels, prepare(): pl.pallas_call(prepare_kernel, out_shape=(shape(RANKS, LANES), shape(80,...  21.3 us
    pallas_call x1, Pallas kernels, place(): pl.pallas_call(place_kernel, out_shape=jax.ShapeDtypeStruct((CAP, LANES),...  14.8 us
    pallas_call x1, Pallas kernels, scatter(): pl.pallas_call(scatter_kernel, out_shape=(grid,) * GRIDS, in_specs=[SMEM_...  11 us
    pallas_call x1, Pallas kernels, pick(): pl.pallas_call(pick_kernel, out_shape=(jax.ShapeDtypeStruct((N_LON, 8, LA...  10.7 us

profile of v7, /device:TPU:1, one launch (start us, length us, event | category | flops | bytes accessed | tf_op | source)
XLA Modules:
  0.0 107.0 jit_solution(8598388064903549915)
XLA Ops:
  0.6 0.8 pad_add_fusion.ints_ref.refs_9_
  1.5 0.9 reshape.28
  2.4 0.8 select_maximum_fusion.floats_ref
  3.3 21.3 %prepare.1 = (f32[128,128]{1,0:T(8,128)S(1)}, f32[80,128]{1,0:T(8,128)S(1)}, f32[80,128]{1,0:T(8,128)S(1)}, f32[2,8,128]{2,1,0:T(8,128)S(1)}, f32[2,40,128]{2,1,...) custom-call(s32[200,128]{1,0:T(8,128)S(1)} %pad_add_fusion.ints_ref., ...), custom_call_target="tpu_custom_call" | custom-call | bytes 54000000 | tf_op jit(solution)/shard_map/prepare/pallas_call | solution.py:330
  24.6 0.0 copy-start
  24.6 11.0 %scatter.1 = (f32[6400,128]{1,0:T(8,128)S(1)}, f32[6400,128]{1,0:T(8,128)S(1)}, f32[6400,128]{1,0:T(8,128)S(1)}, f32[6400,128]{1,0:T(8,128)S(1)}, f32[6400,128]{...) custom-call(s32[10240]{0:T(1024)S(1)} %bitcast.14, ...), custom_call_target="tpu_custom_call", output_to_operand_aliasing={{0}: (3, {}), {1}: (4, {}), {2}: (5, {}), {3}: (6, {}), {4}... | custom-call | bytes 43200000 | tf_op jit(solution)/shard_map/scatter/pallas_call | solution.py:394
  35.6 0.0 copy-done
  35.6 0.6 copy.20
  36.2 44.7 %solve.1 = f32[2,40,80,128]{3,2,1,0:T(8,128)S(1)} custom-call(f32[6400,128]{1,0:T(8,128)S(1)} %get-tuple-element.45.refs_0_, f32[6400,128]{1,0:T(8,128)S(1)} %get-tuple-element.46.refs_1_, f32[6400,128]{1,0:T(8,128)S(1)} %get-tuple-element.47.refs_2_, f32[6400,128]{1,0:T(8,128)S(1)} %get-tuple-element.48.refs_3_, f32[6400,128]{1,0:T(8,128)S(1)} %get-tuple-element.49.refs_4_, ...), custom_call_target="tpu_custom_call" | custom-call | bytes 144000000 | tf_op jit(solution)/shard_map/solve/pallas_call | solution.py:733
  80.9 10.7 %pick.1 = (f32[32,8,128]{2,1,0:T(8,128)S(1)}, f32[2,75,40,128]{3,2,1,0:T(8,128)}) custom-call(s32[10240]{0:T(1024)S(1)} %bitcast.15, s32[200,128]{1,0:T(8,128)S(1)} %pad_add_fusion.ints_ref.refs_9_, f32[6400,128]{1,0:T(8,128)S(1)} %bitcast.13), custom_call_target="tpu_custom_call" | custom-call | bytes 50400000 | tf_op jit(solution)/shard_map/pick/pallas_call | solution.py:791
  91.6 14.8 %place.1 = f32[80,128]{1,0:T(8,128)S(1)} custom-call(f32[32,8,128]{2,1,0:T(8,128)S(1)} %get-tuple-element.67.tile_out, s32[200,128]{1,0:T(8,128)S(1)} %pad_add_fusion.ints_ref.refs_9_), custom_call_target="tpu_custom_call" | custom-call | bytes 54000000 | tf_op jit(solution)/shard_map/place/pallas_call | solution.py:854
  106.4 0.6 copy.30
  (1 shorter events, 0.0 us)
Async XLA Ops:
  24.6 11.0 %copy-start = (f32[2,75,40,128]{3,2,1,0:T(8,128)S(1)}, f32[2,75,40,128]{3,2,1,0:T(8,128)}, u32[]{:S(2)}) copy-start(f32[2,75,40,128]{3,2,1,0:T(8,128)} %param.15) | copy-start | bytes 9216004

commit v8 on v7

--- a/solution.py
+++ b/solution.py
@@ -64,6 +64,12 @@
 
 def over_lon(action):
     over("lon", N_LON, action)
+
+
+def each_lon(action):
+    mine = lax.axis_index("lon")
+    for step in range(1, N_LON):
+        action((mine + step) % N_LON)
 
 
 def over_lat(action):
@@ -215,11 +221,11 @@
     )
 
     def begin():
-        over_lon(lambda device: first(device, me).start())
+        each_lon(lambda device: first(device, me).start())
         tile_in[me] = tile_out[me]
 
     def middle():
-        over_lon(lambda device: first(0, device).wait_recv())
+        each_lon(lambda device: first(0, device).wait_recv())
         for lat in range(N_LAT):
             rows_out[lat] = tile_in[:, lat, :]
         over_lat(lambda device: second(device, my).start())
@@ -270,8 +276,7 @@
         jnp.concatenate([picked, jnp.zeros((LANES - CAP, LANES), F32)], axis=0)
     )
     for device in range(N_LON):
-        tile_out[device, 0:4, :] = picked[4 * device : 4 * device + 4]
-        tile_out[device, 4:8, :] = jnp.zeros((4, LANES), F32)
+        tile_out[device] = picked[4 * device : 4 * device + 4]
 
     begin, middle, end, sent = two_phase(tile_out, tile_in, rows_out, rows_in, (o1s, o1r, o2s, o2r))
     zco_copy = lambda device, slot: push(
@@ -344,7 +349,7 @@
         scratch_shapes=[
             vmem(LANES, LANES), vmem(LANES, LANES), vmem(LANES, LANES), vmem(NF, NLAT, LANES),
             vmem(ZP, LANES),
-            vmem(N_LON, 8, LANES), vmem(N_LON, 8, LANES),
+            vmem(N_LON, 4, LANES), vmem(N_LON, 4, LANES),
             vmem(N_LAT, N_LON, LANES), vmem(N_LAT, N_LON, LANES),
             vmem(8, LANES), vmem(N_LON, 8, LANES), vmem(NF, 8, LANES), vmem(N_LAT, NF, 8, LANES),
             dma((N_LON,)), dma((N_LON,)), dma((N_LAT,)), dma((N_LAT,)),
@@ -488,7 +493,7 @@
 
     def zonal_reduced(turn):
         mine = me % half
-        over_lon(lambda device: zonal_out(turn, 0, 0, device).wait_recv())
+        each_lon(lambda device: zonal_out(turn, 0, 0, device).wait_recv())
         right_side = [
             zrecv[turn, k] + pltpu.roll(zrecv[turn, (k - 1) % N_LON], HALF, 1) for k in range(N_LON)
         ]
@@ -505,7 +510,7 @@
             zret[turn, k] = jnp.where(
                 iota[0:8] < HALF, values[k], pltpu.roll(values[(k + 1) % N_LON], HALF, 1)
             )
-        over_lon(lambda device: zonal_back(turn, device, my_field, mine).start())
+        each_lon(lambda device: zonal_back(turn, device, my_field, mine).start())
         zres[turn, my_field, mine] = zret[turn, me]
 
     def zonal_receive(turn, field):
@@ -782,8 +787,7 @@
     whole = jnp.concatenate(list(acc) + [jnp.zeros((LANES - CAP, LANES), F32)], axis=0)
     whole = jnp.transpose(whole)
     for device in range(N_LON):
-        out_ref[device, 0:4, :] = whole[4 * device : 4 * device + 4]
-        out_ref[device, 4:8, :] = jnp.zeros((4, LANES), F32)
+        out_ref[device] = whole[4 * device : 4 * device + 4]
     pltpu.make_async_copy(inc_ref, inc_ref, inc_sem).wait()
 
 
@@ -791,7 +795,7 @@
     return pl.pallas_call(
         pick_kernel,
         out_shape=(
-            jax.ShapeDtypeStruct((N_LON, 8, LANES), F32),
+            jax.ShapeDtypeStruct((N_LON, 4, LANES), F32),
             jax.ShapeDtypeStruct((NF, NZ, NLAT, LANES), F32),
         ),
         in_specs=[SMEM_SPEC, VMEM_SPEC, VMEM_SPEC],
@@ -860,7 +864,7 @@
             pltpu.VMEM((RANKS, LANES), jnp.int32), vmem(RANKS, LANES),
             pltpu.VMEM((RANKS // 2, CAP, 2 * LANES), BF16),
             pltpu.VMEM((RANKS // 2, LANES, 2 * LANES), BF16),
-            vmem(N_LON, 8, LANES), vmem(N_LAT, N_LON, LANES), vmem(N_LAT, N_LON, LANES),
+            vmem(N_LON, 4, LANES), vmem(N_LAT, N_LON, LANES), vmem(N_LAT, N_LON, LANES),
             dma((N_LON,)), dma((N_LON,)), dma((N_LAT,)), dma((N_LAT,)),
         ],
         compiler_params=pltpu.CompilerParams(

time: 107 us -> 107 us (level)
  no operation moved by 1% of the time
where the time goes in v8:
time: 107 us; the launch traced here: 106 us
  Pallas kernels  102 us (95%)
  local copies, waits for them, and re-layouts  2.18 us (2%)
  other arithmetic  1.66 us (2%)
    pallas_call x1, Pallas kernels, solve(): pl.pallas_call(solve_kernel, out_shape=jax.ShapeDtypeStruct((NF, NLAT, ZP...  44.5 us
    pallas_call x1, Pallas kernels, prepare(): pl.pallas_call(prepare_kernel, out_shape=(shape(RANKS, LANES), shape(80,...  21.1 us
    pallas_call x1, Pallas kernels, place(): pl.pallas_call(place_kernel, out_shape=jax.ShapeDtypeStruct((CAP, LANES),...  14.6 us
    pallas_call x1, Pallas kernels, scatter(): pl.pallas_call(scatter_kernel, out_shape=(grid,) * GRIDS, in_specs=[SMEM_...  11 us
    pallas_call x1, Pallas kernels, pick(): pl.pallas_call(pick_kernel, out_shape=(jax.ShapeDtypeStruct((N_LON, 4, LA...  10.7 us

profile of v8, /device:TPU:1, one launch (start us, length us, event | category | flops | bytes accessed | tf_op | source)
XLA Modules:
  0.0 106.4 jit_solution(15213313671072846048)
XLA Ops:
  0.6 0.8 pad_add_fusion.ints_ref.refs_9_
  1.5 0.9 reshape.28
  2.4 0.8 select_maximum_fusion.floats_ref
  3.3 21.1 %prepare.1 = (f32[128,128]{1,0:T(8,128)S(1)}, f32[80,128]{1,0:T(8,128)S(1)}, f32[80,128]{1,0:T(8,128)S(1)}, f32[2,8,128]{2,1,0:T(8,128)S(1)}, f32[2,40,128]{2,1,...) custom-call(s32[200,128]{1,0:T(8,128)S(1)} %pad_add_fusion.ints_ref., ...), custom_call_target="tpu_custom_call" | custom-call | bytes 54000000 | tf_op jit(solution)/shard_map/prepare/pallas_call | solution.py:335
  24.3 0.0 copy-start
  24.4 11.0 %scatter.1 = (f32[6400,128]{1,0:T(8,128)S(1)}, f32[6400,128]{1,0:T(8,128)S(1)}, f32[6400,128]{1,0:T(8,128)S(1)}, f32[6400,128]{1,0:T(8,128)S(1)}, f32[6400,128]{...) custom-call(s32[10240]{0:T(1024)S(1)} %bitcast.14, ...), custom_call_target="tpu_custom_call", output_to_operand_aliasing={{0}: (3, {}), {1}: (4, {}), {2}: (5, {}), {3}: (6, {}), {4}... | custom-call | bytes 43200000 | tf_op jit(solution)/shard_map/scatter/pallas_call | solution.py:399
  35.4 0.0 copy-done
  35.4 0.6 copy.20
  36.0 44.5 %solve.1 = f32[2,40,80,128]{3,2,1,0:T(8,128)S(1)} custom-call(f32[6400,128]{1,0:T(8,128)S(1)} %get-tuple-element.45.refs_0_, f32[6400,128]{1,0:T(8,128)S(1)} %get-tuple-element.46.refs_1_, f32[6400,128]{1,0:T(8,128)S(1)} %get-tuple-element.47.refs_2_, f32[6400,128]{1,0:T(8,128)S(1)} %get-tuple-element.48.refs_3_, f32[6400,128]{1,0:T(8,128)S(1)} %get-tuple-element.49.refs_4_, ...), custom_call_target="tpu_custom_call" | custom-call | bytes 144000000 | tf_op jit(solution)/shard_map/solve/pallas_call | solution.py:738
  80.5 10.7 %pick.1 = (f32[32,4,128]{2,1,0:T(4,128)S(1)}, f32[2,75,40,128]{3,2,1,0:T(8,128)}) custom-call(s32[10240]{0:T(1024)S(1)} %bitcast.15, s32[200,128]{1,0:T(8,128)S(1)} %pad_add_fusion.ints_ref.refs_9_, f32[6400,128]{1,0:T(8,128)S(1)} %bitcast.13), custom_call_target="tpu_custom_call" | custom-call | bytes 50400000 | tf_op jit(solution)/shard_map/pick/pallas_call | solution.py:795
  91.2 14.6 %place.1 = f32[80,128]{1,0:T(8,128)S(1)} custom-call(f32[32,4,128]{2,1,0:T(4,128)S(1)} %get-tuple-element.67.tile_out, s32[200,128]{1,0:T(8,128)S(1)} %pad_add_fusion.ints_ref.refs_9_), custom_call_target="tpu_custom_call" | custom-call | bytes 54000000 | tf_op jit(solution)/shard_map/place/pallas_call | solution.py:858
  105.8 0.6 copy.30
  (1 shorter events, 0.0 us)
Async XLA Ops:
  24.3 11.0 %copy-start = (f32[2,75,40,128]{3,2,1,0:T(8,128)S(1)}, f32[2,75,40,128]{3,2,1,0:T(8,128)}, u32[]{:S(2)}) copy-start(f32[2,75,40,128]{3,2,1,0:T(8,128)} %param.15) | copy-start | bytes 9216004

commit v9 on v8

--- a/solution.py
+++ b/solution.py
@@ -234,11 +234,13 @@
     def end():
         over_lat(lambda device: second(0, device).wait_recv())
 
-    def sent():
+    def sent_first():
         over_lon(lambda device: first(device, me).wait_send())
+
+    def sent_second():
         over_lat(lambda device: second(device, my).wait_send())
 
-    return begin, middle, end, sent
+    return begin, middle, end, sent_first, sent_second
 
 
 def prepare_kernel(
@@ -278,7 +280,9 @@
     for device in range(N_LON):
         tile_out[device] = picked[4 * device : 4 * device + 4]
 
-    begin, middle, end, sent = two_phase(tile_out, tile_in, rows_out, rows_in, (o1s, o1r, o2s, o2r))
+    begin, middle, end, sent_first, sent_second = two_phase(
+        tile_out, tile_in, rows_out, rows_in, (o1s, o1r, o2s, o2r)
+    )
     zco_copy = lambda device, slot: push(
         zco_ref, zco_all.at[slot], zco_s.at[device], zco_r.at[slot], "lon", device
     )
@@ -316,6 +320,8 @@
     source = lax.broadcasted_iota(jnp.int32, (2 * LANES, 2 * LANES), 0) & 127
     target = lax.broadcasted_iota(jnp.int32, (2 * LANES, 2 * LANES), 1)
     sums_ref[...] = jnp.where(source <= target, 1.0, 0.0).astype(BF16)
+    sent_first()
+    over_lon(lambda device: zco_copy(device, me).wait_send())
     end()
     for lat in range(N_LAT):
         out_ref[N_LON * lat : N_LON * lat + N_LON, :] = rows_in[lat]
@@ -323,8 +329,7 @@
     zonal_factor(zco_all, alpha, gamma, minv)
     over_lat(lambda device: mco_copy(0, device).wait_recv())
     mco_out[...] = mco_all[...]
-    sent()
-    over_lon(lambda device: zco_copy(device, me).wait_send())
+    sent_second()
     over_lat(lambda device: mco_copy(device, my).wait_send())
 
 
@@ -705,17 +710,6 @@
         zonal_pass(1, field, lambda row, field=field: merid_value(field, row))
         zonal_send(1, field)
     pl.when(is_solver)(lambda: zonal_reduced(1))
-    for field in range(NF):
-        zonal_receive(1, field)
-
-        def last_pass(chunk, _, field=field):
-            found = zonal_values(field, chunk)
-            for step in range(CHUNK):
-                row = chunk * CHUNK + step
-                x_ref[field, row] = found[step] * scale(field, row)
-            return 0
-
-        lax.fori_loop(0, NLAT // CHUNK, last_pass, 0)
 
     for field in range(NF):
         over_lat(lambda device, field=field: merid_out(field, device, my).wait_send())
@@ -730,6 +724,18 @@
     def _():
         for turn in range(2):
             over_lon(lambda device, turn=turn: zonal_back(turn, device, 0, 0).wait_send())
+
+    for field in range(NF):
+        zonal_receive(1, field)
+
+        def last_pass(chunk, _, field=field):
+            found = zonal_values(field, chunk)
+            for step in range(CHUNK):
+                row = chunk * CHUNK + step
+                x_ref[field, row] = found[step] * scale(field, row)
+            return 0
+
+        lax.fori_loop(0, NLAT // CHUNK, last_pass, 0)
 
 
 def solve(grids, norm, ints, coefs):
@@ -814,7 +820,9 @@
     greet()
     none = jnp.full((LANES - CAP, LANES), -1, jnp.int32)
     idx_ref[...] = jnp.transpose(jnp.concatenate([ints_ref[0:CAP, :], none], axis=0))
-    begin, middle, end, sent = two_phase(tile_out, tile_in, rows_out, rows_in, (b1s, b1r, b2s, b2r))
+    begin, middle, end, sent_first, sent_second = two_phase(
+        tile_out, tile_in, rows_out, rows_in, (b1s, b1r, b2s, b2r)
+    )
     row_iota = lax.broadcasted_iota(jnp.int32, (CAP, 2 * LANES), 0)
     col_iota = lax.broadcasted_iota(jnp.int32, (LANES, 2 * LANES), 0)
 
@@ -844,12 +852,13 @@
     lax.fori_loop(0, RANKS // 4, build, 0, unroll=2)
     middle()
     lax.fori_loop(RANKS // 4, RANKS // 2, build, 0, unroll=2)
+    sent_first()
     end()
     for lat in range(N_LAT):
         val_ref[N_LON * lat : N_LON * lat + N_LON, :] = rows_in[lat]
     acc = lax.fori_loop(0, RANKS // 2, add, jnp.zeros((2 * CAP, LANES), F32), unroll=8)
     out_ref[...] = acc[:CAP] + acc[CAP:]
-    sent()
+    sent_second()
 
 
 def place(tiles, ints):

time: 107 us -> 104 us (0.972)
  Pallas kernels: 102 us -> 99.3 us
    pallas_call x1, Pallas kernels: 44.5 us -> 43.1 us  [solve(): pl.pallas_call(solve_kernel, out_shape=jax.ShapeDtypeStruct((NF, NLAT, ZP...]
where the time goes in v9:
time: 104 us
  Pallas kernels  99.3 us (95%)
  local copies, waits for them, and re-layouts  2.18 us (2%)
  other arithmetic  1.66 us (2%)
    pallas_call x1, Pallas kernels, solve(): pl.pallas_call(solve_kernel, out_shape=jax.ShapeDtypeStruct((NF, NLAT, ZP...  43.1 us
    pallas_call x1, Pallas kernels, prepare(): pl.pallas_call(prepare_kernel, out_shape=(shape(RANKS, LANES), shape(80,...  20.4 us
    pallas_call x1, Pallas kernels, place(): pl.pallas_call(place_kernel, out_shape=jax.ShapeDtypeStruct((CAP, LANES),...  14.1 us
    pallas_call x1, Pallas kernels, scatter(): pl.pallas_call(scatter_kernel, out_shape=(grid,) * GRIDS, in_specs=[SMEM_...  11 us
    pallas_call x1, Pallas kernels, pick(): pl.pallas_call(pick_kernel, out_shape=(jax.ShapeDtypeStruct((N_LON, 4, LA...  10.7 us

profile of v9, /device:TPU:1, one launch (start us, length us, event | category | flops | bytes accessed | tf_op | source)
XLA Modules:
  0.0 103.8 jit_solution(15253264586922462204)
XLA Ops:
  0.6 0.8 pad_add_fusion.ints_ref.refs_9_
  1.5 0.9 reshape.28
  2.4 0.8 select_maximum_fusion.floats_ref
  3.3 20.4 %prepare.1 = (f32[128,128]{1,0:T(8,128)S(1)}, f32[80,128]{1,0:T(8,128)S(1)}, f32[80,128]{1,0:T(8,128)S(1)}, f32[2,8,128]{2,1,0:T(8,128)S(1)}, f32[2,40,128]{2,1,...) custom-call(s32[200,128]{1,0:T(8,128)S(1)} %pad_add_fusion.ints_ref., ...), custom_call_target="tpu_custom_call" | custom-call | bytes 54000000 | tf_op jit(solution)/shard_map/prepare/pallas_call | solution.py:340
  23.6 0.0 copy-start
  23.6 11.0 %scatter.1 = (f32[6400,128]{1,0:T(8,128)S(1)}, f32[6400,128]{1,0:T(8,128)S(1)}, f32[6400,128]{1,0:T(8,128)S(1)}, f32[6400,128]{1,0:T(8,128)S(1)}, f32[6400,128]{...) custom-call(s32[10240]{0:T(1024)S(1)} %bitcast.14, ...), custom_call_target="tpu_custom_call", output_to_operand_aliasing={{0}: (3, {}), {1}: (4, {}), {2}: (5, {}), {3}: (6, {}), {4}... | custom-call | bytes 43200000 | tf_op jit(solution)/shard_map/scatter/pallas_call | solution.py:404
  34.7 0.0 copy-done
  34.7 0.6 copy.20
  35.3 43.1 %solve.1 = f32[2,40,80,128]{3,2,1,0:T(8,128)S(1)} custom-call(f32[6400,128]{1,0:T(8,128)S(1)} %get-tuple-element.45.refs_0_, f32[6400,128]{1,0:T(8,128)S(1)} %get-tuple-element.46.refs_1_, f32[6400,128]{1,0:T(8,128)S(1)} %get-tuple-element.47.refs_2_, f32[6400,128]{1,0:T(8,128)S(1)} %get-tuple-element.48.refs_3_, f32[6400,128]{1,0:T(8,128)S(1)} %get-tuple-element.49.refs_4_, ...), custom_call_target="tpu_custom_call" | custom-call | bytes 144000000 | tf_op jit(solution)/shard_map/solve/pallas_call | solution.py:744
  78.4 10.7 %pick.1 = (f32[32,4,128]{2,1,0:T(4,128)S(1)}, f32[2,75,40,128]{3,2,1,0:T(8,128)}) custom-call(s32[10240]{0:T(1024)S(1)} %bitcast.15, s32[200,128]{1,0:T(8,128)S(1)} %pad_add_fusion.ints_ref.refs_9_, f32[6400,128]{1,0:T(8,128)S(1)} %bitcast.13), custom_call_target="tpu_custom_call" | custom-call | bytes 50400000 | tf_op jit(solution)/shard_map/pick/pallas_call | solution.py:801
  89.1 14.1 %place.1 = f32[80,128]{1,0:T(8,128)S(1)} custom-call(f32[32,4,128]{2,1,0:T(4,128)S(1)} %get-tuple-element.67.tile_out, s32[200,128]{1,0:T(8,128)S(1)} %pad_add_fusion.ints_ref.refs_9_), custom_call_target="tpu_custom_call" | custom-call | bytes 54000000 | tf_op jit(solution)/shard_map/place/pallas_call | solution.py:867
  103.2 0.6 copy.30
  (1 shorter events, 0.0 us)
Async XLA Ops:
  23.6 11.1 %copy-start = (f32[2,75,40,128]{3,2,1,0:T(8,128)S(1)}, f32[2,75,40,128]{3,2,1,0:T(8,128)}, u32[]{:S(2)}) copy-start(f32[2,75,40,128]{3,2,1,0:T(8,128)} %param.15) | copy-start | bytes 9216004
